TPU v7x, 512 devices: a whole 4x8x8 slice. The times are simulated.
512 devices in a mesh: slab: 64 (over x, z, core), filt: 8 (over y).
Axes of the slice: x: 4, y: 8, z: 8, core: 2. Of those that a mesh axis runs over, the one named last changes fastest.
Arguments:
- volume: bfloat16 [128, 128, 16, 256], P('slab', 'filt'), may hold values from -6 to 6
- weights: bfloat16 [3, 3, 3, 128, 256], replicated, may hold values from -0.109375 to 0.109375
- out_error: bfloat16 [64, 256, 8, 128], P('slab', 'filt'), may hold values from -6 to 6
Outputs:
- in_grad: bfloat16 [128, 128, 16, 256], P('slab', None, 'filt')
- weight_grad: float32 [3, 3, 3, 128, 256], P(None, None, None, None, 'filt')
All inputs are finite; a program needn't handle non-finite values.
Results may differ from a plain program's by a relative error of at most 0.0049.
Values may be sent and summed in bfloat16 or wider, within the bound.
No kernel may reach another device: no remote copies, remote signals or barrier semaphores. Data moves between devices by JAX's collectives and lax.ppermute only.
A program may use at most 64 MiB of HBM per device.

v0:
```python
import math

import jax
import jax.numpy as jnp
from jax import lax
from jax.sharding import PartitionSpec as P


def shifted_2(value, axis, steps):
    count = lax.axis_size(axis)
    first, last = (max(0, -steps), min(count, count - steps))
    return lax.ppermute(value, axis, [(source, source + steps) for source in range(first, last)])


def tap_pieces(extended, top):
    depth = (extended.shape[0] - 1) // 2
    rows = (extended.shape[2] + top - 1) // 2
    cols = extended.shape[3] // 2
    chans = extended.shape[1]
    padded = jnp.pad(extended, ((0, 1), (0, 0), (top, 1), (1, 1)))
    split = padded.reshape(depth + 1, 2, chans, rows + 1, 2, cols + 1, 2)
    pieces = []
    for a in range(3):
        for b in range(3):
            for c in range(3):
                piece = split[
                    a // 2 : a // 2 + depth,
                    a % 2,
                    :,
                    b // 2 : b // 2 + rows,
                    b % 2,
                    c // 2 : c // 2 + cols,
                    c % 2,
                ]
                pieces.append(((a, b, c), piece))
    return pieces


def forward_taps(pieces, kernel):
    total = None
    for (a, b, c), piece in pieces:
        term = jnp.einsum(
            "dkhw,kf->dfhw", piece, kernel[a, b, c], preferred_element_type=jnp.float32
        )
        total = term if total is None else total + term
    return total


def weight_taps(pieces, grad):
    terms = []
    for (a, b, c), piece in pieces:
        terms.append(jnp.einsum("dkhw,dfhw->kf", piece, grad, preferred_element_type=jnp.float32))
    stacked = jnp.stack(terms, 0)
    return stacked.reshape((3, 3, 3) + stacked.shape[1:])


def input_taps(grad_ext, kernel):
    depth = grad_ext.shape[0] - 1
    rows = grad_ext.shape[2] - 1
    cols = grad_ext.shape[3]
    chans = kernel.shape[3]
    parity_taps = ((1,), (2, 0))
    shifted = {}
    for a in range(3):
        for b in range(3):
            for c in range(3):
                term = jnp.einsum(
                    "dfhw,kf->dkhw", grad_ext, kernel[a, b, c], preferred_element_type=jnp.float32
                )
                start_d = 1 if a == 0 else 0
                start_r = 1 if b == 0 else 0
                term = term[start_d : start_d + depth, :, start_r : start_r + rows]
                if c == 0:
                    term = jnp.pad(term[..., 1:], ((0, 0), (0, 0), (0, 0), (0, 1)))
                shifted[a, b, c] = term
    depth_parts = []
    for even_d in range(2):
        row_parts = []
        for even_r in range(2):
            col_parts = []
            for even_c in range(2):
                total = None
                for a in parity_taps[even_d]:
                    for b in parity_taps[even_r]:
                        for c in parity_taps[even_c]:
                            total = shifted[a, b, c] if total is None else total + shifted[a, b, c]
                col_parts.append(total)
            row_parts.append(jnp.stack(col_parts, -1))
        row_parts = jnp.stack(row_parts, 3)
        depth_parts.append(row_parts)
    joined = jnp.stack(depth_parts, 1)
    return joined.reshape(2 * depth, chans, 2 * rows, 2 * cols)


def activation_grad(preact, error):
    sigma = jax.nn.sigmoid(preact)
    return (error * (sigma * (1.0 + preact * (1.0 - sigma)))).astype(jnp.bfloat16)


def on_device(volume, weights, out_error):
    member = lax.axis_index("filt")
    tile = out_error.shape[1]
    below = shifted_2(volume[-1:], "slab", 1)
    extended = jnp.concatenate([below, volume], 0)
    whole = lax.all_gather(extended, "filt", axis=1, tiled=True)
    pieces = tap_pieces(whole, 1)
    kernel_tile = lax.dynamic_slice_in_dim(weights, member * tile, tile, 4)
    preact = forward_taps(pieces, kernel_tile)
    grad = activation_grad(preact, out_error)
    weight_part = weight_taps(pieces, grad)
    grad_rows = lax.all_to_all(grad, "filt", split_axis=2, concat_axis=1, tiled=True)
    count = out_error.shape[0] * lax.axis_size("slab") * out_error.shape[2] * out_error.shape[3]
    weight_grad = lax.psum(weight_part, "slab") * (1.0 / math.sqrt(count))
    upper = shifted_2(grad_rows, "slab", -1)
    grad_ext = jnp.concatenate([grad_rows, upper], 0)
    right_row = shifted_2(grad_ext, "filt", -1)
    grad_ext = jnp.concatenate([grad_ext, right_row], 2)
    in_grad = input_taps(grad_ext, weights).astype(jnp.bfloat16)
    return (in_grad, weight_grad)


def solution(mesh):
    in_specs = (P("slab", "filt", None, None), P(), P("slab", "filt", None, None))
    out_specs = (P("slab", None, "filt", None), P(None, None, None, None, "filt"))
    return jax.shard_map(
        on_device, mesh=mesh, in_specs=in_specs, out_specs=out_specs, check_vma=False
    )
```

profile of v0, /device:TPU:1, one launch (start us, length us, event | category | flops | bytes accessed | tf_op | source)
XLA Modules:
  0.0 422.1 jit_solution(12113445541933201036)
XLA Ops:
  8.1 5.4 %collective-permute-start = (bf16[1,16,16,256]{3,2,1,0:T(8,128)(2,1)S(1)}, bf16[1,16,16,256]{3,2,1,0:T(8,128)(2,1)S(1)}, u32[]{:S(2)}, u32[]{:S(2)}) collective-permute-start(bf16[1,16,16,256]{3,2,1,0:T(8,128)(2,1)S(1)} %slice.347), channel_id=1, source_target_pairs={{0,8},{8,16},{16,24},{24,32},{32,40},{40,48},{48,56},{56,64},{64,7... | collective-permute-start | bytes 393224 | tf_op jit(solution)/shard_map/ppermute | solution.py:12
  13.5 3.6 collective-permute-done
  18.9 51.0 %all-gather.2.cloned.1.call-done = bf16[3,128,16,256]{3,2,1,0:T(8,128)(2,1)} async-done(((bf16[3,16,16,256]{3,2,1,0:T(8,128)(2,1)}), bf16[3,128,16,256]{3,2,1,0:T(8,128)(2,1)}) %all-gather.2.cloned.1.call-update) | async-done | bytes 3145744 | tf_op jit(solution)/shard_map/all_gather | solution.py:105
  69.9 6.1 %copy.203 = bf16[3,128,16,256]{1,0,3,2:T(4,128)(2,1)} copy(bf16[3,128,16,256]{3,2,1,0:T(8,128)(2,1)} %all-gather.2.cloned.1.call-done) | data formatting | bytes 6291456
  76.0 3.9 pad.32.clone
  79.9 4.1 fusion.214
  84.0 11.3 %fusion.213 = (bf16[1,1,128,8,1,128,1]{2,1,0,6,5,4,3:T(2,128)(2,1)}, bf16[1,1,128,8,1,128,1]{2,1,0,6,5,4,3:T(2,128)(2,1)}, bf16[1,1,128,8,1,128,1]{2,1,0,6,5,4,3...) fusion(bf16[2,2,128,9,2,129,2]{2,1,0,6,5,4,3:T(2,128)(2,1)S(1)}, ...), kind=kLoop, calls=%fused_computation.343 | loop fusion | bytes 9961472 | tf_op jit(solution)/shard_map/slice | solution.py:26
  97.4 1.9 copy.158
  101.2 1.9 copy.154
  103.0 1.9 copy.152
  104.9 1.9 copy.150
  106.8 1.9 copy.202
  118.8 1.9 copy.180
  120.7 1.9 copy.178
  122.6 1.9 copy.176
  124.5 1.9 copy.174
  126.3 1.9 copy.172
  128.2 1.9 copy.170
  130.1 1.9 copy.168
  132.0 1.9 copy.166
  165.6 4.6 %all-to-all-start = ((bf16[1,32,8,128]{3,1,0,2:T(8,128)(2,1)}), bf16[1,32,8,128]{3,1,0,2:T(8,128)(2,1)S(1)}, u32[]{:S(2)}, u32[]{:S(2)}) async-start(bf16[1,32,8,128]{3,1,0,2:T(8,128)(2,1)} %bitcast.83), calls=%async_computation | async-start | bytes 131072 | tf_op jit(solution)/shard_map/all_to_all | solution.py:111
  214.3 3.0 collective-permute-start.1
  217.3 3.2 collective-permute-done.1
  221.8 183.9 %all-reduce.12.cloned.1.call-done = f32[3,3,3,128,32]{3,4,2,1,0:T(8,128)} async-done(((f32[3,3,3,128,32]{3,4,2,1,0:T(8,128)}), f32[3,3,3,128,32]{3,4,2,1,0:T(8,128)}) %all-reduce.12.cloned.1.call-update) | async-done | bytes 442384 | tf_op jit(solution)/shard_map/psum | solution.py:113
  (175 shorter events, 102.6 us)
Async XLA Ops:
  7.2 62.7 %all-gather.2.cloned.1.call-start = ((), (), s32[]{:S(2)}) async-start(), calls=%async_computation.1 | async-start | bytes 3538944 | tf_op jit(solution)/shard_map/all_gather | solution.py:105
  8.1 9.0 %collective-permute-start = (bf16[1,16,16,256]{3,2,1,0:T(8,128)(2,1)S(1)}, bf16[1,16,16,256]{3,2,1,0:T(8,128)(2,1)S(1)}, u32[]{:S(2)}, u32[]{:S(2)}) collective-permute-start(bf16[1,16,16,256]{3,2,1,0:T(8,128)(2,1)S(1)} %slice.347), channel_id=1, source_target_pairs={{0,8},{8,16},{16,24},{24,32},{32,40},{40,48},{48,56},{56,64},{64,7... | collective-permute-start | bytes 393224 | tf_op jit(solution)/shard_map/ppermute | solution.py:12
  136.4 7.0 %copy-start.16 = (bf16[1,1,128,8,1,128,1]{5,2,3,6,4,1,0:T(8,128)(2,1)S(1)}, bf16[1,1,128,8,1,128,1]{5,2,3,6,4,1,0:T(8,128)(2,1)}, u32[]{:S(2)}) copy-start(bf16[1,1,128,8,1,128,1]{5,2,3,6,4,1,0:T(8,128)(2,1)} %copy.166) | copy-start | bytes 786436
  137.7 6.8 %copy-start.14 = (bf16[1,1,128,8,1,128,1]{5,2,3,6,4,1,0:T(8,128)(2,1)S(1)}, bf16[1,1,128,8,1,128,1]{5,2,3,6,4,1,0:T(8,128)(2,1)}, u32[]{:S(2)}) copy-start(bf16[1,1,128,8,1,128,1]{5,2,3,6,4,1,0:T(8,128)(2,1)} %copy.168) | copy-start | bytes 786436
  139.0 6.5 %copy-start.11 = (bf16[1,1,128,8,1,128,1]{5,2,3,6,4,1,0:T(8,128)(2,1)S(1)}, bf16[1,1,128,8,1,128,1]{5,2,3,6,4,1,0:T(8,128)(2,1)}, u32[]{:S(2)}) copy-start(bf16[1,1,128,8,1,128,1]{5,2,3,6,4,1,0:T(8,128)(2,1)} %copy.170) | copy-start | bytes 786436
  140.1 6.5 %copy-start.9 = (bf16[1,1,128,8,1,128,1]{5,2,3,6,4,1,0:T(8,128)(2,1)S(1)}, bf16[1,1,128,8,1,128,1]{5,2,3,6,4,1,0:T(8,128)(2,1)}, u32[]{:S(2)}) copy-start(bf16[1,1,128,8,1,128,1]{5,2,3,6,4,1,0:T(8,128)(2,1)} %copy.172) | copy-start | bytes 786436
  141.1 6.5 %copy-start.7 = (bf16[1,1,128,8,1,128,1]{5,2,3,6,4,1,0:T(8,128)(2,1)S(1)}, bf16[1,1,128,8,1,128,1]{5,2,3,6,4,1,0:T(8,128)(2,1)}, u32[]{:S(2)}) copy-start(bf16[1,1,128,8,1,128,1]{5,2,3,6,4,1,0:T(8,128)(2,1)} %copy.174) | copy-start | bytes 786436
  142.2 6.4 %copy-start.5 = (bf16[1,1,128,8,1,128,1]{5,2,3,6,4,1,0:T(8,128)(2,1)S(1)}, bf16[1,1,128,8,1,128,1]{5,2,3,6,4,1,0:T(8,128)(2,1)}, u32[]{:S(2)}) copy-start(bf16[1,1,128,8,1,128,1]{5,2,3,6,4,1,0:T(8,128)(2,1)} %copy.176) | copy-start | bytes 786436
  143.3 6.4 %copy-start.3 = (bf16[1,1,128,8,1,128,1]{5,2,3,6,4,1,0:T(8,128)(2,1)S(1)}, bf16[1,1,128,8,1,128,1]{5,2,3,6,4,1,0:T(8,128)(2,1)}, u32[]{:S(2)}) copy-start(bf16[1,1,128,8,1,128,1]{5,2,3,6,4,1,0:T(8,128)(2,1)} %copy.178) | copy-start | bytes 786436
  157.0 7.0 %copy-start.13 = (bf16[1,1,128,8,1,128,1]{5,2,3,6,4,1,0:T(8,128)(2,1)S(1)}, bf16[1,1,128,8,1,128,1]{5,2,3,6,4,1,0:T(8,128)(2,1)}, u32[]{:S(2)}) copy-start(bf16[1,1,128,8,1,128,1]{5,2,3,6,4,1,0:T(8,128)(2,1)} %copy.150) | copy-start | bytes 786436
  165.6 48.6 %all-to-all-start = ((bf16[1,32,8,128]{3,1,0,2:T(8,128)(2,1)}), bf16[1,32,8,128]{3,1,0,2:T(8,128)(2,1)S(1)}, u32[]{:S(2)}, u32[]{:S(2)}) async-start(bf16[1,32,8,128]{3,1,0,2:T(8,128)(2,1)} %bitcast.83), calls=%async_computation | async-start | bytes 131072 | tf_op jit(solution)/shard_map/all_to_all | solution.py:111
  170.3 235.4 %all-reduce.12.cloned.1.call-start = ((), (), s32[]{:S(2)}) async-start(), calls=%async_computation.2 | async-start | bytes 884736 | tf_op jit(solution)/shard_map/psum | solution.py:113
  170.5 12.3 %copy-start.17 = (bf16[1,1,128,8,1,128,1]{5,2,3,6,4,1,0:T(8,128)(2,1)S(1)}, bf16[1,1,128,8,1,128,1]{5,2,3,6,4,1,0:T(8,128)(2,1)}, u32[]{:S(2)}) copy-start(bf16[1,1,128,8,1,128,1]{5,2,3,6,4,1,0:T(8,128)(2,1)} %copy.166) | copy-start | bytes 786436
  170.5 13.9 %copy-start.15 = (bf16[1,1,128,8,1,128,1]{5,2,3,6,4,1,0:T(8,128)(2,1)S(1)}, bf16[1,1,128,8,1,128,1]{5,2,3,6,4,1,0:T(8,128)(2,1)}, u32[]{:S(2)}) copy-start(bf16[1,1,128,8,1,128,1]{5,2,3,6,4,1,0:T(8,128)(2,1)} %copy.168) | copy-start | bytes 786436
  170.5 15.5 %copy-start.12 = (bf16[1,1,128,8,1,128,1]{5,2,3,6,4,1,0:T(8,128)(2,1)S(1)}, bf16[1,1,128,8,1,128,1]{5,2,3,6,4,1,0:T(8,128)(2,1)}, u32[]{:S(2)}) copy-start(bf16[1,1,128,8,1,128,1]{5,2,3,6,4,1,0:T(8,128)(2,1)} %copy.170) | copy-start | bytes 786436
  170.5 17.2 %copy-start.10 = (bf16[1,1,128,8,1,128,1]{5,2,3,6,4,1,0:T(8,128)(2,1)S(1)}, bf16[1,1,128,8,1,128,1]{5,2,3,6,4,1,0:T(8,128)(2,1)}, u32[]{:S(2)}) copy-start(bf16[1,1,128,8,1,128,1]{5,2,3,6,4,1,0:T(8,128)(2,1)} %copy.172) | copy-start | bytes 786436
  172.4 17.0 %copy-start.8 = (bf16[1,1,128,8,1,128,1]{5,2,3,6,4,1,0:T(8,128)(2,1)S(1)}, bf16[1,1,128,8,1,128,1]{5,2,3,6,4,1,0:T(8,128)(2,1)}, u32[]{:S(2)}) copy-start(bf16[1,1,128,8,1,128,1]{5,2,3,6,4,1,0:T(8,128)(2,1)} %copy.174) | copy-start | bytes 786436
  174.2 16.8 %copy-start.6 = (bf16[1,1,128,8,1,128,1]{5,2,3,6,4,1,0:T(8,128)(2,1)S(1)}, bf16[1,1,128,8,1,128,1]{5,2,3,6,4,1,0:T(8,128)(2,1)}, u32[]{:S(2)}) copy-start(bf16[1,1,128,8,1,128,1]{5,2,3,6,4,1,0:T(8,128)(2,1)} %copy.176) | copy-start | bytes 786436
  176.0 16.7 %copy-start.4 = (bf16[1,1,128,8,1,128,1]{5,2,3,6,4,1,0:T(8,128)(2,1)S(1)}, bf16[1,1,128,8,1,128,1]{5,2,3,6,4,1,0:T(8,128)(2,1)}, u32[]{:S(2)}) copy-start(bf16[1,1,128,8,1,128,1]{5,2,3,6,4,1,0:T(8,128)(2,1)} %copy.178) | copy-start | bytes 786436
  177.8 16.5 %copy-start.2 = (bf16[1,1,128,8,1,128,1]{5,2,3,6,4,1,0:T(8,128)(2,1)S(1)}, bf16[1,1,128,8,1,128,1]{5,2,3,6,4,1,0:T(8,128)(2,1)}, u32[]{:S(2)}) copy-start(bf16[1,1,128,8,1,128,1]{5,2,3,6,4,1,0:T(8,128)(2,1)} %copy.180) | copy-start | bytes 786436
  195.9 16.6 %copy-start.19 = (bf16[1,1,128,8,1,128,1]{5,2,3,6,4,1,0:T(8,128)(2,1)S(1)}, bf16[1,1,128,8,1,128,1]{5,2,3,6,4,1,0:T(8,128)(2,1)}, u32[]{:S(2)}) copy-start(bf16[1,1,128,8,1,128,1]{5,2,3,6,4,1,0:T(8,128)(2,1)} %copy.202) | copy-start | bytes 786436
  207.5 200.0 %copy-start.20 = (bf16[3,3,3,128,256]{4,3,2,1,0:T(8,128)(2,1)S(1)}, bf16[3,3,3,128,256]{4,3,2,1,0:T(8,128)(2,1)}, u32[]{:S(2)}) copy-start(bf16[3,3,3,128,256]{4,3,2,1,0:T(8,128)(2,1)} %param.4) | copy-start | bytes 5308420
  214.3 6.1 %collective-permute-start.1 = (bf16[1,256,1,128]{1,3,2,0:T(8,128)(2,1)S(1)}, bf16[1,256,1,128]{1,3,2,0:T(8,128)(2,1)S(1)}, u32[]{:S(2)}, u32[]{:S(2)}) collective-permute-start(bf16[1,256,1,128]{1,3,2,0:T(8,128)(2,1)S(1)} %copy.115), channel_id=1, source_target_pairs={{8,0},{16,8},{24,16},{32,24},{40,32},{48,40},{56,48},{64,56},{72,6... | collective-permute-start | bytes 196616 | tf_op jit(solution)/shard_map/ppermute | solution.py:12
  220.5 187.0 %collective-permute-start.2 = (bf16[2,256,1,128]{1,3,2,0:T(8,128)(2,1)S(1)}, bf16[2,256,1,128]{1,3,2,0:T(8,128)(2,1)S(1)}, u32[]{:S(2)}, u32[]{:S(2)}) collective-permute-start(bf16[2,256,1,128]{1,3,2,0:T(8,128)(2,1)S(1)} %pad_maximum_fusion.2), channel_id=1, source_target_pairs={{1,0},{2,1},{3,2},{4,3},{5,4},{6,5},{7,6},{9,8},{10,9},{11,10},{12... | collective-permute-start | bytes 393224 | tf_op jit(solution)/shard_map/ppermute | solution.py:12
  (4 other events, 24.1 us)
Sparse Core Ops, SparseCore 0:
  19.0 50.8 all-gather.1
  214.3 191.2 all-reduce.11
where the time goes:
time: 425 us; the launch traced here: 422 us
  waiting for transfers between devices  242 us (57%)
  matrix products  80.7 us (19%)
  local copies, waits for them, and re-layouts  66.4 us (16%)
  between operations  15 us (4%)
  starting transfers between devices  14.5 us (3%)
    psum x1, waiting for transfers between devices, on_device(): weight_grad = lax.psum(weight_part, 'slab') * (1.0 / math.sqrt(count))  184 us
    all_gather x1, waiting for transfers between devices, on_device(): whole = lax.all_gather(extended, 'filt', axis=1, tiled=True)  51 us
    unnamed x73, local copies, waits for them, and re-layouts  45.6 us
    dot_general x27, matrix products, weight_taps(): jnp.einsum('dkhw,dfhw->kf', piece, grad, preferred_element_type=jnp.float32)  45.2 us
    dot_general x27, matrix products, forward_taps(): jnp.einsum('dkhw,kf->dfhw', piece, kernel[a, b, c], preferred_element_typ...  29.6 us
    slice x2, local copies, waits for them, and re-layouts, tap_pieces(): split[a // 2:a // 2 + depth, a % 2, :, b // 2:b // 2 + rows, b % 2, c //...  15.4 us
    ppermute x3, starting transfers between devices, shifted_2(): lax.ppermute(value, axis, [(source, source + steps) for source in range(f...  9.64 us
  transfers between devices with their start and end apart: 6, of which 4 were waited for; matrix products, arithmetic and copies ran while one was open for 11% of the time, Pallas kernels for 0%

commit v1 on v0

v1 whole, which is shorter than its diff:
```python
import jax
import jax.numpy as jnp
from jax import lax
from jax.experimental import pallas as pl
from jax.experimental.pallas import tpu as pltpu
from jax.sharding import PartitionSpec as P

F32 = jnp.float32
BF16 = jnp.bfloat16
VMEM = pl.BlockSpec(memory_space=pltpu.VMEM)
SMEM = pl.BlockSpec(memory_space=pltpu.SMEM)
LIMIT = 48 * 1024 * 1024

NX, NZ, NC = 4, 8, 2
XC_GROUPS = [[(x * NZ + z) * NC + c for x in range(NX) for c in range(NC)] for z in range(NZ)]
Z_GROUPS = [[(x * NZ + z) * NC + c for z in range(NZ)] for x in range(NX) for c in range(NC)]
Y_GROUPS = [[0, 1, 2, 3], [4, 5, 6, 7]]


def call(body, out_shape, in_specs, cost, scratch=()):
    many = isinstance(out_shape, (tuple, list))
    return pl.pallas_call(
        body,
        out_shape=out_shape,
        in_specs=in_specs,
        out_specs=[VMEM] * len(out_shape) if many else VMEM,
        scratch_shapes=list(scratch),
        compiler_params=pltpu.CompilerParams(vmem_limit_bytes=LIMIT),
        cost_estimate=pl.CostEstimate(flops=cost[0], bytes_accessed=cost[1], transcendentals=0),
    )


def mm(left, right):
    return jnp.dot(left, right, preferred_element_type=F32)


def mm_nt(left, right):
    return lax.dot_general(left, right, (((1,), (1,)), ((), ())), preferred_element_type=F32)


def ones_where(cond):
    return jnp.where(cond, 1.0, 0.0).astype(BF16)


def iotas(rows, cols):
    return (
        lax.broadcasted_iota(jnp.int32, (rows, cols), 0),
        lax.broadcasted_iota(jnp.int32, (rows, cols), 1),
    )


def pack_body(vol_ref, err_ref, send_ref):
    i, j = iotas(256, 256)
    row_first = ones_where(j == ((i & 15) << 4) + (i >> 4))
    even_odd = ones_where(i == ((j & 127) << 1) + (j >> 7))
    error_rows = ones_where(j == ((i & 31) << 3) + (i >> 5))
    for p in range(2):
        plane = vol_ref[p].reshape(256, 256)
        plane = mm(row_first, plane).astype(BF16)
        plane = mm(plane, even_odd).astype(BF16)
        for yr in range(4):
            for rr in range(5):
                row = 4 * yr - 1 + rr
                if row < 0:
                    piece = jnp.zeros((16, 256), BF16)
                else:
                    piece = plane[row * 16 : row * 16 + 16]
                send_ref[yr, p * 5 + rr] = piece
                send_ref[yr + 4, p * 5 + rr] = piece
    error = mm(error_rows, err_ref[0].reshape(256, 128)).astype(BF16)
    for yr in range(4):
        for u in range(2):
            for j in range(2):
                start = (2 * yr + j) * 32 + u * 16
                piece = error[start : start + 16]
                send_ref[yr, 10 + u, :, j * 128 : j * 128 + 128] = piece
                send_ref[yr + 4, 10 + u, :, j * 128 : j * 128 + 128] = piece


def turn_body(half_ref, w_ref, even_ref, odd_ref):
    i, j = iotas(128, 256)
    pick = ones_where(j == i + half_ref[0] * 128)
    for ab in range(9):
        cols = slice(ab * 128, ab * 128 + 128)
        even_ref[:, cols] = mm_nt(pick, w_ref[ab, 1]).astype(BF16)
        odd_ref[:128, cols] = mm_nt(pick, w_ref[ab, 2]).astype(BF16)
        odd_ref[128:, cols] = mm_nt(pick, w_ref[ab, 0]).astype(BF16)


def conv_body(half_ref, rec_ref, rim_ref, even_ref, odd_ref, grad_ref, part_ref, ze, zo):
    for a in range(3):
        for b in range(3):
            rows = slice((a * 3 + b) * 128, (a * 3 + b) * 128 + 128)
            for j in range(2):
                if a == 0:
                    tile = rim_ref[:, 2 * j + b]
                else:
                    tile = rec_ref[:, (a - 1) * 5 + 2 * j + b]
                tile = tile.reshape(128, 256)
                ze[rows, j * 128 : j * 128 + 128] = tile[:, :128]
                zo[rows, j * 128 : j * 128 + 128] = tile[:, 128:]
    center = mm(even_ref[...], ze[...])
    sides = mm(odd_ref[...], zo[...])
    error = rec_ref[pl.ds(half_ref[0] * 4, 4), 10:12].reshape(128, 256).astype(F32)
    lane = lax.broadcasted_iota(jnp.int32, (128, 128), 1)
    grads, nexts = [], []
    for j in range(2):
        cols = slice(j * 128, j * 128 + 128)
        before = jnp.where(lane == 0, 0.0, pltpu.roll(sides[128:, cols], 1, 1))
        preact = center[:, cols] + sides[:128, cols] + before
        sigma = jax.nn.sigmoid(preact)
        grad = (error[:, cols] * (sigma * (1.0 + preact * (1.0 - sigma)))).astype(BF16)
        grads.append(grad)
        shifted = jnp.where(lane == 127, 0.0, pltpu.roll(grad.astype(F32), 127, 1))
        nexts.append(shifted.astype(BF16))
    grad = jnp.concatenate(grads, 1)
    grad_ref[...] = grad
    i, j = iotas(128, 128)
    order = ones_where(j == (((i >> 2) & 3) << 5) + ((i >> 4) << 2) + (i & 3))
    grad = mm(order, grad).astype(BF16)
    after = mm(order, jnp.concatenate(nexts, 1)).astype(BF16)
    part_ref[:, 1152:2304] = mm_nt(grad, ze[...]).astype(BF16)
    part_ref[:, 2304:3456] = mm_nt(grad, zo[...]).astype(BF16)
    part_ref[:, 0:1152] = mm_nt(after, zo[...]).astype(BF16)


def rows_body(member_ref, all_ref, out_ref):
    y = member_ref[0]
    nxt = jnp.minimum(y + 1, 7)
    for h in range(2):
        for n, row in enumerate((y, nxt)):
            both = all_ref[4 * h + (row >> 1)].astype(F32)
            one = jnp.where((row & 1) == 0, both[:, :128], both[:, 128:])
            if n == 1:
                one = jnp.where(y == 7, 0.0, one)
            out_ref[n, h * 128 : h * 128 + 128] = one.astype(BF16)


def input_body(own_ref, up_ref, w_ref, out_ref):
    lane = lax.broadcasted_iota(jnp.int32, (128, 128), 1)
    i, j = iotas(256, 256)
    weave = ones_where(j == ((i & 127) << 1) + (i >> 7))
    taps = ((( 1, 0),), ((2, 0), (0, 1)))
    for ed in range(2):
        for er in range(2):
            sums = []
            for c in range(3):
                total = None
                for a, od in taps[ed]:
                    for b, pd in taps[er]:
                        grad = (up_ref if od else own_ref)[pd]
                        term = mm(w_ref[a * 3 + b, c], grad)
                        total = term if total is None else total + term
                sums.append(total)
            nxt = jnp.where(lane == 127, 0.0, pltpu.roll(sums[0], 127, 1))
            both = jnp.concatenate([sums[1].astype(BF16), (sums[2] + nxt).astype(BF16)], 1)
            out_ref[ed, er] = mm(both, weave).astype(BF16)


def shifted_2(value, axis, steps):
    count = lax.axis_size(axis)
    first, last = (max(0, -steps), min(count, count - steps))
    return lax.ppermute(value, axis, [(source, source + steps) for source in range(first, last)])


def exchange(value, axis, groups=None):
    return lax.all_to_all(
        value, axis, split_axis=0, concat_axis=0, axis_index_groups=groups, tiled=True
    )


def to_all(value, count):
    return jnp.broadcast_to(value[None], (count,) + value.shape)


def on_device(volume, weights, out_error):
    member = lax.axis_index("filt")
    half = (member // 4).astype(jnp.int32).reshape(1)
    taps = weights.reshape(9, 3, 128, 256)
    shape = jax.ShapeDtypeStruct
    mb = 1 << 20

    send = call(pack_body, shape((8, 12, 16, 256), BF16), [VMEM] * 2, (2 * mb, mb))(
        volume, out_error
    )
    received = exchange(send, "filt")
    even, odd = call(
        turn_body,
        (shape((128, 1152), BF16), shape((256, 1152), BF16)),
        [SMEM, VMEM],
        (226 * mb, 3 * mb),
    )(half, taps)
    rim = shifted_2(received[:, 5:10], "slab", 1)
    grad, part = call(
        conv_body,
        (shape((128, 256), BF16), shape((128, 3456), BF16)),
        [SMEM, VMEM, VMEM, VMEM, VMEM],
        (453 * mb, 4 * mb),
        [pltpu.VMEM((1152, 256), BF16), pltpu.VMEM((1152, 256), BF16)],
    )(half, received, rim, even, odd)

    pieces = exchange(part.reshape(8, 16, 3456), "slab", XC_GROUPS)
    piece = jnp.sum(pieces.astype(F32), 0).astype(BF16)
    rows = exchange(to_all(grad, 8), "filt")

    own = call(rows_body, shape((2, 256, 128), BF16), [SMEM, VMEM], (mb, mb))(
        member.astype(jnp.int32).reshape(1), rows
    )
    upper = shifted_2(own, "slab", -1)
    in_grad = call(
        input_body, shape((2, 2, 128, 256), BF16), [VMEM] * 3, (226 * mb, 3 * mb)
    )(own, upper, taps)
    in_grad = in_grad.transpose(0, 2, 1, 3)

    tiles = exchange(piece.reshape(4, 4, 3456), "filt", Y_GROUPS)
    tile = jnp.sum(tiles.astype(F32), 0).astype(BF16)
    tiles = exchange(to_all(tile, 8), "slab", Z_GROUPS)
    tile = (jnp.sum(tiles.astype(F32), 0) * (1.0 / 256.0)).astype(BF16)
    tiles = exchange(to_all(tile, 8), "slab", XC_GROUPS)
    tiles = tiles.astype(F32).reshape(32, 3, 3, 3, 128)
    weight_grad = tiles.transpose(2, 3, 1, 4, 0)
    return (in_grad, weight_grad)


def solution(mesh):
    in_specs = (P("slab", "filt", None, None), P(), P("slab", "filt", None, None))
    out_specs = (P("slab", None, "filt", None), P(None, None, None, None, "filt"))
    return jax.shard_map(
        on_device, mesh=mesh, in_specs=in_specs, out_specs=out_specs, check_vma=False
    )
```

time: 425 us -> 127 us (0.30)
  waiting for transfers between devices: 242 us -> 21.8 us
  matrix products: 80.7 us -> 0 us
  blocking collectives: 0 us -> 73.1 us
  local copies, waits for them, and re-layouts: 66.4 us -> 5.43 us
  between operations: 15 us -> 0.75 us
  starting transfers between devices: 14.5 us -> 20.7 us
    psum x1 -> x0, waiting for transfers between devices: 184 us -> none  [on_device(): weight_grad = lax.psum(weight_part, 'slab') * (1.0 / math.sqrt(count))]
    dot_general x81 -> x0, matrix products: 80.7 us -> none  [the longest x27 45.2 us: weight_taps(): jnp.einsum('dkhw,dfhw->kf', piece, grad, preferred_element_type=jnp.float32)]
    all_to_all x0 -> x4, blocking collectives: none -> 73.1 us  [exchange(): lax.all_to_all(value, axis, split_axis=0, concat_axis=0, axis_index_group...]
    all_gather x1 -> x0, waiting for transfers between devices: 51 us -> none  [on_device(): whole = lax.all_gather(extended, 'filt', axis=1, tiled=True)]
    unnamed x73 -> x8, local copies, waits for them, and re-layouts: 45.6 us -> 3.58 us
    slice x12 -> x1, local copies, waits for them, and re-layouts: 16.4 us -> 0.02 us  [on_device(): rim = shifted_2(received[:, 5:10], 'slab', 1)]
    all_to_all x1 -> x2, waiting for transfers between devices: 0.01 us -> 13.9 us  [exchange(): lax.all_to_all(value, axis, split_axis=0, concat_axis=0, axis_index_group...]
    all_to_all x1 -> x2, starting transfers between devices: 4.63 us -> 11.1 us  [exchange(): lax.all_to_all(value, axis, split_axis=0, concat_axis=0, axis_index_group...]
  transfers between devices with their start and end apart: 6 -> 4, of which waited for: 4 -> 3; matrix products, arithmetic and copies ran while one was open for 11% -> 1% of each run, Pallas kernels for 0% -> 1%
where the time goes in v1:
time: 127 us; the launch traced here: 126 us
  blocking collectives  73.1 us (58%)
  waiting for transfers between devices  21.8 us (17%)
  starting transfers between devices  20.7 us (16%)
  local copies, waits for them, and re-layouts  5.43 us (4%)
  Pallas kernels  3.98 us (3%)
    all_to_all x4, blocking collectives, exchange(): lax.all_to_all(value, axis, split_axis=0, concat_axis=0, axis_index_group...  73.1 us
    all_to_all x2, waiting for transfers between devices, exchange(): lax.all_to_all(value, axis, split_axis=0, concat_axis=0, axis_index_group...  13.9 us
    all_to_all x2, starting transfers between devices, exchange(): lax.all_to_all(value, axis, split_axis=0, concat_axis=0, axis_index_group...  11.1 us
    ppermute x2, starting transfers between devices, shifted_2(): lax.ppermute(value, axis, [(source, source + steps) for source in range(f...  9.63 us
    ppermute x2, waiting for transfers between devices, shifted_2(): lax.ppermute(value, axis, [(source, source + steps) for source in range(f...  7.9 us
    unnamed x8, local copies, waits for them, and re-layouts  3.58 us
  transfers between devices with their start and end apart: 4, of which 3 were waited for; matrix products, arithmetic and copies ran while one was open for 1% of the time, Pallas kernels for 1%

profile of v1, /device:TPU:1, one launch (start us, length us, event | category | flops | bytes accessed | tf_op | source)
XLA Modules:
  0.0 126.1 jit_solution(12366805931213927000)
XLA Ops:
  0.6 0.9 copy-done.1
  1.6 0.8 copy-done.2
  2.4 0.4 shard_map.50
  2.9 27.9 %all_to_all.30.rec_ref = bf16[8,12,16,256]{3,2,1,0:T(8,128)(2,1)S(1)} all-to-all(bf16[8,12,16,256]{3,2,1,0:T(8,128)(2,1)S(1)} %shard_map.50), channel_id=1, replica_groups=mesh['slab'=64,'filt'=8] {'filt'}, dimensions={0} | all-to-all | bytes 1572864 | tf_op jit(solution)/shard_map/all_to_all | solution.py:167
  30.8 7.6 %collective-permute-start = (bf16[8,5,16,256]{3,2,1,0:T(8,128)(2,1)S(1)}, bf16[8,5,16,256]{3,2,1,0:T(8,128)(2,1)S(1)}, u32[]{:S(2)}, u32[]{:S(2)}) collective-permute-start(bf16[8,5,16,256]{3,2,1,0:T(8,128)(2,1)S(1)} %slice.4), channel_id=1, source_target_pairs={{0,8},{8,16},{16,24},{24,32},{32,40},{40,48},{48,56},{56,64},{64,7... | collective-permute-start | bytes 983048 | tf_op jit(solution)/shard_map/ppermute | solution.py:163
  38.4 0.6 shard_map.51
  39.1 3.3 %collective-permute-done.rim_ref = bf16[8,5,16,256]{3,2,1,0:T(8,128)(2,1)S(1)} collective-permute-done((bf16[8,5,16,256]{3,2,1,0:T(8,128)(2,1)S(1)}, bf16[8,5,16,256]{3,2,1,0:T(8,128)(2,1)S(1)}, u32[]{:S(2)}, u32[]{:S(2)}) %collective-permute-start) | collective-permute-done | bytes 327712 | tf_op jit(solution)/shard_map/ppermute | solution.py:163
  42.4 1.7 %shard_map.52 = (bf16[128,256]{1,0:T(8,128)(2,1)S(1)}, bf16[128,3456]{1,0:T(8,128)(2,1)S(1)}) custom-call(s32[1]{0:T(128)} %bitcast.1.half_ref, bf16[8,12,16,256]{3,2,1,0:T(8,128)(2,1)S(1)} %all_to_all.30.rec_ref, bf16[8,5,16,256]{3,2,1,0:T(8,128)(2,1)S(1)} %collective-permute-done.rim_ref, bf16[128,1152]{1,0:T(8,128)(2,1)S(1)} %get-tuple-element.6.even_ref, ...), custom_call_target="tpu_custom_call" | custom-call | flops 475004928 | bytes 4194304 | tf_op jit(solution)/shard_map/pallas_call | solution.py:194
  44.2 23.0 %all_to_all.31 = bf16[8,16,3456]{2,1,0:T(8,128)(2,1)S(1)} all-to-all(bf16[8,16,3456]{2,1,0:T(8,128)(2,1)S(1)} %bitcast.9), channel_id=1, replica_groups={{0,8,128,136,256,264,384,392},{16,24,144,152,272,280,400,408},{32,40,16..., dimensions={0} | all-to-all | bytes 1769472 | tf_op jit(solution)/shard_map/all_to_all | solution.py:167
  67.2 0.1 reduce_sum.33
  67.4 7.1 %all_to_all.32 = bf16[4,4,3456]{2,1,0:T(4,128)(2,1)S(1)} all-to-all(bf16[4,4,3456]{2,1,0:T(4,128)(2,1)S(1)} %reshape.33), channel_id=1, replica_groups={{0,1,2,3},{4,5,6,7},{8,9,10,11},{12,13,14,15},{16,17,18,19},{20,21,22,2..., dimensions={0} | all-to-all | bytes 221184 | tf_op jit(solution)/shard_map/all_to_all | solution.py:167
  74.6 15.0 %all_to_all.33 = bf16[8,4,3456]{2,1,0:T(4,128)(2,1)S(1)} all-to-all(bf16[8,4,3456]{2,1,0:T(4,128)(2,1)S(1)} %broadcast_in_dim.7), channel_id=1, replica_groups={{0,16,32,48,64,80,96,112},{8,24,40,56,72,88,104,120},{128,144,160,176,1..., dimensions={0} | all-to-all | bytes 442368 | tf_op jit(solution)/shard_map/all_to_all | solution.py:167
  89.6 0.8 broadcast_in_dim.6
  90.4 3.5 %all-to-all-start.1 = ((bf16[8,128,256]{2,1,0:T(8,128)(2,1)}), bf16[8,128,256]{2,1,0:T(8,128)(2,1)S(1)}, u32[]{:S(2)}, u32[]{:S(2)}) async-start(bf16[8,128,256]{2,1,0:T(8,128)(2,1)} %broadcast_in_dim.6), calls=%async_computation.1 | async-start | bytes 1048576 | tf_op jit(solution)/shard_map/all_to_all | solution.py:167
  93.9 0.2 convert_reduce_fusion
  94.1 13.9 %all-to-all-done.1.all_ref = bf16[8,128,256]{2,1,0:T(8,128)(2,1)S(1)} async-done(((bf16[8,128,256]{2,1,0:T(8,128)(2,1)}), bf16[8,128,256]{2,1,0:T(8,128)(2,1)S(1)}, u32[]{:S(2)}, u32[]{:S(2)}) %all-to-all-start.1) | async-done | bytes 524320 | tf_op jit(solution)/shard_map/all_to_all | solution.py:167
  108.0 0.7 broadcast_in_dim.8
  108.8 7.6 %all-to-all-start.5 = ((bf16[8,4,3456]{2,1,0:T(4,128)(2,1)}), bf16[8,4,3456]{2,1,0:T(4,128)(2,1)S(1)}, u32[]{:S(2)}, u32[]{:S(2)}) async-start(bf16[8,4,3456]{2,1,0:T(4,128)(2,1)} %broadcast_in_dim.8), calls=%async_computation.5 | async-start | bytes 442368 | tf_op jit(solution)/shard_map/all_to_all | solution.py:167
  116.4 2.0 %collective-permute-start.1 = (bf16[2,256,128]{2,1,0:T(8,128)(2,1)S(1)}, bf16[2,256,128]{2,1,0:T(8,128)(2,1)S(1)}, u32[]{:S(2)}, u32[]{:S(2)}) collective-permute-start(bf16[2,256,128]{2,1,0:T(8,128)(2,1)S(1)} %shard_map.53.own_ref), channel_id=1, source_target_pairs={{8,0},{16,8},{24,16},{32,24},{40,32},{48,40},{56,48},{64,56},{72,6... | collective-permute-start | bytes 393224 | tf_op jit(solution)/shard_map/ppermute | solution.py:163
  118.4 4.5 %collective-permute-done.1.up_ref = bf16[2,256,128]{2,1,0:T(8,128)(2,1)S(1)} collective-permute-done((bf16[2,256,128]{2,1,0:T(8,128)(2,1)S(1)}, bf16[2,256,128]{2,1,0:T(8,128)(2,1)S(1)}, u32[]{:S(2)}, u32[]{:S(2)}) %collective-permute-start.1) | collective-permute-done | bytes 131104 | tf_op jit(solution)/shard_map/ppermute | solution.py:163
  123.0 1.2 shard_map.54
  124.1 1.0 copy.14
  125.1 0.2 reshape.35
  125.3 0.8 copy.15
  (11 shorter events, 0.2 us)
Async XLA Ops:
  0.6 1.0 copy-start.1
  1.6 0.8 copy-start.2
  2.4 36.0 %copy-start = (bf16[3,3,3,128,256]{4,3,2,1,0:T(8,128)(2,1)S(1)}, bf16[3,3,3,128,256]{4,3,2,1,0:T(8,128)(2,1)}, u32[]{:S(2)}) copy-start(bf16[3,3,3,128,256]{4,3,2,1,0:T(8,128)(2,1)} %param.4) | copy-start | bytes 5308420
  30.8 11.6 %collective-permute-start = (bf16[8,5,16,256]{3,2,1,0:T(8,128)(2,1)S(1)}, bf16[8,5,16,256]{3,2,1,0:T(8,128)(2,1)S(1)}, u32[]{:S(2)}, u32[]{:S(2)}) collective-permute-start(bf16[8,5,16,256]{3,2,1,0:T(8,128)(2,1)S(1)} %slice.4), channel_id=1, source_target_pairs={{0,8},{8,16},{16,24},{24,32},{32,40},{40,48},{48,56},{56,64},{64,7... | collective-permute-start | bytes 983048 | tf_op jit(solution)/shard_map/ppermute | solution.py:163
  90.4 17.6 %all-to-all-start.1 = ((bf16[8,128,256]{2,1,0:T(8,128)(2,1)}), bf16[8,128,256]{2,1,0:T(8,128)(2,1)S(1)}, u32[]{:S(2)}, u32[]{:S(2)}) async-start(bf16[8,128,256]{2,1,0:T(8,128)(2,1)} %broadcast_in_dim.6), calls=%async_computation.1 | async-start | bytes 1048576 | tf_op jit(solution)/shard_map/all_to_all | solution.py:167
  108.8 16.3 %all-to-all-start.5 = ((bf16[8,4,3456]{2,1,0:T(4,128)(2,1)}), bf16[8,4,3456]{2,1,0:T(4,128)(2,1)S(1)}, u32[]{:S(2)}, u32[]{:S(2)}) async-start(bf16[8,4,3456]{2,1,0:T(4,128)(2,1)} %broadcast_in_dim.8), calls=%async_computation.5 | async-start | bytes 442368 | tf_op jit(solution)/shard_map/all_to_all | solution.py:167
  116.4 6.6 %collective-permute-start.1 = (bf16[2,256,128]{2,1,0:T(8,128)(2,1)S(1)}, bf16[2,256,128]{2,1,0:T(8,128)(2,1)S(1)}, u32[]{:S(2)}, u32[]{:S(2)}) collective-permute-start(bf16[2,256,128]{2,1,0:T(8,128)(2,1)S(1)} %shard_map.53.own_ref), channel_id=1, source_target_pairs={{8,0},{16,8},{24,16},{32,24},{40,32},{48,40},{56,48},{64,56},{72,6... | collective-permute-start | bytes 393224 | tf_op jit(solution)/shard_map/ppermute | solution.py:163

commit v2 on v1

v2 whole, which is shorter than its diff:
```python
import jax
import jax.numpy as jnp
from jax import lax
from jax.experimental import pallas as pl
from jax.experimental.pallas import tpu as pltpu
from jax.sharding import PartitionSpec as P

F32 = jnp.float32
BF16 = jnp.bfloat16
VMEM = pl.BlockSpec(memory_space=pltpu.VMEM)
SMEM = pl.BlockSpec(memory_space=pltpu.SMEM)
LIMIT = 48 * 1024 * 1024

NX, NZ, NC = 4, 8, 2
X_GROUPS = [[(x * NZ + z) * NC + c for x in range(NX)] for z in range(NZ) for c in range(NC)]
XC_GROUPS = [[(x * NZ + z) * NC + c for x in range(NX) for c in range(NC)] for z in range(NZ)]
Z_GROUPS = [[(x * NZ + z) * NC + c for z in range(NZ)] for x in range(NX) for c in range(NC)]
CORE_PAIRS = [(s, s ^ 1) for s in range(NX * NZ * NC)]


def call(body, out_shape, in_specs, cost, scratch=()):
    many = isinstance(out_shape, (tuple, list))
    return pl.pallas_call(
        body,
        out_shape=out_shape,
        in_specs=in_specs,
        out_specs=[VMEM] * len(out_shape) if many else VMEM,
        scratch_shapes=list(scratch),
        compiler_params=pltpu.CompilerParams(vmem_limit_bytes=LIMIT),
        cost_estimate=pl.CostEstimate(flops=cost[0], bytes_accessed=cost[1], transcendentals=0),
    )


def mm(left, right):
    return jnp.dot(left, right, preferred_element_type=F32)


def mm_nt(left, right):
    return lax.dot_general(left, right, (((1,), (1,)), ((), ())), preferred_element_type=F32)


def ones_where(cond):
    return jnp.where(cond, 1.0, 0.0).astype(BF16)


def iotas(rows, cols):
    return (
        lax.broadcasted_iota(jnp.int32, (rows, cols), 0),
        lax.broadcasted_iota(jnp.int32, (rows, cols), 1),
    )


def pack_body(vol_ref, err_ref, send_ref):
    i, j = iotas(256, 256)
    row_first = ones_where(j == ((i & 15) << 4) + (i >> 4))
    even_odd = ones_where(i == ((j & 127) << 1) + (j >> 7))
    error_rows = ones_where(j == ((i & 31) << 3) + (i >> 5))
    for p in range(2):
        plane = vol_ref[p].reshape(256, 256)
        plane = mm(row_first, plane).astype(BF16)
        plane = mm(plane, even_odd).astype(BF16)
        for y in range(8):
            for b in range(3):
                row = 2 * y - 1 + b
                if row < 0:
                    piece = jnp.zeros((16, 256), BF16)
                else:
                    piece = plane[row * 16 : row * 16 + 16]
                send_ref[y, p * 3 + b] = piece
    error = mm(error_rows, err_ref[0].reshape(256, 128)).astype(BF16)
    for y in range(8):
        for u in range(2):
            start = y * 32 + u * 16
            send_ref[y, 6, :, u * 128 : u * 128 + 128] = error[start : start + 16]


def turn_body(w_ref, even_ref, odd_ref):
    i, j = iotas(256, 256)
    same = ones_where(i == j)
    for ab in range(9):
        cols = slice(ab * 128, ab * 128 + 128)
        even_ref[:, cols] = mm_nt(same, w_ref[ab, 1]).astype(BF16)
        odd_ref[:256, cols] = mm_nt(same, w_ref[ab, 2]).astype(BF16)
        odd_ref[256:, cols] = mm_nt(same, w_ref[ab, 0]).astype(BF16)


def core_rows(core):
    i, j = iotas(128, 256)
    return ones_where(j == (((i >> 2) & 7) << 5) + ((i >> 5) << 3) + (i & 3) + core * 4)


def taps_of(order, both, ze, zo):
    now = mm(order, both[:, :128]).astype(BF16)
    after = mm(order, both[:, 128:]).astype(BF16)
    return mm_nt(after, zo[...]), mm_nt(now, ze[...]), mm_nt(now, zo[...])


def conv_body(core_ref, rec_ref, rim_ref, even_ref, odd_ref, grad_ref, both_ref, ze, zo, part_ref):
    for a in range(3):
        for b in range(3):
            rows = slice((a * 3 + b) * 128, (a * 3 + b) * 128 + 128)
            tile = rim_ref[:, b] if a == 0 else rec_ref[:, (a - 1) * 3 + b]
            tile = tile.reshape(128, 256)
            ze[rows] = tile[:, :128]
            zo[rows] = tile[:, 128:]
    center = mm(even_ref[...], ze[...])
    sides = mm(odd_ref[...], zo[...])
    errors = []
    for y in range(8):
        errors += [rec_ref[y, 6][:, :128], rec_ref[y, 6][:, 128:]]
    error = jnp.concatenate(errors, 0).astype(F32)
    lane = lax.broadcasted_iota(jnp.int32, (256, 128), 1)
    before = jnp.where(lane == 0, 0.0, pltpu.roll(sides[256:], 1, 1))
    preact = center + sides[:256] + before
    sigma = jax.nn.sigmoid(preact)
    grad = (error * (sigma * (1.0 + preact * (1.0 - sigma)))).astype(BF16)
    grad_ref[...] = grad
    after = jnp.where(lane == 127, 0.0, pltpu.roll(grad.astype(F32), 127, 1)).astype(BF16)
    both = jnp.concatenate([grad, after], 1)
    both_ref[...] = both
    parts = taps_of(core_rows(1 - core_ref[0]), both, ze, zo)
    for c in range(3):
        part_ref[:, c * 1152 : c * 1152 + 1152] = parts[c].astype(BF16)


def keep_body(core_ref, both_ref, ze, zo, other_ref, part_ref):
    parts = taps_of(core_rows(core_ref[0]), both_ref[...], ze, zo)
    for c in range(3):
        cols = slice(c * 1152, c * 1152 + 1152)
        part_ref[:, cols] = (parts[c] + other_ref[:, cols].astype(F32)).astype(BF16)


def sum_body(in_ref, out_ref):
    total = in_ref[0].astype(F32)
    for n in range(1, in_ref.shape[0]):
        total = total + in_ref[n].astype(F32)
    out_ref[...] = total.astype(BF16)


def input_body(own_ref, up_ref, w_ref, out_ref):
    lane = lax.broadcasted_iota(jnp.int32, (128, 128), 1)
    i, j = iotas(256, 256)
    weave = ones_where(j == ((i & 127) << 1) + (i >> 7))
    taps = ((( 1, 0),), ((2, 0), (0, 1)))
    for ed in range(2):
        for er in range(2):
            sums = []
            for c in range(3):
                total = None
                for a, od in taps[ed]:
                    for b, pd in taps[er]:
                        grad = (up_ref if od else own_ref)[pd]
                        term = mm(w_ref[a * 3 + b, c], grad)
                        total = term if total is None else total + term
                sums.append(total)
            nxt = jnp.where(lane == 127, 0.0, pltpu.roll(sums[0], 127, 1))
            both = jnp.concatenate([sums[1].astype(BF16), (sums[2] + nxt).astype(BF16)], 1)
            out_ref[ed, er] = mm(both, weave).astype(BF16)


def shifted_2(value, axis, steps):
    count = lax.axis_size(axis)
    first, last = (max(0, -steps), min(count, count - steps))
    return lax.ppermute(value, axis, [(source, source + steps) for source in range(first, last)])


def exchange(value, axis, groups=None):
    return lax.all_to_all(
        value, axis, split_axis=0, concat_axis=0, axis_index_groups=groups, tiled=True
    )


def to_all(value, count):
    return jnp.broadcast_to(value[None], (count,) + value.shape)


def add_up(value):
    size = value.size * 2
    return call(sum_body, jax.ShapeDtypeStruct(value.shape[1:], BF16), [VMEM], (size, size))(value)


def on_device(volume, weights, out_error):
    core = (lax.axis_index("slab") & 1).astype(jnp.int32).reshape(1)
    taps = weights.reshape(9, 3, 128, 256)
    shape = jax.ShapeDtypeStruct
    mb = 1 << 20

    send = call(pack_body, shape((8, 7, 16, 256), BF16), [VMEM] * 2, (2 * mb, mb))(
        volume, out_error
    )
    received = exchange(send, "filt")
    even, odd = call(
        turn_body, (shape((256, 1152), BF16), shape((512, 1152), BF16)), [VMEM], (452 * mb, 4 * mb)
    )(taps)
    rim = shifted_2(received[:, 3:6], "slab", 1)
    stack = shape((1152, 128), BF16)
    grad, both, ze, zo, part = call(
        conv_body,
        (shape((256, 128), BF16), shape((256, 256), BF16), stack, stack, shape((128, 3456), BF16)),
        [SMEM, VMEM, VMEM, VMEM, VMEM],
        (453 * mb, 4 * mb),
    )(core, received, rim, even, odd)

    other = lax.ppermute(part, "slab", CORE_PAIRS)
    right = shifted_2(grad, "filt", -1)
    part = call(
        keep_body, shape((128, 3456), BF16), [SMEM, VMEM, VMEM, VMEM, VMEM], (113 * mb, 3 * mb)
    )(core, both, ze, zo, other)
    piece = add_up(exchange(part.reshape(4, 32, 3456), "slab", X_GROUPS))

    own = jnp.stack([grad, right])
    upper = shifted_2(own, "slab", -1)
    in_grad = call(
        input_body, shape((2, 2, 128, 256), BF16), [VMEM] * 3, (226 * mb, 3 * mb)
    )(own, upper, taps)
    in_grad = in_grad.transpose(0, 2, 1, 3)

    tile = add_up(exchange(piece.reshape(8, 4, 3456), "filt"))
    tile = add_up(exchange(to_all(tile, 8), "slab", Z_GROUPS))
    tiles = exchange(to_all(tile, 8), "slab", XC_GROUPS)
    tiles = tiles.astype(F32).reshape(32, 3, 3, 3, 128) * (1.0 / 256.0)
    weight_grad = tiles.transpose(2, 3, 1, 4, 0)
    return (in_grad, weight_grad)


def solution(mesh):
    in_specs = (P("slab", "filt", None, None), P(), P("slab", "filt", None, None))
    out_specs = (P("slab", None, "filt", None), P(None, None, None, None, "filt"))
    return jax.shard_map(
        on_device, mesh=mesh, in_specs=in_specs, out_specs=out_specs, check_vma=False
    )
```

time: 127 us -> 108 us (0.85)
  blocking collectives: 73.1 us -> 54.4 us
  waiting for transfers between devices: 21.8 us -> 16.1 us
  starting transfers between devices: 20.7 us -> 26.1 us
    all_to_all x4 -> x3, blocking collectives: 73.1 us -> 54.4 us  [exchange(): lax.all_to_all(value, axis, split_axis=0, concat_axis=0, axis_index_group...]
    all_to_all x2, waiting for transfers between devices: 13.9 us -> 7.66 us  [exchange(): lax.all_to_all(value, axis, split_axis=0, concat_axis=0, axis_index_group...]
    all_to_all x2, starting transfers between devices: 11.1 us -> 13.8 us  [exchange(): lax.all_to_all(value, axis, split_axis=0, concat_axis=0, axis_index_group...]
    ppermute x0 -> x1, waiting for transfers between devices: none -> 2.39 us  [on_device(): other = lax.ppermute(part, 'slab', CORE_PAIRS)]
    ppermute x0 -> x1, starting transfers between devices: none -> 1.92 us  [on_device(): other = lax.ppermute(part, 'slab', CORE_PAIRS)]
    ppermute x2 -> x3, waiting for transfers between devices: 7.9 us -> 6.04 us  [shifted_2(): lax.ppermute(value, axis, [(source, source + steps) for source in range(f...]
    pallas_call x4 -> x7, Pallas kernels: 2.82 us -> 3.67 us  [the longest x1 1.46 us: on_device(): call(conv_body, (shape((256, 128), BF16), shape((256, 256), BF16), stack,...]
    ppermute x2 -> x3, starting transfers between devices: 9.63 us -> 10.4 us  [shifted_2(): lax.ppermute(value, axis, [(source, source + steps) for source in range(f...]
  transfers between devices with their start and end apart: 4 -> 6, of which waited for: 3 -> 4; matrix products, arithmetic and copies ran while one was open for 1% -> 2% of each run, Pallas kernels for 1% -> 2%
where the time goes in v2:
time: 108 us
  blocking collectives  54.4 us (50%)
  starting transfers between devices  26.1 us (24%)
  waiting for transfers between devices  16.1 us (15%)
  local copies, waits for them, and re-layouts  5.42 us (5%)
  Pallas kernels  4.83 us (4%)
    all_to_all x3, blocking collectives, exchange(): lax.all_to_all(value, axis, split_axis=0, concat_axis=0, axis_index_group...  54.4 us
    all_to_all x2, starting transfers between devices, exchange(): lax.all_to_all(value, axis, split_axis=0, concat_axis=0, axis_index_group...  13.8 us
    ppermute x3, starting transfers between devices, shifted_2(): lax.ppermute(value, axis, [(source, source + steps) for source in range(f...  10.4 us
    all_to_all x2, waiting for transfers between devices, exchange(): lax.all_to_all(value, axis, split_axis=0, concat_axis=0, axis_index_group...  7.66 us
    ppermute x3, waiting for transfers between devices, shifted_2(): lax.ppermute(value, axis, [(source, source + steps) for source in range(f...  6.04 us
    unnamed x8, local copies, waits for them, and re-layouts  3.58 us
    ppermute x1, waiting for transfers between devices, on_device(): other = lax.ppermute(part, 'slab', CORE_PAIRS)  2.39 us
  transfers between devices with their start and end apart: 6, of which 4 were waited for; matrix products, arithmetic and copies ran while one was open for 2% of the time, Pallas kernels for 2%

profile of v2, /device:TPU:1, one launch (start us, length us, event | category | flops | bytes accessed | tf_op | source)
XLA Modules:
  0.0 107.7 jit_solution(7974864561008684645)
XLA Ops:
  0.6 0.9 copy-done.1
  1.6 0.8 copy-done.2
  2.4 0.4 shard_map.50
  2.9 21.4 %all_to_all.25.rec_ref = bf16[8,7,16,256]{3,2,1,0:T(8,128)(2,1)S(1)} all-to-all(bf16[8,7,16,256]{3,2,1,0:T(8,128)(2,1)S(1)} %shard_map.50), channel_id=1, replica_groups=mesh['slab'=64,'filt'=8] {'filt'}, dimensions={0} | all-to-all | bytes 917504 | tf_op jit(solution)/shard_map/all_to_all | solution.py:168
  24.3 7.1 %collective-permute-start = (bf16[8,3,16,256]{3,2,1,0:T(8,128)(2,1)S(1)}, bf16[8,3,16,256]{3,2,1,0:T(8,128)(2,1)S(1)}, u32[]{:S(2)}, u32[]{:S(2)}) collective-permute-start(bf16[8,3,16,256]{3,2,1,0:T(8,128)(2,1)S(1)} %slice.4), channel_id=1, source_target_pairs={{0,8},{8,16},{16,24},{24,32},{32,40},{40,48},{48,56},{56,64},{64,7... | collective-permute-start | bytes 589832 | tf_op jit(solution)/shard_map/ppermute | solution.py:164
  31.4 1.1 %shard_map.51 = (bf16[256,1152]{1,0:T(8,128)(2,1)S(1)}, bf16[512,1152]{1,0:T(8,128)(2,1)S(1)}) custom-call(bf16[9,3,128,256]{3,2,1,0:T(8,128)(2,1)S(1)} %bitcast.7), custom_call_target="tpu_custom_call" | custom-call | flops 473956352 | bytes 4194304 | tf_op jit(solution)/shard_map/pallas_call | solution.py:192
  32.5 1.5 %collective-permute-done.rim_ref = bf16[8,3,16,256]{3,2,1,0:T(8,128)(2,1)S(1)} collective-permute-done((bf16[8,3,16,256]{3,2,1,0:T(8,128)(2,1)S(1)}, bf16[8,3,16,256]{3,2,1,0:T(8,128)(2,1)S(1)}, u32[]{:S(2)}, u32[]{:S(2)}) %collective-permute-start) | collective-permute-done | bytes 196640 | tf_op jit(solution)/shard_map/ppermute | solution.py:164
  34.0 1.5 %shard_map.52 = (bf16[256,128]{1,0:T(8,128)(2,1)S(1)}, bf16[256,256]{1,0:T(8,128)(2,1)S(1)}, bf16[1152,128]{1,0:T(8,128)(2,1)S(1)}, bf16[1152,128]{1,0:T(8,128)(2,1)S(1)}, bf16[128,3456]{1,0:T(8,128)(2,1)S(1)}) custom-call(s32[1]{0:T(128)} %bitcast.core_ref, bf16[8,7,16,256]{3,2,1,0:T(8,128)(2,1)S(1)} %all_to_all.25.rec_ref, ...), custom_call_target="tpu_custom_call" | custom-call | flops 475004928 | bytes 4194304 | tf_op jit(solution)/shard_map/pallas_call | solution.py:197
  35.4 1.9 %collective-permute-start.3 = (bf16[128,3456]{1,0:T(8,128)(2,1)S(1)}, bf16[128,3456]{1,0:T(8,128)(2,1)S(1)}, u32[]{:S(2)}, u32[]{:S(2)}) collective-permute-start(bf16[128,3456]{1,0:T(8,128)(2,1)S(1)} %get-tuple-element.15), channel_id=1, source_target_pairs={{0,8},{8,0},{16,24},{24,16},{32,40},{40,32},{48,56},{56,48},{64,72... | collective-permute-start | bytes 2654216 | tf_op jit(solution)/shard_map/ppermute | solution.py:204
  37.4 2.4 %collective-permute-done.3.other_ref = bf16[128,3456]{1,0:T(8,128)(2,1)S(1)} collective-permute-done((bf16[128,3456]{1,0:T(8,128)(2,1)S(1)}, bf16[128,3456]{1,0:T(8,128)(2,1)S(1)}, u32[]{:S(2)}, u32[]{:S(2)}) %collective-permute-start.3) | collective-permute-done | bytes 884768 | tf_op jit(solution)/shard_map/ppermute | solution.py:204
  39.8 0.5 shard_map.54
  40.3 21.4 %all_to_all.26.in_ref = bf16[4,32,3456]{2,1,0:T(8,128)(2,1)S(1)} all-to-all(bf16[4,32,3456]{2,1,0:T(8,128)(2,1)S(1)} %bitcast.9), channel_id=1, replica_groups={{0,128,256,384},{8,136,264,392},{16,144,272,400},{24,152,280,408},{32,1..., dimensions={0} | all-to-all | bytes 1769472 | tf_op jit(solution)/shard_map/all_to_all | solution.py:168
  61.9 11.6 %all_to_all.27.in_ref = bf16[8,4,3456]{2,1,0:T(4,128)(2,1)S(1)} all-to-all(bf16[8,4,3456]{2,1,0:T(4,128)(2,1)S(1)} %reshape.24), channel_id=1, replica_groups=mesh['slab'=64,'filt'=8] {'filt'}, dimensions={0} | all-to-all | bytes 442368 | tf_op jit(solution)/shard_map/all_to_all | solution.py:168
  73.5 0.7 broadcast_in_dim.4
  74.3 5.9 %all-to-all-start.3 = ((bf16[8,4,3456]{2,1,0:T(4,128)(2,1)}), bf16[8,4,3456]{2,1,0:T(4,128)(2,1)S(1)}, u32[]{:S(2)}, u32[]{:S(2)}) async-start(bf16[8,4,3456]{2,1,0:T(4,128)(2,1)} %broadcast_in_dim.4), calls=%async_computation.3 | async-start | bytes 442368 | tf_op jit(solution)/shard_map/all_to_all | solution.py:168
  80.2 1.3 %collective-permute-start.1 = (bf16[256,128]{1,0:T(8,128)(2,1)S(1)}, bf16[256,128]{1,0:T(8,128)(2,1)S(1)}, u32[]{:S(2)}, u32[]{:S(2)}) collective-permute-start(bf16[256,128]{1,0:T(8,128)(2,1)S(1)} %get-tuple-element.11), channel_id=1, source_target_pairs={{1,0},{2,1},{3,2},{4,3},{5,4},{6,5},{7,6},{9,8},{10,9},{11,10},{12... | collective-permute-start | bytes 196616 | tf_op jit(solution)/shard_map/ppermute | solution.py:164
  81.5 7.7 %all-to-all-done.3.in_ref = bf16[8,4,3456]{2,1,0:T(4,128)(2,1)S(1)} async-done(((bf16[8,4,3456]{2,1,0:T(4,128)(2,1)}), bf16[8,4,3456]{2,1,0:T(4,128)(2,1)S(1)}, u32[]{:S(2)}, u32[]{:S(2)}) %all-to-all-start.3) | async-done | bytes 221216 | tf_op jit(solution)/shard_map/all_to_all | solution.py:168
  89.2 0.7 broadcast_in_dim.5
  89.9 7.9 %all-to-all-start.4 = ((bf16[8,4,3456]{2,1,0:T(4,128)(2,1)}), bf16[8,4,3456]{2,1,0:T(4,128)(2,1)S(1)}, u32[]{:S(2)}, u32[]{:S(2)}) async-start(bf16[8,4,3456]{2,1,0:T(4,128)(2,1)} %broadcast_in_dim.5), calls=%async_computation.4 | async-start | bytes 442368 | tf_op jit(solution)/shard_map/all_to_all | solution.py:168
  97.8 2.0 %collective-permute-start.2 = (bf16[2,256,128]{2,1,0:T(8,128)(2,1)S(1)}, bf16[2,256,128]{2,1,0:T(8,128)(2,1)S(1)}, u32[]{:S(2)}, u32[]{:S(2)}) collective-permute-start(bf16[2,256,128]{2,1,0:T(8,128)(2,1)S(1)} %pad_maximum_fusion.own_ref), channel_id=1, source_target_pairs={{8,0},{16,8},{24,16},{32,24},{40,32},{48,40},{56,48},{64,56},{72,6... | collective-permute-start | bytes 393224 | tf_op jit(solution)/shard_map/ppermute | solution.py:164
  99.9 4.5 %collective-permute-done.2.up_ref = bf16[2,256,128]{2,1,0:T(8,128)(2,1)S(1)} collective-permute-done((bf16[2,256,128]{2,1,0:T(8,128)(2,1)S(1)}, bf16[2,256,128]{2,1,0:T(8,128)(2,1)S(1)}, u32[]{:S(2)}, u32[]{:S(2)}) %collective-permute-start.2) | collective-permute-done | bytes 131104 | tf_op jit(solution)/shard_map/ppermute | solution.py:164
  104.4 1.2 %shard_map.53 = bf16[2,2,128,256]{3,2,1,0:T(8,128)(2,1)S(1)} custom-call(bf16[2,256,128]{2,1,0:T(8,128)(2,1)S(1)} %pad_maximum_fusion.own_ref, bf16[2,256,128]{2,1,0:T(8,128)(2,1)S(1)} %collective-permute-done.2.up_ref, bf16[9,3,128,256]{3,2,1,0:T(8,128)(2,1)S(1)} %bitcast.8), custom_call_target="tpu_custom_call" | custom-call | flops 236978176 | bytes 3145728 | tf_op jit(solution)/shard_map/pallas_call | solution.py:213
  105.6 1.0 copy.6
  106.9 0.8 copy.7
  (14 shorter events, 0.7 us)
Async XLA Ops:
  0.6 1.0 copy-start.1
  1.6 0.8 copy-start.2
  2.4 29.0 %copy-start = (bf16[3,3,3,128,256]{4,3,2,1,0:T(8,128)(2,1)S(1)}, bf16[3,3,3,128,256]{4,3,2,1,0:T(8,128)(2,1)}, u32[]{:S(2)}) copy-start(bf16[3,3,3,128,256]{4,3,2,1,0:T(8,128)(2,1)} %param.4) | copy-start | bytes 5308420
  24.3 9.7 %collective-permute-start = (bf16[8,3,16,256]{3,2,1,0:T(8,128)(2,1)S(1)}, bf16[8,3,16,256]{3,2,1,0:T(8,128)(2,1)S(1)}, u32[]{:S(2)}, u32[]{:S(2)}) collective-permute-start(bf16[8,3,16,256]{3,2,1,0:T(8,128)(2,1)S(1)} %slice.4), channel_id=1, source_target_pairs={{0,8},{8,16},{16,24},{24,32},{32,40},{40,48},{48,56},{56,64},{64,7... | collective-permute-start | bytes 589832 | tf_op jit(solution)/shard_map/ppermute | solution.py:164
  35.4 4.3 %collective-permute-start.3 = (bf16[128,3456]{1,0:T(8,128)(2,1)S(1)}, bf16[128,3456]{1,0:T(8,128)(2,1)S(1)}, u32[]{:S(2)}, u32[]{:S(2)}) collective-permute-start(bf16[128,3456]{1,0:T(8,128)(2,1)S(1)} %get-tuple-element.15), channel_id=1, source_target_pairs={{0,8},{8,0},{16,24},{24,16},{32,40},{40,32},{48,56},{56,48},{64,72... | collective-permute-start | bytes 2654216 | tf_op jit(solution)/shard_map/ppermute | solution.py:204
  74.3 14.8 %all-to-all-start.3 = ((bf16[8,4,3456]{2,1,0:T(4,128)(2,1)}), bf16[8,4,3456]{2,1,0:T(4,128)(2,1)S(1)}, u32[]{:S(2)}, u32[]{:S(2)}) async-start(bf16[8,4,3456]{2,1,0:T(4,128)(2,1)} %broadcast_in_dim.4), calls=%async_computation.3 | async-start | bytes 442368 | tf_op jit(solution)/shard_map/all_to_all | solution.py:168
  80.2 17.6 %collective-permute-start.1 = (bf16[256,128]{1,0:T(8,128)(2,1)S(1)}, bf16[256,128]{1,0:T(8,128)(2,1)S(1)}, u32[]{:S(2)}, u32[]{:S(2)}) collective-permute-start(bf16[256,128]{1,0:T(8,128)(2,1)S(1)} %get-tuple-element.11), channel_id=1, source_target_pairs={{1,0},{2,1},{3,2},{4,3},{5,4},{6,5},{7,6},{9,8},{10,9},{11,10},{12... | collective-permute-start | bytes 196616 | tf_op jit(solution)/shard_map/ppermute | solution.py:164
  89.9 16.6 %all-to-all-start.4 = ((bf16[8,4,3456]{2,1,0:T(4,128)(2,1)}), bf16[8,4,3456]{2,1,0:T(4,128)(2,1)S(1)}, u32[]{:S(2)}, u32[]{:S(2)}) async-start(bf16[8,4,3456]{2,1,0:T(4,128)(2,1)} %broadcast_in_dim.5), calls=%async_computation.4 | async-start | bytes 442368 | tf_op jit(solution)/shard_map/all_to_all | solution.py:168
  97.8 6.6 %collective-permute-start.2 = (bf16[2,256,128]{2,1,0:T(8,128)(2,1)S(1)}, bf16[2,256,128]{2,1,0:T(8,128)(2,1)S(1)}, u32[]{:S(2)}, u32[]{:S(2)}) collective-permute-start(bf16[2,256,128]{2,1,0:T(8,128)(2,1)S(1)} %pad_maximum_fusion.own_ref), channel_id=1, source_target_pairs={{8,0},{16,8},{24,16},{32,24},{40,32},{48,40},{56,48},{64,56},{72,6... | collective-permute-start | bytes 393224 | tf_op jit(solution)/shard_map/ppermute | solution.py:164

commit v3 on v2

--- a/solution.py
+++ b/solution.py
@@ -8,6 +8,7 @@
 F32 = jnp.float32
 BF16 = jnp.bfloat16
 VMEM = pl.BlockSpec(memory_space=pltpu.VMEM)
+ANY = pl.BlockSpec(memory_space=pl.ANY)
 SMEM = pl.BlockSpec(memory_space=pltpu.SMEM)
 LIMIT = 48 * 1024 * 1024
 
@@ -18,7 +19,7 @@
 CORE_PAIRS = [(s, s ^ 1) for s in range(NX * NZ * NC)]
 
 
-def call(body, out_shape, in_specs, cost, scratch=()):
+def call(body, out_shape, in_specs, cost, scratch=(), limit=LIMIT):
     many = isinstance(out_shape, (tuple, list))
     return pl.pallas_call(
         body,
@@ -26,7 +27,7 @@
         in_specs=in_specs,
         out_specs=[VMEM] * len(out_shape) if many else VMEM,
         scratch_shapes=list(scratch),
-        compiler_params=pltpu.CompilerParams(vmem_limit_bytes=LIMIT),
+        compiler_params=pltpu.CompilerParams(vmem_limit_bytes=limit),
         cost_estimate=pl.CostEstimate(flops=cost[0], bytes_accessed=cost[1], transcendentals=0),
     )
 
@@ -50,11 +51,18 @@
     )
 
 
-def pack_body(vol_ref, err_ref, send_ref):
+def pack_body(vol_hbm, err_hbm, send_ref, vol_ref, err_ref, sems):
+    copies = [
+        pltpu.make_async_copy(vol_hbm, vol_ref, sems.at[0]),
+        pltpu.make_async_copy(err_hbm, err_ref, sems.at[1]),
+    ]
+    for copy in copies:
+        copy.start()
     i, j = iotas(256, 256)
     row_first = ones_where(j == ((i & 15) << 4) + (i >> 4))
     even_odd = ones_where(i == ((j & 127) << 1) + (j >> 7))
     error_rows = ones_where(j == ((i & 31) << 3) + (i >> 5))
+    copies[0].wait()
     for p in range(2):
         plane = vol_ref[p].reshape(256, 256)
         plane = mm(row_first, plane).astype(BF16)
@@ -67,6 +75,7 @@
                 else:
                     piece = plane[row * 16 : row * 16 + 16]
                 send_ref[y, p * 3 + b] = piece
+    copies[1].wait()
     error = mm(error_rows, err_ref[0].reshape(256, 128)).astype(BF16)
     for y in range(8):
         for u in range(2):
@@ -134,7 +143,21 @@
     total = in_ref[0].astype(F32)
     for n in range(1, in_ref.shape[0]):
         total = total + in_ref[n].astype(F32)
-    out_ref[...] = total.astype(BF16)
+    total = total.astype(BF16)
+    if len(out_ref.shape) == len(total.shape):
+        out_ref[...] = total
+    else:
+        for n in range(out_ref.shape[0]):
+            out_ref[n] = total
+
+
+def last_body(in_ref, out_ref):
+    for m in range(8):
+        rows = in_ref[m].astype(F32) * (1.0 / 256.0)
+        for c in range(3):
+            for ab in range(9):
+                start = (c * 9 + ab) * 128
+                out_ref[ab * 3 + c, 4 * m : 4 * m + 4] = rows[:, start : start + 128]
 
 
 def input_body(own_ref, up_ref, w_ref, out_ref):
@@ -170,13 +193,10 @@
     )
 
 
-def to_all(value, count):
-    return jnp.broadcast_to(value[None], (count,) + value.shape)
-
-
-def add_up(value):
+def add_up(value, copies=()):
     size = value.size * 2
-    return call(sum_body, jax.ShapeDtypeStruct(value.shape[1:], BF16), [VMEM], (size, size))(value)
+    out_shape = jax.ShapeDtypeStruct(copies + value.shape[1:], BF16)
+    return call(sum_body, out_shape, [VMEM], (size, size))(value)
 
 
 def on_device(volume, weights, out_error):
@@ -185,9 +205,18 @@
     shape = jax.ShapeDtypeStruct
     mb = 1 << 20
 
-    send = call(pack_body, shape((8, 7, 16, 256), BF16), [VMEM] * 2, (2 * mb, mb))(
-        volume, out_error
-    )
+    send = call(
+        pack_body,
+        shape((8, 7, 16, 256), BF16),
+        [ANY] * 2,
+        (2 * mb, mb),
+        [
+            pltpu.VMEM(volume.shape, BF16),
+            pltpu.VMEM(out_error.shape, BF16),
+            pltpu.SemaphoreType.DMA((2,)),
+        ],
+        64 * 1024 * 1024,
+    )(volume, out_error)
     received = exchange(send, "filt")
     even, odd = call(
         turn_body, (shape((256, 1152), BF16), shape((512, 1152), BF16)), [VMEM], (452 * mb, 4 * mb)
@@ -206,20 +235,22 @@
     part = call(
         keep_body, shape((128, 3456), BF16), [SMEM, VMEM, VMEM, VMEM, VMEM], (113 * mb, 3 * mb)
     )(core, both, ze, zo, other)
+    own = jnp.stack([grad, right])
+    part, own = lax.optimization_barrier((part, own))
+    upper = shifted_2(own, "slab", -1)
     piece = add_up(exchange(part.reshape(4, 32, 3456), "slab", X_GROUPS))
-
-    own = jnp.stack([grad, right])
-    upper = shifted_2(own, "slab", -1)
+    piece, upper = lax.optimization_barrier((piece, upper))
+
     in_grad = call(
         input_body, shape((2, 2, 128, 256), BF16), [VMEM] * 3, (226 * mb, 3 * mb)
     )(own, upper, taps)
     in_grad = in_grad.transpose(0, 2, 1, 3)
 
-    tile = add_up(exchange(piece.reshape(8, 4, 3456), "filt"))
-    tile = add_up(exchange(to_all(tile, 8), "slab", Z_GROUPS))
-    tiles = exchange(to_all(tile, 8), "slab", XC_GROUPS)
-    tiles = tiles.astype(F32).reshape(32, 3, 3, 3, 128) * (1.0 / 256.0)
-    weight_grad = tiles.transpose(2, 3, 1, 4, 0)
+    tiles = add_up(exchange(piece.reshape(8, 4, 3456), "filt"), (8,))
+    tiles = add_up(exchange(tiles, "slab", Z_GROUPS), (8,))
+    tiles = exchange(tiles, "slab", XC_GROUPS)
+    out = call(last_body, shape((27, 32, 128), F32), [VMEM], (mb, mb))(tiles)
+    weight_grad = out.reshape(3, 3, 3, 32, 128).transpose(0, 1, 2, 4, 3)
     return (in_grad, weight_grad)
 
 

time: 108 us -> 109 us (level)
  blocking collectives: 54.4 us -> 46.7 us
  starting transfers between devices: 26.1 us -> 32.5 us
  Pallas kernels: 4.83 us -> 9.24 us
  local copies, waits for them, and re-layouts: 5.42 us -> 2.52 us
    all_to_all x3, blocking collectives: 54.4 us -> 46.7 us  [exchange(): lax.all_to_all(value, axis, split_axis=0, concat_axis=0, axis_index_group...]
    all_to_all x2, waiting for transfers between devices: 7.66 us -> 13.2 us  [exchange(): lax.all_to_all(value, axis, split_axis=0, concat_axis=0, axis_index_group...]
    all_to_all x2, starting transfers between devices: 13.8 us -> 18 us  [exchange(): lax.all_to_all(value, axis, split_axis=0, concat_axis=0, axis_index_group...]
    pallas_call x4 -> x5, Pallas kernels: 0.62 us -> 4.11 us  [the longest x1 2.36 us: on_device(): call(pack_body, shape((8, 7, 16, 256), BF16), [ANY] * 2, (2 * mb, mb), [p...]
    ppermute x1, waiting for transfers between devices: 2.39 us -> 0.01 us  [on_device(): other = lax.ppermute(part, 'slab', CORE_PAIRS)]
    ppermute x3, waiting for transfers between devices: 6.04 us -> 3.73 us  [shifted_2(): lax.ppermute(value, axis, [(source, source + steps) for source in range(f...]
    ppermute x3, starting transfers between devices: 10.4 us -> 12.7 us  [shifted_2(): lax.ppermute(value, axis, [(source, source + steps) for source in range(f...]
    broadcast_in_dim x2 -> x0, local copies, waits for them, and re-layouts: 1.49 us -> none  [to_all(): return jnp.broadcast_to(value[None], (count,) + value.shape)]
  transfers between devices with their start and end apart: 6 -> 6, of which waited for: 4 -> 3; matrix products, arithmetic and copies ran while one was open for 2% -> 1% of each run, Pallas kernels for 2% -> 2%
where the time goes in v3:
time: 109 us
  blocking collectives  46.7 us (43%)
  starting transfers between devices  32.5 us (30%)
  waiting for transfers between devices  16.9 us (16%)
  Pallas kernels  9.24 us (8%)
  local copies, waits for them, and re-layouts  2.52 us (2%)
    all_to_all x3, blocking collectives, exchange(): lax.all_to_all(value, axis, split_axis=0, concat_axis=0, axis_index_group...  46.7 us
    all_to_all x2, starting transfers between devices, exchange(): lax.all_to_all(value, axis, split_axis=0, concat_axis=0, axis_index_group...  18 us
    all_to_all x2, waiting for transfers between devices, exchange(): lax.all_to_all(value, axis, split_axis=0, concat_axis=0, axis_index_group...  13.2 us
    ppermute x3, starting transfers between devices, shifted_2(): lax.ppermute(value, axis, [(source, source + steps) for source in range(f...  12.7 us
    ppermute x3, waiting for transfers between devices, shifted_2(): lax.ppermute(value, axis, [(source, source + steps) for source in range(f...  3.73 us
    unnamed x5, local copies, waits for them, and re-layouts  2.45 us
    pallas_call x1, Pallas kernels, on_device(): call(pack_body, shape((8, 7, 16, 256), BF16), [ANY] * 2, (2 * mb, mb), [p...  2.36 us
  transfers between devices with their start and end apart: 6, of which 3 were waited for; matrix products, arithmetic and copies ran while one was open for 1% of the time, Pallas kernels for 2%

profile of v3, /device:TPU:1, one launch (start us, length us, event | category | flops | bytes accessed | tf_op | source)
XLA Modules:
  0.0 108.7 jit_solution(2997265549932905355)
XLA Ops:
  0.6 2.4 %shard_map.50 = bf16[8,7,16,256]{3,2,1,0:T(8,128)(2,1)} custom-call(bf16[2,16,16,256]{3,2,1,0:T(8,128)(2,1)} %vol_hbm.1, bf16[1,32,8,128]{3,2,1,0:T(8,128)(2,1)} %err_hbm.1), custom_call_target="tpu_custom_call" | custom-call | flops 2097152 | bytes 1048576 | tf_op jit(solution)/shard_map/pallas_call | solution.py:208
  3.0 20.3 %all_to_all.25.rec_ref = bf16[8,7,16,256]{3,2,1,0:T(8,128)(2,1)S(1)} all-to-all(bf16[8,7,16,256]{3,2,1,0:T(8,128)(2,1)} %shard_map.50), channel_id=1, replica_groups=mesh['slab'=64,'filt'=8] {'filt'}, dimensions={0} | all-to-all | bytes 917504 | tf_op jit(solution)/shard_map/all_to_all | solution.py:191
  23.3 8.3 %collective-permute-start = (bf16[8,3,16,256]{3,2,1,0:T(8,128)(2,1)S(1)}, bf16[8,3,16,256]{3,2,1,0:T(8,128)(2,1)S(1)}, u32[]{:S(2)}, u32[]{:S(2)}) collective-permute-start(bf16[8,3,16,256]{3,2,1,0:T(8,128)(2,1)S(1)} %slice.4), channel_id=1, source_target_pairs={{0,8},{8,16},{16,24},{24,32},{32,40},{40,48},{48,56},{56,64},{64,7... | collective-permute-start | bytes 589832 | tf_op jit(solution)/shard_map/ppermute | solution.py:187
  31.6 1.5 %copy-done = bf16[3,3,3,128,256]{4,3,2,1,0:T(8,128)(2,1)S(1)} copy-done((bf16[3,3,3,128,256]{4,3,2,1,0:T(8,128)(2,1)S(1)}, bf16[3,3,3,128,256]{4,3,2,1,0:T(8,128)(2,1)}, u32[]{:S(2)}) %copy-start) | copy-done | bytes 1769496
  33.1 1.1 shard_map.51
  34.2 0.0 collective-permute-done.rim_ref
  34.2 1.4 %shard_map.52 = (bf16[256,128]{1,0:T(8,128)(2,1)S(1)}, bf16[256,256]{1,0:T(8,128)(2,1)S(1)}, bf16[1152,128]{1,0:T(8,128)(2,1)S(1)}, bf16[1152,128]{1,0:T(8,128)(2,1)S(1)}, bf16[128,3456]{1,0:T(8,128)(2,1)S(1)}) custom-call(s32[1]{0:T(128)} %bitcast.core_ref, bf16[8,7,16,256]{3,2,1,0:T(8,128)(2,1)S(1)} %all_to_all.25.rec_ref, ...), custom_call_target="tpu_custom_call" | custom-call | flops 475004928 | bytes 4194304 | tf_op jit(solution)/shard_map/pallas_call | solution.py:226
  35.7 1.9 %collective-permute-start.1 = (bf16[128,3456]{1,0:T(8,128)(2,1)S(1)}, bf16[128,3456]{1,0:T(8,128)(2,1)S(1)}, u32[]{:S(2)}, u32[]{:S(2)}) collective-permute-start(bf16[128,3456]{1,0:T(8,128)(2,1)S(1)} %get-tuple-element.18), channel_id=1, source_target_pairs={{0,8},{8,0},{16,24},{24,16},{32,40},{40,32},{48,56},{56,48},{64,72... | collective-permute-start | bytes 2654216 | tf_op jit(solution)/shard_map/ppermute | solution.py:233
  37.6 1.3 %collective-permute-start.2 = (bf16[256,128]{1,0:T(8,128)(2,1)S(1)}, bf16[256,128]{1,0:T(8,128)(2,1)S(1)}, u32[]{:S(2)}, u32[]{:S(2)}) collective-permute-start(bf16[256,128]{1,0:T(8,128)(2,1)S(1)} %get-tuple-element.19), channel_id=1, source_target_pairs={{1,0},{2,1},{3,2},{4,3},{5,4},{6,5},{7,6},{9,8},{10,9},{11,10},{12... | collective-permute-start | bytes 196616 | tf_op jit(solution)/shard_map/ppermute | solution.py:187
  38.9 3.7 %collective-permute-done.2 = bf16[256,128]{1,0:T(8,128)(2,1)S(1)} collective-permute-done((bf16[256,128]{1,0:T(8,128)(2,1)S(1)}, bf16[256,128]{1,0:T(8,128)(2,1)S(1)}, u32[]{:S(2)}, u32[]{:S(2)}) %collective-permute-start.2) | collective-permute-done | bytes 65568 | tf_op jit(solution)/shard_map/ppermute | solution.py:187
  42.6 1.5 %shard_map.53 = bf16[128,3456]{1,0:T(8,128)(2,1)} custom-call(s32[1]{0:T(128)} %bitcast.core_ref, bf16[256,256]{1,0:T(8,128)(2,1)S(1)} %get-tuple-element.15.both_ref, bf16[1152,128]{1,0:T(8,128)(2,1)S(1)} %get-tuple-element.16.ze, bf16[1152,128]{1,0:T(8,128)(2,1)S(1)} %get-tuple-element.17.zo, bf16[128,3456]{1,0:T(8,128)(2,1)S(1)} %collective-permute-done.1.other_ref), custom_call_target="tpu_custom_call" | custom-call | flops 118489088 | bytes 3145728 | tf_op jit(solution)/shard_map/pallas_call | solution.py:235
  44.1 10.0 %all-to-all-start.1 = ((bf16[4,32,3456]{2,1,0:T(8,128)(2,1)}), bf16[4,32,3456]{2,1,0:T(8,128)(2,1)S(1)}, u32[]{:S(2)}, u32[]{:S(2)}) async-start(bf16[4,32,3456]{2,1,0:T(8,128)(2,1)} %bitcast.4), calls=%async_computation.1 | async-start | bytes 1769472 | tf_op jit(solution)/shard_map/all_to_all | solution.py:191
  54.1 3.1 %collective-permute-start.3 = (bf16[2,256,128]{2,1,0:T(8,128)(2,1)S(1)}, bf16[2,256,128]{2,1,0:T(8,128)(2,1)S(1)}, u32[]{:S(2)}, u32[]{:S(2)}) collective-permute-start(bf16[2,256,128]{2,1,0:T(8,128)(2,1)S(1)} %pad_maximum_fusion.own_ref), channel_id=1, source_target_pairs={{8,0},{16,8},{24,16},{32,24},{40,32},{48,40},{56,48},{64,56},{72,6... | collective-permute-start | bytes 393224 | tf_op jit(solution)/shard_map/ppermute | solution.py:187
  57.2 9.2 %all-to-all-done.1.in_ref = bf16[4,32,3456]{2,1,0:T(8,128)(2,1)S(1)} async-done(((bf16[4,32,3456]{2,1,0:T(8,128)(2,1)}), bf16[4,32,3456]{2,1,0:T(8,128)(2,1)S(1)}, u32[]{:S(2)}, u32[]{:S(2)}) %all-to-all-start.1) | async-done | bytes 884768 | tf_op jit(solution)/shard_map/all_to_all | solution.py:191
  66.4 0.1 shard_map.54
  66.5 0.1 reshape.22
  66.6 11.8 %all_to_all.26.in_ref = bf16[8,4,3456]{2,1,0:T(4,128)(2,1)S(1)} all-to-all(bf16[8,4,3456]{2,1,0:T(4,128)(2,1)S(1)} %reshape.22), channel_id=1, replica_groups=mesh['slab'=64,'filt'=8] {'filt'}, dimensions={0} | all-to-all | bytes 442368 | tf_op jit(solution)/shard_map/all_to_all | solution.py:191
  78.4 14.6 %all_to_all.27.in_ref = bf16[8,4,3456]{2,1,0:T(4,128)(2,1)S(1)} all-to-all(bf16[8,4,3456]{2,1,0:T(4,128)(2,1)S(1)} %shard_map.56), channel_id=1, replica_groups={{0,16,32,48,64,80,96,112},{8,24,40,56,72,88,104,120},{128,144,160,176,1..., dimensions={0} | all-to-all | bytes 442368 | tf_op jit(solution)/shard_map/all_to_all | solution.py:191
  93.0 0.7 shard_map.57
  93.8 7.9 %all-to-all-start.4 = ((bf16[8,4,3456]{2,1,0:T(4,128)(2,1)}), bf16[8,4,3456]{2,1,0:T(4,128)(2,1)S(1)}, u32[]{:S(2)}, u32[]{:S(2)}) async-start(bf16[8,4,3456]{2,1,0:T(4,128)(2,1)} %shard_map.57), calls=%async_computation.4 | async-start | bytes 442368 | tf_op jit(solution)/shard_map/all_to_all | solution.py:191
  101.7 1.2 %shard_map.55 = bf16[2,2,128,256]{3,2,1,0:T(8,128)(2,1)S(1)} custom-call(bf16[2,256,128]{2,1,0:T(8,128)(2,1)S(1)} %pad_maximum_fusion.own_ref, bf16[2,256,128]{2,1,0:T(8,128)(2,1)S(1)} %collective-permute-done.3.up_ref, bf16[9,3,128,256]{3,2,1,0:T(8,128)(2,1)S(1)} %bitcast.10), custom_call_target="tpu_custom_call" | custom-call | flops 236978176 | bytes 3145728 | tf_op jit(solution)/shard_map/pallas_call | solution.py:244
  102.9 1.0 copy.5
  103.8 4.0 %all-to-all-done.4.in_ref = bf16[8,4,3456]{2,1,0:T(4,128)(2,1)S(1)} async-done(((bf16[8,4,3456]{2,1,0:T(4,128)(2,1)}), bf16[8,4,3456]{2,1,0:T(4,128)(2,1)S(1)}, u32[]{:S(2)}, u32[]{:S(2)}) %all-to-all-start.4) | async-done | bytes 221216 | tf_op jit(solution)/shard_map/all_to_all | solution.py:191
  107.9 0.9 shard_map.58
  (8 shorter events, 0.1 us)
Async XLA Ops:
  23.3 10.9 %collective-permute-start = (bf16[8,3,16,256]{3,2,1,0:T(8,128)(2,1)S(1)}, bf16[8,3,16,256]{3,2,1,0:T(8,128)(2,1)S(1)}, u32[]{:S(2)}, u32[]{:S(2)}) collective-permute-start(bf16[8,3,16,256]{3,2,1,0:T(8,128)(2,1)S(1)} %slice.4), channel_id=1, source_target_pairs={{0,8},{8,16},{16,24},{24,32},{32,40},{40,48},{48,56},{56,64},{64,7... | collective-permute-start | bytes 589832 | tf_op jit(solution)/shard_map/ppermute | solution.py:187
  31.6 1.5 %copy-start = (bf16[3,3,3,128,256]{4,3,2,1,0:T(8,128)(2,1)S(1)}, bf16[3,3,3,128,256]{4,3,2,1,0:T(8,128)(2,1)}, u32[]{:S(2)}) copy-start(bf16[3,3,3,128,256]{4,3,2,1,0:T(8,128)(2,1)} %param.4) | copy-start | bytes 5308420
  35.7 7.0 %collective-permute-start.1 = (bf16[128,3456]{1,0:T(8,128)(2,1)S(1)}, bf16[128,3456]{1,0:T(8,128)(2,1)S(1)}, u32[]{:S(2)}, u32[]{:S(2)}) collective-permute-start(bf16[128,3456]{1,0:T(8,128)(2,1)S(1)} %get-tuple-element.18), channel_id=1, source_target_pairs={{0,8},{8,0},{16,24},{24,16},{32,40},{40,32},{48,56},{56,48},{64,72... | collective-permute-start | bytes 2654216 | tf_op jit(solution)/shard_map/ppermute | solution.py:233
  37.6 5.0 %collective-permute-start.2 = (bf16[256,128]{1,0:T(8,128)(2,1)S(1)}, bf16[256,128]{1,0:T(8,128)(2,1)S(1)}, u32[]{:S(2)}, u32[]{:S(2)}) collective-permute-start(bf16[256,128]{1,0:T(8,128)(2,1)S(1)} %get-tuple-element.19), channel_id=1, source_target_pairs={{1,0},{2,1},{3,2},{4,3},{5,4},{6,5},{7,6},{9,8},{10,9},{11,10},{12... | collective-permute-start | bytes 196616 | tf_op jit(solution)/shard_map/ppermute | solution.py:187
  44.1 22.3 %all-to-all-start.1 = ((bf16[4,32,3456]{2,1,0:T(8,128)(2,1)}), bf16[4,32,3456]{2,1,0:T(8,128)(2,1)S(1)}, u32[]{:S(2)}, u32[]{:S(2)}) async-start(bf16[4,32,3456]{2,1,0:T(8,128)(2,1)} %bitcast.4), calls=%async_computation.1 | async-start | bytes 1769472 | tf_op jit(solution)/shard_map/all_to_all | solution.py:191
  54.1 47.6 %copy-start.1 = (bf16[3,3,3,128,256]{4,3,2,1,0:T(8,128)(2,1)S(1)}, bf16[3,3,3,128,256]{4,3,2,1,0:T(8,128)(2,1)}, u32[]{:S(2)}) copy-start(bf16[3,3,3,128,256]{4,3,2,1,0:T(8,128)(2,1)} %param.4) | copy-start | bytes 5308420
  54.1 12.4 %collective-permute-start.3 = (bf16[2,256,128]{2,1,0:T(8,128)(2,1)S(1)}, bf16[2,256,128]{2,1,0:T(8,128)(2,1)S(1)}, u32[]{:S(2)}, u32[]{:S(2)}) collective-permute-start(bf16[2,256,128]{2,1,0:T(8,128)(2,1)S(1)} %pad_maximum_fusion.own_ref), channel_id=1, source_target_pairs={{8,0},{16,8},{24,16},{32,24},{40,32},{48,40},{56,48},{64,56},{72,6... | collective-permute-start | bytes 393224 | tf_op jit(solution)/shard_map/ppermute | solution.py:187
  93.8 14.1 %all-to-all-start.4 = ((bf16[8,4,3456]{2,1,0:T(4,128)(2,1)}), bf16[8,4,3456]{2,1,0:T(4,128)(2,1)S(1)}, u32[]{:S(2)}, u32[]{:S(2)}) async-start(bf16[8,4,3456]{2,1,0:T(4,128)(2,1)} %shard_map.57), calls=%async_computation.4 | async-start | bytes 442368 | tf_op jit(solution)/shard_map/all_to_all | solution.py:191

commit v4 on v3

--- a/solution.py
+++ b/solution.py
@@ -12,11 +12,24 @@
 SMEM = pl.BlockSpec(memory_space=pltpu.SMEM)
 LIMIT = 48 * 1024 * 1024
 
-NX, NZ, NC = 4, 8, 2
-X_GROUPS = [[(x * NZ + z) * NC + c for x in range(NX)] for z in range(NZ) for c in range(NC)]
-XC_GROUPS = [[(x * NZ + z) * NC + c for x in range(NX) for c in range(NC)] for z in range(NZ)]
-Z_GROUPS = [[(x * NZ + z) * NC + c for z in range(NZ)] for x in range(NX) for c in range(NC)]
-CORE_PAIRS = [(s, s ^ 1) for s in range(NX * NZ * NC)]
+
+def slab_of(px, pz, bx, bz, core):
+    x = 2 * px + (bx ^ px)
+    z = 2 * pz + (bz ^ (pz & 1))
+    return (x * 8 + z) * 2 + core
+
+
+B2, B4 = range(2), range(4)
+SQUARES = [
+    [slab_of(px, pz, bx, bz, c) for bx in B2 for bz in B2] for px in B2 for pz in B4 for c in B2
+]
+ACROSS = [
+    [slab_of(px, pz, bx, bz, c) for px in B2 for pz in B4] for bx in B2 for bz in B2 for c in B2
+]
+CUBES = [
+    [slab_of(px, pz, bx, bz, c) for bx in B2 for bz in B2 for c in B2] for px in B2 for pz in B4
+]
+CORE_PAIRS = [(s, s ^ 1) for s in range(64)]
 
 
 def call(body, out_shape, in_specs, cost, scratch=(), limit=LIMIT):
@@ -215,7 +228,7 @@
             pltpu.VMEM(out_error.shape, BF16),
             pltpu.SemaphoreType.DMA((2,)),
         ],
-        64 * 1024 * 1024,
+        62500000,
     )(volume, out_error)
     received = exchange(send, "filt")
     even, odd = call(
@@ -235,20 +248,19 @@
     part = call(
         keep_body, shape((128, 3456), BF16), [SMEM, VMEM, VMEM, VMEM, VMEM], (113 * mb, 3 * mb)
     )(core, both, ze, zo, other)
+    piece = add_up(exchange(part.reshape(4, 32, 3456), "slab", SQUARES))
+    tiles = add_up(exchange(piece.reshape(8, 4, 3456), "filt"), (8,))
+    tiles, right = lax.optimization_barrier((tiles, right))
     own = jnp.stack([grad, right])
-    part, own = lax.optimization_barrier((part, own))
     upper = shifted_2(own, "slab", -1)
-    piece = add_up(exchange(part.reshape(4, 32, 3456), "slab", X_GROUPS))
-    piece, upper = lax.optimization_barrier((piece, upper))
-
+    tiles = add_up(exchange(tiles, "slab", ACROSS), (8,))
+    tiles, upper = lax.optimization_barrier((tiles, upper))
     in_grad = call(
         input_body, shape((2, 2, 128, 256), BF16), [VMEM] * 3, (226 * mb, 3 * mb)
     )(own, upper, taps)
     in_grad = in_grad.transpose(0, 2, 1, 3)
 
-    tiles = add_up(exchange(piece.reshape(8, 4, 3456), "filt"), (8,))
-    tiles = add_up(exchange(tiles, "slab", Z_GROUPS), (8,))
-    tiles = exchange(tiles, "slab", XC_GROUPS)
+    tiles = exchange(tiles, "slab", CUBES)
     out = call(last_body, shape((27, 32, 128), F32), [VMEM], (mb, mb))(tiles)
     weight_grad = out.reshape(3, 3, 3, 32, 128).transpose(0, 1, 2, 4, 3)
     return (in_grad, weight_grad)

time: 109 us -> 108 us (level)
  blocking collectives: 46.7 us -> 38.9 us
  starting transfers between devices: 32.5 us -> 37.9 us
  waiting for transfers between devices: 16.9 us -> 18.8 us
    all_to_all x3 -> x2, blocking collectives: 46.7 us -> 38.9 us  [exchange(): lax.all_to_all(value, axis, split_axis=0, concat_axis=0, axis_index_group...]
    all_to_all x2 -> x3, starting transfers between devices: 18 us -> 21.1 us  [exchange(): lax.all_to_all(value, axis, split_axis=0, concat_axis=0, axis_index_group...]
    ppermute x1, waiting for transfers between devices: 0.01 us -> 2.39 us  [on_device(): other = lax.ppermute(part, 'slab', CORE_PAIRS)]
    ppermute x3, waiting for transfers between devices: 3.73 us -> 1.49 us  [shifted_2(): lax.ppermute(value, axis, [(source, source + steps) for source in range(f...]
    ppermute x3, starting transfers between devices: 12.7 us -> 14.9 us  [shifted_2(): lax.ppermute(value, axis, [(source, source + steps) for source in range(f...]
    all_to_all x2 -> x3, waiting for transfers between devices: 13.2 us -> 14.9 us  [exchange(): lax.all_to_all(value, axis, split_axis=0, concat_axis=0, axis_index_group...]
    unnamed x5 -> x3, local copies, waits for them, and re-layouts: 2.45 us -> 0.98 us
  transfers between devices with their start and end apart: 6 -> 7, of which waited for: 3 -> 5; matrix products, arithmetic and copies ran while one was open for 1% -> 1% of each run, Pallas kernels for 2% -> 3%
where the time goes in v4:
time: 108 us; the launch traced here: 107 us
  blocking collectives  38.9 us (36%)
  starting transfers between devices  37.9 us (35%)
  waiting for transfers between devices  18.8 us (17%)
  Pallas kernels  9.14 us (8%)
  local copies, waits for them, and re-layouts  1.74 us (2%)
    all_to_all x2, blocking collectives, exchange(): lax.all_to_all(value, axis, split_axis=0, concat_axis=0, axis_index_group...  38.9 us
    all_to_all x3, starting transfers between devices, exchange(): lax.all_to_all(value, axis, split_axis=0, concat_axis=0, axis_index_group...  21.1 us
    all_to_all x3, waiting for transfers between devices, exchange(): lax.all_to_all(value, axis, split_axis=0, concat_axis=0, axis_index_group...  14.9 us
    ppermute x3, starting transfers between devices, shifted_2(): lax.ppermute(value, axis, [(source, source + steps) for source in range(f...  14.9 us
    pallas_call x1, Pallas kernels, on_device(): call(pack_body, shape((8, 7, 16, 256), BF16), [ANY] * 2, (2 * mb, mb), [p...  2.5 us
    ppermute x1, waiting for transfers between devices, on_device(): other = lax.ppermute(part, 'slab', CORE_PAIRS)  2.39 us
  transfers between devices with their start and end apart: 7, of which 5 were waited for; matrix products, arithmetic and copies ran while one was open for 1% of the time, Pallas kernels for 3%

profile of v4, /device:TPU:1, one launch (start us, length us, event | category | flops | bytes accessed | tf_op | source)
XLA Modules:
  0.0 107.2 jit_solution(18043540142296633541)
XLA Ops:
  0.6 2.5 %shard_map.50 = bf16[8,7,16,256]{3,2,1,0:T(8,128)(2,1)} custom-call(bf16[2,16,16,256]{3,2,1,0:T(8,128)(2,1)} %vol_hbm.1, bf16[1,32,8,128]{3,2,1,0:T(8,128)(2,1)} %err_hbm.1), custom_call_target="tpu_custom_call" | custom-call | flops 2097152 | bytes 1048576 | tf_op jit(solution)/shard_map/pallas_call | solution.py:221
  3.1 20.3 %all_to_all.25.rec_ref = bf16[8,7,16,256]{3,2,1,0:T(8,128)(2,1)S(1)} all-to-all(bf16[8,7,16,256]{3,2,1,0:T(8,128)(2,1)} %shard_map.50), channel_id=1, replica_groups=mesh['slab'=64,'filt'=8] {'filt'}, dimensions={0} | all-to-all | bytes 917504 | tf_op jit(solution)/shard_map/all_to_all | solution.py:204
  23.5 8.3 %collective-permute-start = (bf16[8,3,16,256]{3,2,1,0:T(8,128)(2,1)S(1)}, bf16[8,3,16,256]{3,2,1,0:T(8,128)(2,1)S(1)}, u32[]{:S(2)}, u32[]{:S(2)}) collective-permute-start(bf16[8,3,16,256]{3,2,1,0:T(8,128)(2,1)S(1)} %slice.4), channel_id=1, source_target_pairs={{0,8},{8,16},{16,24},{24,32},{32,40},{40,48},{48,56},{56,64},{64,7... | collective-permute-start | bytes 589832 | tf_op jit(solution)/shard_map/ppermute | solution.py:200
  31.8 1.1 %shard_map.51 = (bf16[256,1152]{1,0:T(8,128)(2,1)S(1)}, bf16[512,1152]{1,0:T(8,128)(2,1)S(1)}) custom-call(bf16[9,3,128,256]{3,2,1,0:T(8,128)(2,1)S(1)} %bitcast.9), custom_call_target="tpu_custom_call" | custom-call | flops 473956352 | bytes 4194304 | tf_op jit(solution)/shard_map/pallas_call | solution.py:234
  32.9 1.5 %collective-permute-done.rim_ref = bf16[8,3,16,256]{3,2,1,0:T(8,128)(2,1)S(1)} collective-permute-done((bf16[8,3,16,256]{3,2,1,0:T(8,128)(2,1)S(1)}, bf16[8,3,16,256]{3,2,1,0:T(8,128)(2,1)S(1)}, u32[]{:S(2)}, u32[]{:S(2)}) %collective-permute-start) | collective-permute-done | bytes 196640 | tf_op jit(solution)/shard_map/ppermute | solution.py:200
  34.4 1.4 %shard_map.52 = (bf16[256,128]{1,0:T(8,128)(2,1)S(1)}, bf16[256,256]{1,0:T(8,128)(2,1)S(1)}, bf16[1152,128]{1,0:T(8,128)(2,1)S(1)}, bf16[1152,128]{1,0:T(8,128)(2,1)S(1)}, bf16[128,3456]{1,0:T(8,128)(2,1)S(1)}) custom-call(s32[1]{0:T(128)} %bitcast.core_ref, bf16[8,7,16,256]{3,2,1,0:T(8,128)(2,1)S(1)} %all_to_all.25.rec_ref, ...), custom_call_target="tpu_custom_call" | custom-call | flops 475004928 | bytes 4194304 | tf_op jit(solution)/shard_map/pallas_call | solution.py:239
  35.8 1.9 %collective-permute-start.1 = (bf16[128,3456]{1,0:T(8,128)(2,1)S(1)}, bf16[128,3456]{1,0:T(8,128)(2,1)S(1)}, u32[]{:S(2)}, u32[]{:S(2)}) collective-permute-start(bf16[128,3456]{1,0:T(8,128)(2,1)S(1)} %get-tuple-element.19), channel_id=1, source_target_pairs={{0,8},{8,0},{16,24},{24,16},{32,40},{40,32},{48,56},{56,48},{64,72... | collective-permute-start | bytes 2654216 | tf_op jit(solution)/shard_map/ppermute | solution.py:246
  37.7 2.4 %collective-permute-done.1.other_ref = bf16[128,3456]{1,0:T(8,128)(2,1)S(1)} collective-permute-done((bf16[128,3456]{1,0:T(8,128)(2,1)S(1)}, bf16[128,3456]{1,0:T(8,128)(2,1)S(1)}, u32[]{:S(2)}, u32[]{:S(2)}) %collective-permute-start.1) | collective-permute-done | bytes 884768 | tf_op jit(solution)/shard_map/ppermute | solution.py:246
  40.1 0.5 shard_map.53
  40.7 18.6 %all_to_all.26.in_ref = bf16[4,32,3456]{2,1,0:T(8,128)(2,1)S(1)} all-to-all(bf16[4,32,3456]{2,1,0:T(8,128)(2,1)S(1)} %bitcast.11), channel_id=1, replica_groups={{0,16,128,144},{8,24,136,152},{48,32,176,160},{56,40,184,168},{64,80,19..., dimensions={0} | all-to-all | bytes 1769472 | tf_op jit(solution)/shard_map/all_to_all | solution.py:204
  59.4 0.7 reshape.22
  60.1 3.4 %all-to-all-start.2 = ((bf16[8,4,3456]{2,1,0:T(4,128)(2,1)}), bf16[8,4,3456]{2,1,0:T(4,128)(2,1)S(1)}, u32[]{:S(2)}, u32[]{:S(2)}) async-start(bf16[8,4,3456]{2,1,0:T(4,128)(2,1)} %reshape.22), calls=%async_computation.2 | async-start | bytes 442368 | tf_op jit(solution)/shard_map/all_to_all | solution.py:204
  63.5 1.3 %collective-permute-start.2 = (bf16[256,128]{1,0:T(8,128)(2,1)S(1)}, bf16[256,128]{1,0:T(8,128)(2,1)S(1)}, u32[]{:S(2)}, u32[]{:S(2)}) collective-permute-start(bf16[256,128]{1,0:T(8,128)(2,1)S(1)} %get-tuple-element.15), channel_id=1, source_target_pairs={{1,0},{2,1},{3,2},{4,3},{5,4},{6,5},{7,6},{9,8},{10,9},{11,10},{12... | collective-permute-start | bytes 196616 | tf_op jit(solution)/shard_map/ppermute | solution.py:200
  64.8 7.6 %all-to-all-done.2.in_ref = bf16[8,4,3456]{2,1,0:T(4,128)(2,1)S(1)} async-done(((bf16[8,4,3456]{2,1,0:T(4,128)(2,1)}), bf16[8,4,3456]{2,1,0:T(4,128)(2,1)S(1)}, u32[]{:S(2)}, u32[]{:S(2)}) %all-to-all-start.2) | async-done | bytes 221216 | tf_op jit(solution)/shard_map/all_to_all | solution.py:204
  72.4 0.7 shard_map.55
  73.2 9.1 %all-to-all-start.3 = ((bf16[8,4,3456]{2,1,0:T(4,128)(2,1)}), bf16[8,4,3456]{2,1,0:T(4,128)(2,1)S(1)}, u32[]{:S(2)}, u32[]{:S(2)}) async-start(bf16[8,4,3456]{2,1,0:T(4,128)(2,1)} %shard_map.55), calls=%async_computation.3 | async-start | bytes 442368 | tf_op jit(solution)/shard_map/all_to_all | solution.py:204
  82.3 5.3 %collective-permute-start.3 = (bf16[2,256,128]{2,1,0:T(8,128)(2,1)S(1)}, bf16[2,256,128]{2,1,0:T(8,128)(2,1)S(1)}, u32[]{:S(2)}, u32[]{:S(2)}) collective-permute-start(bf16[2,256,128]{2,1,0:T(8,128)(2,1)S(1)} %pad_maximum_fusion.own_ref), channel_id=1, source_target_pairs={{8,0},{16,8},{24,16},{32,24},{40,32},{48,40},{56,48},{64,56},{72,6... | collective-permute-start | bytes 393224 | tf_op jit(solution)/shard_map/ppermute | solution.py:200
  87.6 4.0 %all-to-all-done.3.in_ref = bf16[8,4,3456]{2,1,0:T(4,128)(2,1)S(1)} async-done(((bf16[8,4,3456]{2,1,0:T(4,128)(2,1)}), bf16[8,4,3456]{2,1,0:T(4,128)(2,1)S(1)}, u32[]{:S(2)}, u32[]{:S(2)}) %all-to-all-start.3) | async-done | bytes 221216 | tf_op jit(solution)/shard_map/all_to_all | solution.py:204
  91.6 0.7 shard_map.56
  92.4 8.6 %all-to-all-start.4 = ((bf16[8,4,3456]{2,1,0:T(4,128)(2,1)}), bf16[8,4,3456]{2,1,0:T(4,128)(2,1)S(1)}, u32[]{:S(2)}, u32[]{:S(2)}) async-start(bf16[8,4,3456]{2,1,0:T(4,128)(2,1)} %shard_map.56), calls=%async_computation.4 | async-start | bytes 442368 | tf_op jit(solution)/shard_map/all_to_all | solution.py:204
  100.9 1.2 %shard_map.57 = bf16[2,2,128,256]{3,2,1,0:T(8,128)(2,1)S(1)} custom-call(bf16[2,256,128]{2,1,0:T(8,128)(2,1)S(1)} %pad_maximum_fusion.own_ref, bf16[2,256,128]{2,1,0:T(8,128)(2,1)S(1)} %collective-permute-done.3.up_ref, bf16[9,3,128,256]{3,2,1,0:T(8,128)(2,1)S(1)} %bitcast.10), custom_call_target="tpu_custom_call" | custom-call | flops 236978176 | bytes 3145728 | tf_op jit(solution)/shard_map/pallas_call | solution.py:258
  102.1 1.0 copy.5
  103.1 3.3 %all-to-all-done.4.in_ref = bf16[8,4,3456]{2,1,0:T(4,128)(2,1)S(1)} async-done(((bf16[8,4,3456]{2,1,0:T(4,128)(2,1)}), bf16[8,4,3456]{2,1,0:T(4,128)(2,1)S(1)}, u32[]{:S(2)}, u32[]{:S(2)}) %all-to-all-start.4) | async-done | bytes 221216 | tf_op jit(solution)/shard_map/all_to_all | solution.py:204
  106.4 0.9 shard_map.58
  (7 shorter events, 0.1 us)
Async XLA Ops:
  0.6 31.1 %copy-start = (bf16[3,3,3,128,256]{4,3,2,1,0:T(8,128)(2,1)S(1)}, bf16[3,3,3,128,256]{4,3,2,1,0:T(8,128)(2,1)}, u32[]{:S(2)}) copy-start(bf16[3,3,3,128,256]{4,3,2,1,0:T(8,128)(2,1)} %param.4) | copy-start | bytes 5308420
  23.5 10.9 %collective-permute-start = (bf16[8,3,16,256]{3,2,1,0:T(8,128)(2,1)S(1)}, bf16[8,3,16,256]{3,2,1,0:T(8,128)(2,1)S(1)}, u32[]{:S(2)}, u32[]{:S(2)}) collective-permute-start(bf16[8,3,16,256]{3,2,1,0:T(8,128)(2,1)S(1)} %slice.4), channel_id=1, source_target_pairs={{0,8},{8,16},{16,24},{24,32},{32,40},{40,48},{48,56},{56,64},{64,7... | collective-permute-start | bytes 589832 | tf_op jit(solution)/shard_map/ppermute | solution.py:200
  35.8 4.3 %collective-permute-start.1 = (bf16[128,3456]{1,0:T(8,128)(2,1)S(1)}, bf16[128,3456]{1,0:T(8,128)(2,1)S(1)}, u32[]{:S(2)}, u32[]{:S(2)}) collective-permute-start(bf16[128,3456]{1,0:T(8,128)(2,1)S(1)} %get-tuple-element.19), channel_id=1, source_target_pairs={{0,8},{8,0},{16,24},{24,16},{32,40},{40,32},{48,56},{56,48},{64,72... | collective-permute-start | bytes 2654216 | tf_op jit(solution)/shard_map/ppermute | solution.py:246
  60.1 12.3 %all-to-all-start.2 = ((bf16[8,4,3456]{2,1,0:T(4,128)(2,1)}), bf16[8,4,3456]{2,1,0:T(4,128)(2,1)S(1)}, u32[]{:S(2)}, u32[]{:S(2)}) async-start(bf16[8,4,3456]{2,1,0:T(4,128)(2,1)} %reshape.22), calls=%async_computation.2 | async-start | bytes 442368 | tf_op jit(solution)/shard_map/all_to_all | solution.py:204
  63.5 9.6 %collective-permute-start.2 = (bf16[256,128]{1,0:T(8,128)(2,1)S(1)}, bf16[256,128]{1,0:T(8,128)(2,1)S(1)}, u32[]{:S(2)}, u32[]{:S(2)}) collective-permute-start(bf16[256,128]{1,0:T(8,128)(2,1)S(1)} %get-tuple-element.15), channel_id=1, source_target_pairs={{1,0},{2,1},{3,2},{4,3},{5,4},{6,5},{7,6},{9,8},{10,9},{11,10},{12... | collective-permute-start | bytes 196616 | tf_op jit(solution)/shard_map/ppermute | solution.py:200
  73.2 18.5 %all-to-all-start.3 = ((bf16[8,4,3456]{2,1,0:T(4,128)(2,1)}), bf16[8,4,3456]{2,1,0:T(4,128)(2,1)S(1)}, u32[]{:S(2)}, u32[]{:S(2)}) async-start(bf16[8,4,3456]{2,1,0:T(4,128)(2,1)} %shard_map.55), calls=%async_computation.3 | async-start | bytes 442368 | tf_op jit(solution)/shard_map/all_to_all | solution.py:204
  82.3 10.0 %collective-permute-start.3 = (bf16[2,256,128]{2,1,0:T(8,128)(2,1)S(1)}, bf16[2,256,128]{2,1,0:T(8,128)(2,1)S(1)}, u32[]{:S(2)}, u32[]{:S(2)}) collective-permute-start(bf16[2,256,128]{2,1,0:T(8,128)(2,1)S(1)} %pad_maximum_fusion.own_ref), channel_id=1, source_target_pairs={{8,0},{16,8},{24,16},{32,24},{40,32},{48,40},{56,48},{64,56},{72,6... | collective-permute-start | bytes 393224 | tf_op jit(solution)/shard_map/ppermute | solution.py:200
  92.4 14.0 %all-to-all-start.4 = ((bf16[8,4,3456]{2,1,0:T(4,128)(2,1)}), bf16[8,4,3456]{2,1,0:T(4,128)(2,1)S(1)}, u32[]{:S(2)}, u32[]{:S(2)}) async-start(bf16[8,4,3456]{2,1,0:T(4,128)(2,1)} %shard_map.56), calls=%async_computation.4 | async-start | bytes 442368 | tf_op jit(solution)/shard_map/all_to_all | solution.py:204

commit v5 on v4

--- a/solution.py
+++ b/solution.py
@@ -12,23 +12,14 @@
 SMEM = pl.BlockSpec(memory_space=pltpu.SMEM)
 LIMIT = 48 * 1024 * 1024
 
-
-def slab_of(px, pz, bx, bz, core):
-    x = 2 * px + (bx ^ px)
-    z = 2 * pz + (bz ^ (pz & 1))
+def slab_of(x, z, core):
     return (x * 8 + z) * 2 + core
 
 
-B2, B4 = range(2), range(4)
-SQUARES = [
-    [slab_of(px, pz, bx, bz, c) for bx in B2 for bz in B2] for px in B2 for pz in B4 for c in B2
-]
-ACROSS = [
-    [slab_of(px, pz, bx, bz, c) for px in B2 for pz in B4] for bx in B2 for bz in B2 for c in B2
-]
-CUBES = [
-    [slab_of(px, pz, bx, bz, c) for bx in B2 for bz in B2 for c in B2] for px in B2 for pz in B4
-]
+XS, ZS, CS = range(4), range(8), range(2)
+X_RINGS = [[slab_of(x, z, c) for x in XS] for z in ZS for c in CS]
+Z_RINGS = [[slab_of(x, z, c) for z in ZS] for x in XS for c in CS]
+XC_RINGS = [[slab_of(x, z, c) for x in XS for c in CS] for z in ZS]
 CORE_PAIRS = [(s, s ^ 1) for s in range(64)]
 
 
@@ -157,11 +148,9 @@
     for n in range(1, in_ref.shape[0]):
         total = total + in_ref[n].astype(F32)
     total = total.astype(BF16)
-    if len(out_ref.shape) == len(total.shape):
-        out_ref[...] = total
-    else:
-        for n in range(out_ref.shape[0]):
-            out_ref[n] = total
+    rows = out_ref.shape[1]
+    for n in range(out_ref.shape[0]):
+        out_ref[n] = total if total.shape[0] == rows else total[n * rows : n * rows + rows]
 
 
 def last_body(in_ref, out_ref):
@@ -206,9 +195,9 @@
     )
 
 
-def add_up(value, copies=()):
+def add_up(value):
     size = value.size * 2
-    out_shape = jax.ShapeDtypeStruct(copies + value.shape[1:], BF16)
+    out_shape = jax.ShapeDtypeStruct((8, 4, 3456), BF16)
     return call(sum_body, out_shape, [VMEM], (size, size))(value)
 
 
@@ -248,19 +237,19 @@
     part = call(
         keep_body, shape((128, 3456), BF16), [SMEM, VMEM, VMEM, VMEM, VMEM], (113 * mb, 3 * mb)
     )(core, both, ze, zo, other)
-    piece = add_up(exchange(part.reshape(4, 32, 3456), "slab", SQUARES))
-    tiles = add_up(exchange(piece.reshape(8, 4, 3456), "filt"), (8,))
+    tiles = add_up(exchange(part.reshape(4, 32, 3456), "slab", X_RINGS))
+    tiles = add_up(exchange(tiles, "filt"))
     tiles, right = lax.optimization_barrier((tiles, right))
     own = jnp.stack([grad, right])
     upper = shifted_2(own, "slab", -1)
-    tiles = add_up(exchange(tiles, "slab", ACROSS), (8,))
+    tiles = add_up(exchange(tiles, "slab", Z_RINGS))
     tiles, upper = lax.optimization_barrier((tiles, upper))
     in_grad = call(
         input_body, shape((2, 2, 128, 256), BF16), [VMEM] * 3, (226 * mb, 3 * mb)
     )(own, upper, taps)
     in_grad = in_grad.transpose(0, 2, 1, 3)
 
-    tiles = exchange(tiles, "slab", CUBES)
+    tiles = exchange(tiles, "slab", XC_RINGS)
     out = call(last_body, shape((27, 32, 128), F32), [VMEM], (mb, mb))(tiles)
     weight_grad = out.reshape(3, 3, 3, 32, 128).transpose(0, 1, 2, 4, 3)
     return (in_grad, weight_grad)

time: 108 us -> 107 us (level)
  starting transfers between devices: 37.9 us -> 33.5 us
  blocking collectives: 38.9 us -> 41.7 us
    all_to_all x3, starting transfers between devices: 21.1 us -> 16.6 us  [exchange(): lax.all_to_all(value, axis, split_axis=0, concat_axis=0, axis_index_group...]
    all_to_all x2, blocking collectives: 38.9 us -> 41.7 us  [exchange(): lax.all_to_all(value, axis, split_axis=0, concat_axis=0, axis_index_group...]
  transfers between devices with their start and end apart: 7 -> 7, of which waited for: 5 -> 6; matrix products, arithmetic and copies ran while one was open for 1% -> 1% of each run, Pallas kernels for 3% -> 3%
where the time goes in v5:
time: 107 us
  blocking collectives  41.7 us (39%)
  starting transfers between devices  33.5 us (31%)
  waiting for transfers between devices  19.8 us (19%)
  Pallas kernels  9.84 us (9%)
    all_to_all x2, blocking collectives, exchange(): lax.all_to_all(value, axis, split_axis=0, concat_axis=0, axis_index_group...  41.7 us
    all_to_all x3, starting transfers between devices, exchange(): lax.all_to_all(value, axis, split_axis=0, concat_axis=0, axis_index_group...  16.6 us
    ppermute x3, starting transfers between devices, shifted_2(): lax.ppermute(value, axis, [(source, source + steps) for source in range(f...  15 us
    all_to_all x3, waiting for transfers between devices, exchange(): lax.all_to_all(value, axis, split_axis=0, concat_axis=0, axis_index_group...  14.9 us
    pallas_call x1, Pallas kernels, on_device(): call(pack_body, shape((8, 7, 16, 256), BF16), [ANY] * 2, (2 * mb, mb), [p...  2.5 us
    ppermute x3, waiting for transfers between devices, shifted_2(): lax.ppermute(value, axis, [(source, source + steps) for source in range(f...  2.46 us
    ppermute x1, waiting for transfers between devices, on_device(): other = lax.ppermute(part, 'slab', CORE_PAIRS)  2.39 us
    pallas_call x3, Pallas kernels, add_up(): return call(sum_body, out_shape, [VMEM], (size, size))(value)  2.27 us
  transfers between devices with their start and end apart: 7, of which 6 were waited for; matrix products, arithmetic and copies ran while one was open for 1% of the time, Pallas kernels for 3%

profile of v5, /device:TPU:1, one launch (start us, length us, event | category | flops | bytes accessed | tf_op | source)
XLA Modules:
  0.0 106.6 jit_solution(17414047217294358380)
XLA Ops:
  0.6 2.5 %shard_map.50 = bf16[8,7,16,256]{3,2,1,0:T(8,128)(2,1)} custom-call(bf16[2,16,16,256]{3,2,1,0:T(8,128)(2,1)} %vol_hbm.1, bf16[1,32,8,128]{3,2,1,0:T(8,128)(2,1)} %err_hbm.1), custom_call_target="tpu_custom_call" | custom-call | flops 2097152 | bytes 1048576 | tf_op jit(solution)/shard_map/pallas_call | solution.py:210
  3.1 20.3 %all_to_all.25.rec_ref = bf16[8,7,16,256]{3,2,1,0:T(8,128)(2,1)S(1)} all-to-all(bf16[8,7,16,256]{3,2,1,0:T(8,128)(2,1)} %shard_map.50), channel_id=1, replica_groups=mesh['slab'=64,'filt'=8] {'filt'}, dimensions={0} | all-to-all | bytes 917504 | tf_op jit(solution)/shard_map/all_to_all | solution.py:193
  23.5 8.3 %collective-permute-start = (bf16[8,3,16,256]{3,2,1,0:T(8,128)(2,1)S(1)}, bf16[8,3,16,256]{3,2,1,0:T(8,128)(2,1)S(1)}, u32[]{:S(2)}, u32[]{:S(2)}) collective-permute-start(bf16[8,3,16,256]{3,2,1,0:T(8,128)(2,1)S(1)} %slice.4), channel_id=1, source_target_pairs={{0,8},{8,16},{16,24},{24,32},{32,40},{40,48},{48,56},{56,64},{64,7... | collective-permute-start | bytes 589832 | tf_op jit(solution)/shard_map/ppermute | solution.py:189
  31.8 1.1 %shard_map.51 = (bf16[256,1152]{1,0:T(8,128)(2,1)S(1)}, bf16[512,1152]{1,0:T(8,128)(2,1)S(1)}) custom-call(bf16[9,3,128,256]{3,2,1,0:T(8,128)(2,1)S(1)} %bitcast.9), custom_call_target="tpu_custom_call" | custom-call | flops 473956352 | bytes 4194304 | tf_op jit(solution)/shard_map/pallas_call | solution.py:223
  32.9 1.5 %collective-permute-done.rim_ref = bf16[8,3,16,256]{3,2,1,0:T(8,128)(2,1)S(1)} collective-permute-done((bf16[8,3,16,256]{3,2,1,0:T(8,128)(2,1)S(1)}, bf16[8,3,16,256]{3,2,1,0:T(8,128)(2,1)S(1)}, u32[]{:S(2)}, u32[]{:S(2)}) %collective-permute-start) | collective-permute-done | bytes 196640 | tf_op jit(solution)/shard_map/ppermute | solution.py:189
  34.4 1.4 %shard_map.52 = (bf16[256,128]{1,0:T(8,128)(2,1)S(1)}, bf16[256,256]{1,0:T(8,128)(2,1)S(1)}, bf16[1152,128]{1,0:T(8,128)(2,1)S(1)}, bf16[1152,128]{1,0:T(8,128)(2,1)S(1)}, bf16[128,3456]{1,0:T(8,128)(2,1)S(1)}) custom-call(s32[1]{0:T(128)} %bitcast.core_ref, bf16[8,7,16,256]{3,2,1,0:T(8,128)(2,1)S(1)} %all_to_all.25.rec_ref, ...), custom_call_target="tpu_custom_call" | custom-call | flops 475004928 | bytes 4194304 | tf_op jit(solution)/shard_map/pallas_call | solution.py:228
  35.8 1.9 %collective-permute-start.1 = (bf16[128,3456]{1,0:T(8,128)(2,1)S(1)}, bf16[128,3456]{1,0:T(8,128)(2,1)S(1)}, u32[]{:S(2)}, u32[]{:S(2)}) collective-permute-start(bf16[128,3456]{1,0:T(8,128)(2,1)S(1)} %get-tuple-element.19), channel_id=1, source_target_pairs={{0,8},{8,0},{16,24},{24,16},{32,40},{40,32},{48,56},{56,48},{64,72... | collective-permute-start | bytes 2654216 | tf_op jit(solution)/shard_map/ppermute | solution.py:235
  37.7 2.4 %collective-permute-done.1.other_ref = bf16[128,3456]{1,0:T(8,128)(2,1)S(1)} collective-permute-done((bf16[128,3456]{1,0:T(8,128)(2,1)S(1)}, bf16[128,3456]{1,0:T(8,128)(2,1)S(1)}, u32[]{:S(2)}, u32[]{:S(2)}) %collective-permute-start.1) | collective-permute-done | bytes 884768 | tf_op jit(solution)/shard_map/ppermute | solution.py:235
  40.7 21.4 %all_to_all.26.in_ref = bf16[4,32,3456]{2,1,0:T(8,128)(2,1)S(1)} all-to-all(bf16[4,32,3456]{2,1,0:T(8,128)(2,1)S(1)} %bitcast.11), channel_id=1, replica_groups={{0,128,256,384},{8,136,264,392},{16,144,272,400},{24,152,280,408},{32,1..., dimensions={0} | all-to-all | bytes 1769472 | tf_op jit(solution)/shard_map/all_to_all | solution.py:193
  62.1 0.8 shard_map.54
  62.9 3.4 %all-to-all-start.2 = ((bf16[8,4,3456]{2,1,0:T(4,128)(2,1)}), bf16[8,4,3456]{2,1,0:T(4,128)(2,1)S(1)}, u32[]{:S(2)}, u32[]{:S(2)}) async-start(bf16[8,4,3456]{2,1,0:T(4,128)(2,1)} %shard_map.54), calls=%async_computation.2 | async-start | bytes 442368 | tf_op jit(solution)/shard_map/all_to_all | solution.py:193
  66.3 1.3 %collective-permute-start.2 = (bf16[256,128]{1,0:T(8,128)(2,1)S(1)}, bf16[256,128]{1,0:T(8,128)(2,1)S(1)}, u32[]{:S(2)}, u32[]{:S(2)}) collective-permute-start(bf16[256,128]{1,0:T(8,128)(2,1)S(1)} %get-tuple-element.15), channel_id=1, source_target_pairs={{1,0},{2,1},{3,2},{4,3},{5,4},{6,5},{7,6},{9,8},{10,9},{11,10},{12... | collective-permute-start | bytes 196616 | tf_op jit(solution)/shard_map/ppermute | solution.py:189
  67.6 7.4 %all-to-all-done.2.in_ref = bf16[8,4,3456]{2,1,0:T(4,128)(2,1)S(1)} async-done(((bf16[8,4,3456]{2,1,0:T(4,128)(2,1)}), bf16[8,4,3456]{2,1,0:T(4,128)(2,1)S(1)}, u32[]{:S(2)}, u32[]{:S(2)}) %all-to-all-start.2) | async-done | bytes 221216 | tf_op jit(solution)/shard_map/all_to_all | solution.py:193
  75.0 0.7 shard_map.55
  75.7 6.3 %all-to-all-start.3 = ((bf16[8,4,3456]{2,1,0:T(4,128)(2,1)}), bf16[8,4,3456]{2,1,0:T(4,128)(2,1)S(1)}, u32[]{:S(2)}, u32[]{:S(2)}) async-start(bf16[8,4,3456]{2,1,0:T(4,128)(2,1)} %shard_map.55), calls=%async_computation.3 | async-start | bytes 442368 | tf_op jit(solution)/shard_map/all_to_all | solution.py:193
  82.1 5.4 %collective-permute-start.3 = (bf16[2,256,128]{2,1,0:T(8,128)(2,1)S(1)}, bf16[2,256,128]{2,1,0:T(8,128)(2,1)S(1)}, u32[]{:S(2)}, u32[]{:S(2)}) collective-permute-start(bf16[2,256,128]{2,1,0:T(8,128)(2,1)S(1)} %pad_maximum_fusion.own_ref), channel_id=1, source_target_pairs={{8,0},{16,8},{24,16},{32,24},{40,32},{48,40},{56,48},{64,56},{72,6... | collective-permute-start | bytes 393224 | tf_op jit(solution)/shard_map/ppermute | solution.py:189
  87.5 3.5 %all-to-all-done.3.in_ref = bf16[8,4,3456]{2,1,0:T(4,128)(2,1)S(1)} async-done(((bf16[8,4,3456]{2,1,0:T(4,128)(2,1)}), bf16[8,4,3456]{2,1,0:T(4,128)(2,1)S(1)}, u32[]{:S(2)}, u32[]{:S(2)}) %all-to-all-start.3) | async-done | bytes 221216 | tf_op jit(solution)/shard_map/all_to_all | solution.py:193
  91.0 0.7 shard_map.56
  91.7 1.0 collective-permute-done.3.up_ref
  92.7 6.9 %all-to-all-start.4 = ((bf16[8,4,3456]{2,1,0:T(4,128)(2,1)}), bf16[8,4,3456]{2,1,0:T(4,128)(2,1)S(1)}, u32[]{:S(2)}, u32[]{:S(2)}) async-start(bf16[8,4,3456]{2,1,0:T(4,128)(2,1)} %shard_map.56), calls=%async_computation.4 | async-start | bytes 442368 | tf_op jit(solution)/shard_map/all_to_all | solution.py:193
  99.6 1.2 %shard_map.57 = bf16[2,2,128,256]{3,2,1,0:T(8,128)(2,1)S(1)} custom-call(bf16[2,256,128]{2,1,0:T(8,128)(2,1)S(1)} %pad_maximum_fusion.own_ref, bf16[2,256,128]{2,1,0:T(8,128)(2,1)S(1)} %collective-permute-done.3.up_ref, bf16[9,3,128,256]{3,2,1,0:T(8,128)(2,1)S(1)} %bitcast.10), custom_call_target="tpu_custom_call" | custom-call | flops 236978176 | bytes 3145728 | tf_op jit(solution)/shard_map/pallas_call | solution.py:247
  100.8 1.0 copy.5
  101.8 4.0 %all-to-all-done.4.in_ref = bf16[8,4,3456]{2,1,0:T(4,128)(2,1)S(1)} async-done(((bf16[8,4,3456]{2,1,0:T(4,128)(2,1)}), bf16[8,4,3456]{2,1,0:T(4,128)(2,1)S(1)}, u32[]{:S(2)}, u32[]{:S(2)}) %all-to-all-start.4) | async-done | bytes 221216 | tf_op jit(solution)/shard_map/all_to_all | solution.py:193
  105.8 0.9 shard_map.58
  (6 shorter events, 0.6 us)
Async XLA Ops:
  0.6 31.1 %copy-start = (bf16[3,3,3,128,256]{4,3,2,1,0:T(8,128)(2,1)S(1)}, bf16[3,3,3,128,256]{4,3,2,1,0:T(8,128)(2,1)}, u32[]{:S(2)}) copy-start(bf16[3,3,3,128,256]{4,3,2,1,0:T(8,128)(2,1)} %param.4) | copy-start | bytes 5308420
  23.5 10.9 %collective-permute-start = (bf16[8,3,16,256]{3,2,1,0:T(8,128)(2,1)S(1)}, bf16[8,3,16,256]{3,2,1,0:T(8,128)(2,1)S(1)}, u32[]{:S(2)}, u32[]{:S(2)}) collective-permute-start(bf16[8,3,16,256]{3,2,1,0:T(8,128)(2,1)S(1)} %slice.4), channel_id=1, source_target_pairs={{0,8},{8,16},{16,24},{24,32},{32,40},{40,48},{48,56},{56,64},{64,7... | collective-permute-start | bytes 589832 | tf_op jit(solution)/shard_map/ppermute | solution.py:189
  35.8 4.3 %collective-permute-start.1 = (bf16[128,3456]{1,0:T(8,128)(2,1)S(1)}, bf16[128,3456]{1,0:T(8,128)(2,1)S(1)}, u32[]{:S(2)}, u32[]{:S(2)}) collective-permute-start(bf16[128,3456]{1,0:T(8,128)(2,1)S(1)} %get-tuple-element.19), channel_id=1, source_target_pairs={{0,8},{8,0},{16,24},{24,16},{32,40},{40,32},{48,56},{56,48},{64,72... | collective-permute-start | bytes 2654216 | tf_op jit(solution)/shard_map/ppermute | solution.py:235
  62.9 12.1 %all-to-all-start.2 = ((bf16[8,4,3456]{2,1,0:T(4,128)(2,1)}), bf16[8,4,3456]{2,1,0:T(4,128)(2,1)S(1)}, u32[]{:S(2)}, u32[]{:S(2)}) async-start(bf16[8,4,3456]{2,1,0:T(4,128)(2,1)} %shard_map.54), calls=%async_computation.2 | async-start | bytes 442368 | tf_op jit(solution)/shard_map/all_to_all | solution.py:193
  66.3 9.4 %collective-permute-start.2 = (bf16[256,128]{1,0:T(8,128)(2,1)S(1)}, bf16[256,128]{1,0:T(8,128)(2,1)S(1)}, u32[]{:S(2)}, u32[]{:S(2)}) collective-permute-start(bf16[256,128]{1,0:T(8,128)(2,1)S(1)} %get-tuple-element.15), channel_id=1, source_target_pairs={{1,0},{2,1},{3,2},{4,3},{5,4},{6,5},{7,6},{9,8},{10,9},{11,10},{12... | collective-permute-start | bytes 196616 | tf_op jit(solution)/shard_map/ppermute | solution.py:189
  75.7 15.3 %all-to-all-start.3 = ((bf16[8,4,3456]{2,1,0:T(4,128)(2,1)}), bf16[8,4,3456]{2,1,0:T(4,128)(2,1)S(1)}, u32[]{:S(2)}, u32[]{:S(2)}) async-start(bf16[8,4,3456]{2,1,0:T(4,128)(2,1)} %shard_map.55), calls=%async_computation.3 | async-start | bytes 442368 | tf_op jit(solution)/shard_map/all_to_all | solution.py:193
  82.1 10.6 %collective-permute-start.3 = (bf16[2,256,128]{2,1,0:T(8,128)(2,1)S(1)}, bf16[2,256,128]{2,1,0:T(8,128)(2,1)S(1)}, u32[]{:S(2)}, u32[]{:S(2)}) collective-permute-start(bf16[2,256,128]{2,1,0:T(8,128)(2,1)S(1)} %pad_maximum_fusion.own_ref), channel_id=1, source_target_pairs={{8,0},{16,8},{24,16},{32,24},{40,32},{48,40},{56,48},{64,56},{72,6... | collective-permute-start | bytes 393224 | tf_op jit(solution)/shard_map/ppermute | solution.py:189
  92.7 13.1 %all-to-all-start.4 = ((bf16[8,4,3456]{2,1,0:T(4,128)(2,1)}), bf16[8,4,3456]{2,1,0:T(4,128)(2,1)S(1)}, u32[]{:S(2)}, u32[]{:S(2)}) async-start(bf16[8,4,3456]{2,1,0:T(4,128)(2,1)} %shard_map.56), calls=%async_computation.4 | async-start | bytes 442368 | tf_op jit(solution)/shard_map/all_to_all | solution.py:193

commit v6 on v5

--- a/solution.py
+++ b/solution.py
@@ -16,10 +16,10 @@
     return (x * 8 + z) * 2 + core
 
 
-XS, ZS, CS = range(4), range(8), range(2)
-X_RINGS = [[slab_of(x, z, c) for x in XS] for z in ZS for c in CS]
-Z_RINGS = [[slab_of(x, z, c) for z in ZS] for x in XS for c in CS]
-XC_RINGS = [[slab_of(x, z, c) for x in XS for c in CS] for z in ZS]
+X4, Z4, B2 = range(4), range(4), range(2)
+WIDE = [[slab_of(x, 2 * zh + zl, c) for x in X4 for zl in B2] for zh in Z4 for c in B2]
+FAR = [[slab_of(x, 2 * zh + zl, c) for zh in Z4] for x in X4 for zl in B2 for c in B2]
+NEAR = [[slab_of(x, 2 * zh + zl, c) for x in X4 for zl in B2 for c in B2] for zh in Z4]
 CORE_PAIRS = [(s, s ^ 1) for s in range(64)]
 
 
@@ -99,7 +99,7 @@
 
 def core_rows(core):
     i, j = iotas(128, 256)
-    return ones_where(j == (((i >> 2) & 7) << 5) + ((i >> 5) << 3) + (i & 3) + core * 4)
+    return ones_where(j == (((i >> 1) & 7) << 5) + ((i >> 4) << 2) + (i & 1) + core * 2)
 
 
 def taps_of(order, both, ze, zo):
@@ -147,19 +147,18 @@
     total = in_ref[0].astype(F32)
     for n in range(1, in_ref.shape[0]):
         total = total + in_ref[n].astype(F32)
-    total = total.astype(BF16)
-    rows = out_ref.shape[1]
     for n in range(out_ref.shape[0]):
-        out_ref[n] = total if total.shape[0] == rows else total[n * rows : n * rows + rows]
+        rows = total if total.shape[0] == 2 else total[2 * n : 2 * n + 2]
+        out_ref[n] = rows.astype(BF16)
 
 
 def last_body(in_ref, out_ref):
-    for m in range(8):
+    for m in range(16):
         rows = in_ref[m].astype(F32) * (1.0 / 256.0)
         for c in range(3):
             for ab in range(9):
                 start = (c * 9 + ab) * 128
-                out_ref[ab * 3 + c, 4 * m : 4 * m + 4] = rows[:, start : start + 128]
+                out_ref[ab * 3 + c, 2 * m : 2 * m + 2] = rows[:, start : start + 128]
 
 
 def input_body(own_ref, up_ref, w_ref, out_ref):
@@ -195,9 +194,9 @@
     )
 
 
-def add_up(value):
+def add_up(value, count):
     size = value.size * 2
-    out_shape = jax.ShapeDtypeStruct((8, 4, 3456), BF16)
+    out_shape = jax.ShapeDtypeStruct((count, 2, 3456), BF16)
     return call(sum_body, out_shape, [VMEM], (size, size))(value)
 
 
@@ -237,19 +236,19 @@
     part = call(
         keep_body, shape((128, 3456), BF16), [SMEM, VMEM, VMEM, VMEM, VMEM], (113 * mb, 3 * mb)
     )(core, both, ze, zo, other)
-    tiles = add_up(exchange(part.reshape(4, 32, 3456), "slab", X_RINGS))
-    tiles = add_up(exchange(tiles, "filt"))
+    tiles = add_up(exchange(part.reshape(8, 16, 3456), "slab", WIDE), 8)
+    tiles = add_up(exchange(tiles, "filt"), 4)
     tiles, right = lax.optimization_barrier((tiles, right))
     own = jnp.stack([grad, right])
     upper = shifted_2(own, "slab", -1)
-    tiles = add_up(exchange(tiles, "slab", Z_RINGS))
+    tiles = add_up(exchange(tiles, "slab", FAR), 16)
     tiles, upper = lax.optimization_barrier((tiles, upper))
     in_grad = call(
         input_body, shape((2, 2, 128, 256), BF16), [VMEM] * 3, (226 * mb, 3 * mb)
     )(own, upper, taps)
     in_grad = in_grad.transpose(0, 2, 1, 3)
 
-    tiles = exchange(tiles, "slab", XC_RINGS)
+    tiles = exchange(tiles, "slab", NEAR)
     out = call(last_body, shape((27, 32, 128), F32), [VMEM], (mb, mb))(tiles)
     weight_grad = out.reshape(3, 3, 3, 32, 128).transpose(0, 1, 2, 4, 3)
     return (in_grad, weight_grad)

time: 107 us -> 106 us (level)
  blocking collectives: 41.7 us -> 55.7 us
  starting transfers between devices: 33.5 us -> 24.3 us
  waiting for transfers between devices: 19.8 us -> 15 us
    all_to_all x2 -> x3, blocking collectives: 41.7 us -> 55.7 us  [exchange(): lax.all_to_all(value, axis, split_axis=0, concat_axis=0, axis_index_group...]
    all_to_all x3 -> x2, starting transfers between devices: 16.6 us -> 8.08 us  [exchange(): lax.all_to_all(value, axis, split_axis=0, concat_axis=0, axis_index_group...]
    all_to_all x3 -> x2, waiting for transfers between devices: 14.9 us -> 11.1 us  [exchange(): lax.all_to_all(value, axis, split_axis=0, concat_axis=0, axis_index_group...]
  transfers between devices with their start and end apart: 7 -> 6, of which waited for: 6 -> 4; matrix products, arithmetic and copies ran while one was open for 1% -> 1% of each run, Pallas kernels for 3% -> 3%
where the time goes in v6:
time: 106 us
  blocking collectives  55.7 us (53%)
  starting transfers between devices  24.3 us (23%)
  waiting for transfers between devices  15 us (14%)
  Pallas kernels  9.17 us (9%)
    all_to_all x3, blocking collectives, exchange(): lax.all_to_all(value, axis, split_axis=0, concat_axis=0, axis_index_group...  55.7 us
    ppermute x3, starting transfers between devices, shifted_2(): lax.ppermute(value, axis, [(source, source + steps) for source in range(f...  14.3 us
    all_to_all x2, waiting for transfers between devices, exchange(): lax.all_to_all(value, axis, split_axis=0, concat_axis=0, axis_index_group...  11.1 us
    all_to_all x2, starting transfers between devices, exchange(): lax.all_to_all(value, axis, split_axis=0, concat_axis=0, axis_index_group...  8.08 us
    pallas_call x1, Pallas kernels, on_device(): call(pack_body, shape((8, 7, 16, 256), BF16), [ANY] * 2, (2 * mb, mb), [p...  2.48 us
    ppermute x1, waiting for transfers between devices, on_device(): other = lax.ppermute(part, 'slab', CORE_PAIRS)  2.39 us
  transfers between devices with their start and end apart: 6, of which 4 were waited for; matrix products, arithmetic and copies ran while one was open for 1% of the time, Pallas kernels for 3%

profile of v6, /device:TPU:1, one launch (start us, length us, event | category | flops | bytes accessed | tf_op | source)
XLA Modules:
  0.0 105.9 jit_solution(3416790485246793106)
XLA Ops:
  0.6 2.5 %shard_map.50 = bf16[8,7,16,256]{3,2,1,0:T(8,128)(2,1)} custom-call(bf16[2,16,16,256]{3,2,1,0:T(8,128)(2,1)} %vol_hbm.1, bf16[1,32,8,128]{3,2,1,0:T(8,128)(2,1)} %err_hbm.1), custom_call_target="tpu_custom_call" | custom-call | flops 2097152 | bytes 1048576 | tf_op jit(solution)/shard_map/pallas_call | solution.py:209
  3.1 20.3 %all_to_all.25.rec_ref = bf16[8,7,16,256]{3,2,1,0:T(8,128)(2,1)S(1)} all-to-all(bf16[8,7,16,256]{3,2,1,0:T(8,128)(2,1)} %shard_map.50), channel_id=1, replica_groups=mesh['slab'=64,'filt'=8] {'filt'}, dimensions={0} | all-to-all | bytes 917504 | tf_op jit(solution)/shard_map/all_to_all | solution.py:192
  23.5 8.3 %collective-permute-start = (bf16[8,3,16,256]{3,2,1,0:T(8,128)(2,1)S(1)}, bf16[8,3,16,256]{3,2,1,0:T(8,128)(2,1)S(1)}, u32[]{:S(2)}, u32[]{:S(2)}) collective-permute-start(bf16[8,3,16,256]{3,2,1,0:T(8,128)(2,1)S(1)} %slice.4), channel_id=1, source_target_pairs={{0,8},{8,16},{16,24},{24,32},{32,40},{40,48},{48,56},{56,64},{64,7... | collective-permute-start | bytes 589832 | tf_op jit(solution)/shard_map/ppermute | solution.py:188
  31.8 1.1 %shard_map.51 = (bf16[256,1152]{1,0:T(8,128)(2,1)S(1)}, bf16[512,1152]{1,0:T(8,128)(2,1)S(1)}) custom-call(bf16[9,3,128,256]{3,2,1,0:T(8,128)(2,1)S(1)} %bitcast.9), custom_call_target="tpu_custom_call" | custom-call | flops 473956352 | bytes 4194304 | tf_op jit(solution)/shard_map/pallas_call | solution.py:222
  32.8 1.5 %collective-permute-done.rim_ref = bf16[8,3,16,256]{3,2,1,0:T(8,128)(2,1)S(1)} collective-permute-done((bf16[8,3,16,256]{3,2,1,0:T(8,128)(2,1)S(1)}, bf16[8,3,16,256]{3,2,1,0:T(8,128)(2,1)S(1)}, u32[]{:S(2)}, u32[]{:S(2)}) %collective-permute-start) | collective-permute-done | bytes 196640 | tf_op jit(solution)/shard_map/ppermute | solution.py:188
  34.3 1.4 %shard_map.52 = (bf16[256,128]{1,0:T(8,128)(2,1)S(1)}, bf16[256,256]{1,0:T(8,128)(2,1)S(1)}, bf16[1152,128]{1,0:T(8,128)(2,1)S(1)}, bf16[1152,128]{1,0:T(8,128)(2,1)S(1)}, bf16[128,3456]{1,0:T(8,128)(2,1)S(1)}) custom-call(s32[1]{0:T(128)} %bitcast.core_ref, bf16[8,7,16,256]{3,2,1,0:T(8,128)(2,1)S(1)} %all_to_all.25.rec_ref, ...), custom_call_target="tpu_custom_call" | custom-call | flops 475004928 | bytes 4194304 | tf_op jit(solution)/shard_map/pallas_call | solution.py:227
  35.8 1.9 %collective-permute-start.1 = (bf16[128,3456]{1,0:T(8,128)(2,1)S(1)}, bf16[128,3456]{1,0:T(8,128)(2,1)S(1)}, u32[]{:S(2)}, u32[]{:S(2)}) collective-permute-start(bf16[128,3456]{1,0:T(8,128)(2,1)S(1)} %get-tuple-element.19), channel_id=1, source_target_pairs={{0,8},{8,0},{16,24},{24,16},{32,40},{40,32},{48,56},{56,48},{64,72... | collective-permute-start | bytes 2654216 | tf_op jit(solution)/shard_map/ppermute | solution.py:234
  37.7 2.4 %collective-permute-done.1.other_ref = bf16[128,3456]{1,0:T(8,128)(2,1)S(1)} collective-permute-done((bf16[128,3456]{1,0:T(8,128)(2,1)S(1)}, bf16[128,3456]{1,0:T(8,128)(2,1)S(1)}, u32[]{:S(2)}, u32[]{:S(2)}) %collective-permute-start.1) | collective-permute-done | bytes 884768 | tf_op jit(solution)/shard_map/ppermute | solution.py:234
  40.1 0.5 shard_map.53
  40.6 22.2 %all_to_all.26.in_ref = bf16[8,16,3456]{2,1,0:T(8,128)(2,1)S(1)} all-to-all(bf16[8,16,3456]{2,1,0:T(8,128)(2,1)S(1)} %bitcast.11), channel_id=1, replica_groups={{0,16,128,144,256,272,384,400},{8,24,136,152,264,280,392,408},{32,48,16..., dimensions={0} | all-to-all | bytes 1769472 | tf_op jit(solution)/shard_map/all_to_all | solution.py:192
  62.9 0.8 shard_map.54
  63.6 3.4 %all-to-all-start.2 = ((bf16[8,2,3456]{2,1,0:T(2,128)(2,1)}), bf16[8,2,3456]{2,1,0:T(2,128)(2,1)S(1)}, u32[]{:S(2)}, u32[]{:S(2)}) async-start(bf16[8,2,3456]{2,1,0:T(2,128)(2,1)} %shard_map.54), calls=%async_computation.2 | async-start | bytes 221184 | tf_op jit(solution)/shard_map/all_to_all | solution.py:192
  67.0 1.3 %collective-permute-start.2 = (bf16[256,128]{1,0:T(8,128)(2,1)S(1)}, bf16[256,128]{1,0:T(8,128)(2,1)S(1)}, u32[]{:S(2)}, u32[]{:S(2)}) collective-permute-start(bf16[256,128]{1,0:T(8,128)(2,1)S(1)} %get-tuple-element.15), channel_id=1, source_target_pairs={{1,0},{2,1},{3,2},{4,3},{5,4},{6,5},{7,6},{9,8},{10,9},{11,10},{12... | collective-permute-start | bytes 196616 | tf_op jit(solution)/shard_map/ppermute | solution.py:188
  68.3 6.3 %all-to-all-done.2.in_ref = bf16[8,2,3456]{2,1,0:T(2,128)(2,1)S(1)} async-done(((bf16[8,2,3456]{2,1,0:T(2,128)(2,1)}), bf16[8,2,3456]{2,1,0:T(2,128)(2,1)S(1)}, u32[]{:S(2)}, u32[]{:S(2)}) %all-to-all-start.2) | async-done | bytes 110624 | tf_op jit(solution)/shard_map/all_to_all | solution.py:192
  74.7 0.0 collective-permute-done.2
  74.7 4.7 %collective-permute-start.3 = (bf16[2,256,128]{2,1,0:T(8,128)(2,1)S(1)}, bf16[2,256,128]{2,1,0:T(8,128)(2,1)S(1)}, u32[]{:S(2)}, u32[]{:S(2)}) collective-permute-start(bf16[2,256,128]{2,1,0:T(8,128)(2,1)S(1)} %pad_maximum_fusion.own_ref), channel_id=1, source_target_pairs={{8,0},{16,8},{24,16},{32,24},{40,32},{48,40},{56,48},{64,56},{72,6... | collective-permute-start | bytes 393224 | tf_op jit(solution)/shard_map/ppermute | solution.py:188
  79.4 13.1 %all_to_all.27.in_ref = bf16[4,2,3456]{2,1,0:T(2,128)(2,1)S(1)} all-to-all(bf16[4,2,3456]{2,1,0:T(2,128)(2,1)S(1)} %shard_map.55), channel_id=1, replica_groups={{0,32,64,96},{8,40,72,104},{16,48,80,112},{24,56,88,120},{128,160,192,2..., dimensions={0} | all-to-all | bytes 110592 | tf_op jit(solution)/shard_map/all_to_all | solution.py:192
  92.6 0.7 shard_map.56
  93.3 0.0 collective-permute-done.3.up_ref
  93.3 4.7 %all-to-all-start.4 = ((bf16[16,2,3456]{2,1,0:T(2,128)(2,1)}), bf16[16,2,3456]{2,1,0:T(2,128)(2,1)S(1)}, u32[]{:S(2)}, u32[]{:S(2)}) async-start(bf16[16,2,3456]{2,1,0:T(2,128)(2,1)} %shard_map.56), calls=%async_computation.4 | async-start | bytes 442368 | tf_op jit(solution)/shard_map/all_to_all | solution.py:192
  98.0 1.2 %shard_map.57 = bf16[2,2,128,256]{3,2,1,0:T(8,128)(2,1)S(1)} custom-call(bf16[2,256,128]{2,1,0:T(8,128)(2,1)S(1)} %pad_maximum_fusion.own_ref, bf16[2,256,128]{2,1,0:T(8,128)(2,1)S(1)} %collective-permute-done.3.up_ref, bf16[9,3,128,256]{3,2,1,0:T(8,128)(2,1)S(1)} %bitcast.10), custom_call_target="tpu_custom_call" | custom-call | flops 236978176 | bytes 3145728 | tf_op jit(solution)/shard_map/pallas_call | solution.py:246
  99.2 1.0 copy.5
  100.1 4.8 %all-to-all-done.4.in_ref = bf16[16,2,3456]{2,1,0:T(2,128)(2,1)S(1)} async-done(((bf16[16,2,3456]{2,1,0:T(2,128)(2,1)}), bf16[16,2,3456]{2,1,0:T(2,128)(2,1)S(1)}, u32[]{:S(2)}, u32[]{:S(2)}) %all-to-all-start.4) | async-done | bytes 221216 | tf_op jit(solution)/shard_map/all_to_all | solution.py:192
  104.9 1.0 shard_map.58
  (5 shorter events, 0.1 us)
Async XLA Ops:
  0.6 31.1 %copy-start = (bf16[3,3,3,128,256]{4,3,2,1,0:T(8,128)(2,1)S(1)}, bf16[3,3,3,128,256]{4,3,2,1,0:T(8,128)(2,1)}, u32[]{:S(2)}) copy-start(bf16[3,3,3,128,256]{4,3,2,1,0:T(8,128)(2,1)} %param.4) | copy-start | bytes 5308420
  23.5 10.9 %collective-permute-start = (bf16[8,3,16,256]{3,2,1,0:T(8,128)(2,1)S(1)}, bf16[8,3,16,256]{3,2,1,0:T(8,128)(2,1)S(1)}, u32[]{:S(2)}, u32[]{:S(2)}) collective-permute-start(bf16[8,3,16,256]{3,2,1,0:T(8,128)(2,1)S(1)} %slice.4), channel_id=1, source_target_pairs={{0,8},{8,16},{16,24},{24,32},{32,40},{40,48},{48,56},{56,64},{64,7... | collective-permute-start | bytes 589832 | tf_op jit(solution)/shard_map/ppermute | solution.py:188
  35.8 4.3 %collective-permute-start.1 = (bf16[128,3456]{1,0:T(8,128)(2,1)S(1)}, bf16[128,3456]{1,0:T(8,128)(2,1)S(1)}, u32[]{:S(2)}, u32[]{:S(2)}) collective-permute-start(bf16[128,3456]{1,0:T(8,128)(2,1)S(1)} %get-tuple-element.19), channel_id=1, source_target_pairs={{0,8},{8,0},{16,24},{24,16},{32,40},{40,32},{48,56},{56,48},{64,72... | collective-permute-start | bytes 2654216 | tf_op jit(solution)/shard_map/ppermute | solution.py:234
  63.6 11.0 %all-to-all-start.2 = ((bf16[8,2,3456]{2,1,0:T(2,128)(2,1)}), bf16[8,2,3456]{2,1,0:T(2,128)(2,1)S(1)}, u32[]{:S(2)}, u32[]{:S(2)}) async-start(bf16[8,2,3456]{2,1,0:T(2,128)(2,1)} %shard_map.54), calls=%async_computation.2 | async-start | bytes 221184 | tf_op jit(solution)/shard_map/all_to_all | solution.py:192
  67.0 7.7 %collective-permute-start.2 = (bf16[256,128]{1,0:T(8,128)(2,1)S(1)}, bf16[256,128]{1,0:T(8,128)(2,1)S(1)}, u32[]{:S(2)}, u32[]{:S(2)}) collective-permute-start(bf16[256,128]{1,0:T(8,128)(2,1)S(1)} %get-tuple-element.15), channel_id=1, source_target_pairs={{1,0},{2,1},{3,2},{4,3},{5,4},{6,5},{7,6},{9,8},{10,9},{11,10},{12... | collective-permute-start | bytes 196616 | tf_op jit(solution)/shard_map/ppermute | solution.py:188
  74.7 18.6 %collective-permute-start.3 = (bf16[2,256,128]{2,1,0:T(8,128)(2,1)S(1)}, bf16[2,256,128]{2,1,0:T(8,128)(2,1)S(1)}, u32[]{:S(2)}, u32[]{:S(2)}) collective-permute-start(bf16[2,256,128]{2,1,0:T(8,128)(2,1)S(1)} %pad_maximum_fusion.own_ref), channel_id=1, source_target_pairs={{8,0},{16,8},{24,16},{32,24},{40,32},{48,40},{56,48},{64,56},{72,6... | collective-permute-start | bytes 393224 | tf_op jit(solution)/shard_map/ppermute | solution.py:188
  93.3 11.6 %all-to-all-start.4 = ((bf16[16,2,3456]{2,1,0:T(2,128)(2,1)}), bf16[16,2,3456]{2,1,0:T(2,128)(2,1)S(1)}, u32[]{:S(2)}, u32[]{:S(2)}) async-start(bf16[16,2,3456]{2,1,0:T(2,128)(2,1)} %shard_map.56), calls=%async_computation.4 | async-start | bytes 442368 | tf_op jit(solution)/shard_map/all_to_all | solution.py:192

commit v7 on v6

--- a/solution.py
+++ b/solution.py
@@ -236,13 +236,13 @@
     part = call(
         keep_body, shape((128, 3456), BF16), [SMEM, VMEM, VMEM, VMEM, VMEM], (113 * mb, 3 * mb)
     )(core, both, ze, zo, other)
-    tiles = add_up(exchange(part.reshape(8, 16, 3456), "slab", WIDE), 8)
-    tiles = add_up(exchange(tiles, "filt"), 4)
-    tiles, right = lax.optimization_barrier((tiles, right))
     own = jnp.stack([grad, right])
     upper = shifted_2(own, "slab", -1)
+    tiles = exchange(part.reshape(8, 16, 3456), "slab", WIDE)
+    tiles, upper = lax.optimization_barrier((tiles, upper))
+    tiles = add_up(tiles, 8)
+    tiles = add_up(exchange(tiles, "filt"), 4)
     tiles = add_up(exchange(tiles, "slab", FAR), 16)
-    tiles, upper = lax.optimization_barrier((tiles, upper))
     in_grad = call(
         input_body, shape((2, 2, 128, 256), BF16), [VMEM] * 3, (226 * mb, 3 * mb)
     )(own, upper, taps)

time: 106 us -> 104 us (0.981)
  blocking collectives: 55.7 us -> 43.4 us
  starting transfers between devices: 24.3 us -> 31.4 us
  waiting for transfers between devices: 15 us -> 17.7 us
    all_to_all x3, blocking collectives: 55.7 us -> 43.4 us  [exchange(): lax.all_to_all(value, axis, split_axis=0, concat_axis=0, axis_index_group...]
    ppermute x3, waiting for transfers between devices: 1.5 us -> 10.6 us  [shifted_2(): lax.ppermute(value, axis, [(source, source + steps) for source in range(f...]
    all_to_all x2, starting transfers between devices: 8.08 us -> 16.5 us  [exchange(): lax.all_to_all(value, axis, split_axis=0, concat_axis=0, axis_index_group...]
    all_to_all x2, waiting for transfers between devices: 11.1 us -> 4.74 us  [exchange(): lax.all_to_all(value, axis, split_axis=0, concat_axis=0, axis_index_group...]
    ppermute x3, starting transfers between devices: 14.3 us -> 13 us  [shifted_2(): lax.ppermute(value, axis, [(source, source + steps) for source in range(f...]
  transfers between devices with their start and end apart: 6 -> 6, of which waited for: 4 -> 5; matrix products, arithmetic and copies ran while one was open for 1% -> 1% of each run, Pallas kernels for 3% -> 2%
where the time goes in v7:
time: 104 us
  blocking collectives  43.4 us (42%)
  starting transfers between devices  31.4 us (30%)
  waiting for transfers between devices  17.7 us (17%)
  Pallas kernels  9.46 us (9%)
    all_to_all x3, blocking collectives, exchange(): lax.all_to_all(value, axis, split_axis=0, concat_axis=0, axis_index_group...  43.4 us
    all_to_all x2, starting transfers between devices, exchange(): lax.all_to_all(value, axis, split_axis=0, concat_axis=0, axis_index_group...  16.5 us
    ppermute x3, starting transfers between devices, shifted_2(): lax.ppermute(value, axis, [(source, source + steps) for source in range(f...  13 us
    ppermute x3, waiting for transfers between devices, shifted_2(): lax.ppermute(value, axis, [(source, source + steps) for source in range(f...  10.6 us
    all_to_all x2, waiting for transfers between devices, exchange(): lax.all_to_all(value, axis, split_axis=0, concat_axis=0, axis_index_group...  4.74 us
    pallas_call x1, Pallas kernels, on_device(): call(pack_body, shape((8, 7, 16, 256), BF16), [ANY] * 2, (2 * mb, mb), [p...  2.48 us
    ppermute x1, waiting for transfers between devices, on_device(): other = lax.ppermute(part, 'slab', CORE_PAIRS)  2.39 us
  transfers between devices with their start and end apart: 6, of which 5 were waited for; matrix products, arithmetic and copies ran while one was open for 1% of the time, Pallas kernels for 2%

profile of v7, /device:TPU:1, one launch (start us, length us, event | category | flops | bytes accessed | tf_op | source)
XLA Modules:
  0.0 103.7 jit_solution(7371578311444582265)
XLA Ops:
  0.6 2.5 %shard_map.50 = bf16[8,7,16,256]{3,2,1,0:T(8,128)(2,1)} custom-call(bf16[2,16,16,256]{3,2,1,0:T(8,128)(2,1)} %vol_hbm.1, bf16[1,32,8,128]{3,2,1,0:T(8,128)(2,1)} %err_hbm.1), custom_call_target="tpu_custom_call" | custom-call | flops 2097152 | bytes 1048576 | tf_op jit(solution)/shard_map/pallas_call | solution.py:209
  3.1 20.3 %all_to_all.25.rec_ref = bf16[8,7,16,256]{3,2,1,0:T(8,128)(2,1)S(1)} all-to-all(bf16[8,7,16,256]{3,2,1,0:T(8,128)(2,1)} %shard_map.50), channel_id=1, replica_groups=mesh['slab'=64,'filt'=8] {'filt'}, dimensions={0} | all-to-all | bytes 917504 | tf_op jit(solution)/shard_map/all_to_all | solution.py:192
  23.5 8.3 %collective-permute-start = (bf16[8,3,16,256]{3,2,1,0:T(8,128)(2,1)S(1)}, bf16[8,3,16,256]{3,2,1,0:T(8,128)(2,1)S(1)}, u32[]{:S(2)}, u32[]{:S(2)}) collective-permute-start(bf16[8,3,16,256]{3,2,1,0:T(8,128)(2,1)S(1)} %slice.4), channel_id=1, source_target_pairs={{0,8},{8,16},{16,24},{24,32},{32,40},{40,48},{48,56},{56,64},{64,7... | collective-permute-start | bytes 589832 | tf_op jit(solution)/shard_map/ppermute | solution.py:188
  31.8 1.1 %shard_map.51 = (bf16[256,1152]{1,0:T(8,128)(2,1)S(1)}, bf16[512,1152]{1,0:T(8,128)(2,1)S(1)}) custom-call(bf16[9,3,128,256]{3,2,1,0:T(8,128)(2,1)S(1)} %bitcast.9), custom_call_target="tpu_custom_call" | custom-call | flops 473956352 | bytes 4194304 | tf_op jit(solution)/shard_map/pallas_call | solution.py:222
  32.8 1.5 %collective-permute-done.rim_ref = bf16[8,3,16,256]{3,2,1,0:T(8,128)(2,1)S(1)} collective-permute-done((bf16[8,3,16,256]{3,2,1,0:T(8,128)(2,1)S(1)}, bf16[8,3,16,256]{3,2,1,0:T(8,128)(2,1)S(1)}, u32[]{:S(2)}, u32[]{:S(2)}) %collective-permute-start) | collective-permute-done | bytes 196640 | tf_op jit(solution)/shard_map/ppermute | solution.py:188
  34.3 1.4 %shard_map.52 = (bf16[256,128]{1,0:T(8,128)(2,1)S(1)}, bf16[256,256]{1,0:T(8,128)(2,1)S(1)}, bf16[1152,128]{1,0:T(8,128)(2,1)S(1)}, bf16[1152,128]{1,0:T(8,128)(2,1)S(1)}, bf16[128,3456]{1,0:T(8,128)(2,1)S(1)}) custom-call(s32[1]{0:T(128)} %bitcast.core_ref, bf16[8,7,16,256]{3,2,1,0:T(8,128)(2,1)S(1)} %all_to_all.25.rec_ref, ...), custom_call_target="tpu_custom_call" | custom-call | flops 475004928 | bytes 4194304 | tf_op jit(solution)/shard_map/pallas_call | solution.py:227
  35.8 1.9 %collective-permute-start.2 = (bf16[128,3456]{1,0:T(8,128)(2,1)S(1)}, bf16[128,3456]{1,0:T(8,128)(2,1)S(1)}, u32[]{:S(2)}, u32[]{:S(2)}) collective-permute-start(bf16[128,3456]{1,0:T(8,128)(2,1)S(1)} %get-tuple-element.17), channel_id=1, source_target_pairs={{0,8},{8,0},{16,24},{24,16},{32,40},{40,32},{48,56},{56,48},{64,72... | collective-permute-start | bytes 2654216 | tf_op jit(solution)/shard_map/ppermute | solution.py:234
  37.7 2.4 %collective-permute-done.2.other_ref = bf16[128,3456]{1,0:T(8,128)(2,1)S(1)} collective-permute-done((bf16[128,3456]{1,0:T(8,128)(2,1)S(1)}, bf16[128,3456]{1,0:T(8,128)(2,1)S(1)}, u32[]{:S(2)}, u32[]{:S(2)}) %collective-permute-start.2) | collective-permute-done | bytes 884768 | tf_op jit(solution)/shard_map/ppermute | solution.py:234
  40.1 1.5 %shard_map.53 = bf16[128,3456]{1,0:T(8,128)(2,1)} custom-call(s32[1]{0:T(128)} %bitcast.core_ref, bf16[256,256]{1,0:T(8,128)(2,1)S(1)} %get-tuple-element.14.both_ref, bf16[1152,128]{1,0:T(8,128)(2,1)S(1)} %get-tuple-element.15.ze, bf16[1152,128]{1,0:T(8,128)(2,1)S(1)} %get-tuple-element.16.zo, bf16[128,3456]{1,0:T(8,128)(2,1)S(1)} %collective-permute-done.2.other_ref), custom_call_target="tpu_custom_call" | custom-call | flops 118489088 | bytes 3145728 | tf_op jit(solution)/shard_map/pallas_call | solution.py:236
  41.6 9.1 %all-to-all-start.1 = ((bf16[8,16,3456]{2,1,0:T(8,128)(2,1)}), bf16[8,16,3456]{2,1,0:T(8,128)(2,1)S(1)}, u32[]{:S(2)}, u32[]{:S(2)}) async-start(bf16[8,16,3456]{2,1,0:T(8,128)(2,1)} %bitcast.4), calls=%async_computation.1 | async-start | bytes 1769472 | tf_op jit(solution)/shard_map/all_to_all | solution.py:192
  50.6 1.3 %collective-permute-start.1 = (bf16[256,128]{1,0:T(8,128)(2,1)S(1)}, bf16[256,128]{1,0:T(8,128)(2,1)S(1)}, u32[]{:S(2)}, u32[]{:S(2)}) collective-permute-start(bf16[256,128]{1,0:T(8,128)(2,1)S(1)} %get-tuple-element.13), channel_id=1, source_target_pairs={{1,0},{2,1},{3,2},{4,3},{5,4},{6,5},{7,6},{9,8},{10,9},{11,10},{12... | collective-permute-start | bytes 196616 | tf_op jit(solution)/shard_map/ppermute | solution.py:188
  51.9 4.0 %collective-permute-done.1 = bf16[256,128]{1,0:T(8,128)(2,1)S(1)} collective-permute-done((bf16[256,128]{1,0:T(8,128)(2,1)S(1)}, bf16[256,128]{1,0:T(8,128)(2,1)S(1)}, u32[]{:S(2)}, u32[]{:S(2)}) %collective-permute-start.1) | collective-permute-done | bytes 65568 | tf_op jit(solution)/shard_map/ppermute | solution.py:188
  55.9 3.4 %collective-permute-start.3 = (bf16[2,256,128]{2,1,0:T(8,128)(2,1)S(1)}, bf16[2,256,128]{2,1,0:T(8,128)(2,1)S(1)}, u32[]{:S(2)}, u32[]{:S(2)}) collective-permute-start(bf16[2,256,128]{2,1,0:T(8,128)(2,1)S(1)} %pad_maximum_fusion.own_ref), channel_id=1, source_target_pairs={{8,0},{16,8},{24,16},{32,24},{40,32},{48,40},{56,48},{64,56},{72,6... | collective-permute-start | bytes 393224 | tf_op jit(solution)/shard_map/ppermute | solution.py:188
  59.4 5.1 %collective-permute-done.3.up_ref = bf16[2,256,128]{2,1,0:T(8,128)(2,1)S(1)} collective-permute-done((bf16[2,256,128]{2,1,0:T(8,128)(2,1)S(1)}, bf16[2,256,128]{2,1,0:T(8,128)(2,1)S(1)}, u32[]{:S(2)}, u32[]{:S(2)}) %collective-permute-start.3) | collective-permute-done | bytes 131104 | tf_op jit(solution)/shard_map/ppermute | solution.py:188
  64.4 0.0 all-to-all-done.1.in_ref
  64.4 0.1 shard_map.55
  64.6 10.4 %all_to_all.26.in_ref = bf16[8,2,3456]{2,1,0:T(2,128)(2,1)S(1)} all-to-all(bf16[8,2,3456]{2,1,0:T(2,128)(2,1)S(1)} %shard_map.55), channel_id=1, replica_groups=mesh['slab'=64,'filt'=8] {'filt'}, dimensions={0} | all-to-all | bytes 221184 | tf_op jit(solution)/shard_map/all_to_all | solution.py:192
  75.0 12.7 %all_to_all.27.in_ref = bf16[4,2,3456]{2,1,0:T(2,128)(2,1)S(1)} all-to-all(bf16[4,2,3456]{2,1,0:T(2,128)(2,1)S(1)} %shard_map.56), channel_id=1, replica_groups={{0,32,64,96},{8,40,72,104},{16,48,80,112},{24,56,88,120},{128,160,192,2..., dimensions={0} | all-to-all | bytes 110592 | tf_op jit(solution)/shard_map/all_to_all | solution.py:192
  87.7 0.7 shard_map.57
  88.4 7.4 %all-to-all-start.4 = ((bf16[16,2,3456]{2,1,0:T(2,128)(2,1)}), bf16[16,2,3456]{2,1,0:T(2,128)(2,1)S(1)}, u32[]{:S(2)}, u32[]{:S(2)}) async-start(bf16[16,2,3456]{2,1,0:T(2,128)(2,1)} %shard_map.57), calls=%async_computation.4 | async-start | bytes 442368 | tf_op jit(solution)/shard_map/all_to_all | solution.py:192
  95.9 1.2 %shard_map.54 = bf16[2,2,128,256]{3,2,1,0:T(8,128)(2,1)S(1)} custom-call(bf16[2,256,128]{2,1,0:T(8,128)(2,1)S(1)} %pad_maximum_fusion.own_ref, bf16[2,256,128]{2,1,0:T(8,128)(2,1)S(1)} %collective-permute-done.3.up_ref, bf16[9,3,128,256]{3,2,1,0:T(8,128)(2,1)S(1)} %bitcast.10), custom_call_target="tpu_custom_call" | custom-call | flops 236978176 | bytes 3145728 | tf_op jit(solution)/shard_map/pallas_call | solution.py:246
  97.0 1.0 copy.5
  98.0 4.7 %all-to-all-done.4.in_ref = bf16[16,2,3456]{2,1,0:T(2,128)(2,1)S(1)} async-done(((bf16[16,2,3456]{2,1,0:T(2,128)(2,1)}), bf16[16,2,3456]{2,1,0:T(2,128)(2,1)S(1)}, u32[]{:S(2)}, u32[]{:S(2)}) %all-to-all-start.4) | async-done | bytes 221216 | tf_op jit(solution)/shard_map/all_to_all | solution.py:192
  102.7 1.0 shard_map.58
  (5 shorter events, 0.1 us)
Async XLA Ops:
  0.6 31.1 %copy-start = (bf16[3,3,3,128,256]{4,3,2,1,0:T(8,128)(2,1)S(1)}, bf16[3,3,3,128,256]{4,3,2,1,0:T(8,128)(2,1)}, u32[]{:S(2)}) copy-start(bf16[3,3,3,128,256]{4,3,2,1,0:T(8,128)(2,1)} %param.4) | copy-start | bytes 5308420
  23.5 10.9 %collective-permute-start = (bf16[8,3,16,256]{3,2,1,0:T(8,128)(2,1)S(1)}, bf16[8,3,16,256]{3,2,1,0:T(8,128)(2,1)S(1)}, u32[]{:S(2)}, u32[]{:S(2)}) collective-permute-start(bf16[8,3,16,256]{3,2,1,0:T(8,128)(2,1)S(1)} %slice.4), channel_id=1, source_target_pairs={{0,8},{8,16},{16,24},{24,32},{32,40},{40,48},{48,56},{56,64},{64,7... | collective-permute-start | bytes 589832 | tf_op jit(solution)/shard_map/ppermute | solution.py:188
  35.8 4.3 %collective-permute-start.2 = (bf16[128,3456]{1,0:T(8,128)(2,1)S(1)}, bf16[128,3456]{1,0:T(8,128)(2,1)S(1)}, u32[]{:S(2)}, u32[]{:S(2)}) collective-permute-start(bf16[128,3456]{1,0:T(8,128)(2,1)S(1)} %get-tuple-element.17), channel_id=1, source_target_pairs={{0,8},{8,0},{16,24},{24,16},{32,40},{40,32},{48,56},{56,48},{64,72... | collective-permute-start | bytes 2654216 | tf_op jit(solution)/shard_map/ppermute | solution.py:234
  41.6 22.9 %all-to-all-start.1 = ((bf16[8,16,3456]{2,1,0:T(8,128)(2,1)}), bf16[8,16,3456]{2,1,0:T(8,128)(2,1)S(1)}, u32[]{:S(2)}, u32[]{:S(2)}) async-start(bf16[8,16,3456]{2,1,0:T(8,128)(2,1)} %bitcast.4), calls=%async_computation.1 | async-start | bytes 1769472 | tf_op jit(solution)/shard_map/all_to_all | solution.py:192
  50.6 5.3 %collective-permute-start.1 = (bf16[256,128]{1,0:T(8,128)(2,1)S(1)}, bf16[256,128]{1,0:T(8,128)(2,1)S(1)}, u32[]{:S(2)}, u32[]{:S(2)}) collective-permute-start(bf16[256,128]{1,0:T(8,128)(2,1)S(1)} %get-tuple-element.13), channel_id=1, source_target_pairs={{1,0},{2,1},{3,2},{4,3},{5,4},{6,5},{7,6},{9,8},{10,9},{11,10},{12... | collective-permute-start | bytes 196616 | tf_op jit(solution)/shard_map/ppermute | solution.py:188
  55.9 8.5 %collective-permute-start.3 = (bf16[2,256,128]{2,1,0:T(8,128)(2,1)S(1)}, bf16[2,256,128]{2,1,0:T(8,128)(2,1)S(1)}, u32[]{:S(2)}, u32[]{:S(2)}) collective-permute-start(bf16[2,256,128]{2,1,0:T(8,128)(2,1)S(1)} %pad_maximum_fusion.own_ref), channel_id=1, source_target_pairs={{8,0},{16,8},{24,16},{32,24},{40,32},{48,40},{56,48},{64,56},{72,6... | collective-permute-start | bytes 393224 | tf_op jit(solution)/shard_map/ppermute | solution.py:188
  88.4 14.3 %all-to-all-start.4 = ((bf16[16,2,3456]{2,1,0:T(2,128)(2,1)}), bf16[16,2,3456]{2,1,0:T(2,128)(2,1)S(1)}, u32[]{:S(2)}, u32[]{:S(2)}) async-start(bf16[16,2,3456]{2,1,0:T(2,128)(2,1)} %shard_map.57), calls=%async_computation.4 | async-start | bytes 442368 | tf_op jit(solution)/shard_map/all_to_all | solution.py:192

commit v8 on v7

--- a/solution.py
+++ b/solution.py
@@ -23,13 +23,13 @@
 CORE_PAIRS = [(s, s ^ 1) for s in range(64)]
 
 
-def call(body, out_shape, in_specs, cost, scratch=(), limit=LIMIT):
+def call(body, out_shape, in_specs, cost, scratch=(), limit=LIMIT, out_spec=VMEM):
     many = isinstance(out_shape, (tuple, list))
     return pl.pallas_call(
         body,
         out_shape=out_shape,
         in_specs=in_specs,
-        out_specs=[VMEM] * len(out_shape) if many else VMEM,
+        out_specs=[out_spec] * len(out_shape) if many else out_spec,
         scratch_shapes=list(scratch),
         compiler_params=pltpu.CompilerParams(vmem_limit_bytes=limit),
         cost_estimate=pl.CostEstimate(flops=cost[0], bytes_accessed=cost[1], transcendentals=0),
@@ -55,19 +55,25 @@
     )
 
 
-def pack_body(vol_hbm, err_hbm, send_ref, vol_ref, err_ref, sems):
+def pack_body(vol_hbm, err_hbm, send_hbm, vol_ref, err_ref, send_ref, sems, out_sems):
     copies = [
-        pltpu.make_async_copy(vol_hbm, vol_ref, sems.at[0]),
-        pltpu.make_async_copy(err_hbm, err_ref, sems.at[1]),
+        pltpu.make_async_copy(vol_hbm.at[0], vol_ref.at[0], sems.at[0]),
+        pltpu.make_async_copy(vol_hbm.at[1], vol_ref.at[1], sems.at[1]),
+        pltpu.make_async_copy(err_hbm, err_ref, sems.at[2]),
     ]
     for copy in copies:
         copy.start()
+    outs = [
+        pltpu.make_async_copy(send_ref.at[:, 0:3], send_hbm.at[:, 0:3], out_sems.at[0]),
+        pltpu.make_async_copy(send_ref.at[:, 3:6], send_hbm.at[:, 3:6], out_sems.at[1]),
+        pltpu.make_async_copy(send_ref.at[:, 6:7], send_hbm.at[:, 6:7], out_sems.at[2]),
+    ]
     i, j = iotas(256, 256)
     row_first = ones_where(j == ((i & 15) << 4) + (i >> 4))
     even_odd = ones_where(i == ((j & 127) << 1) + (j >> 7))
     error_rows = ones_where(j == ((i & 31) << 3) + (i >> 5))
-    copies[0].wait()
     for p in range(2):
+        copies[p].wait()
         plane = vol_ref[p].reshape(256, 256)
         plane = mm(row_first, plane).astype(BF16)
         plane = mm(plane, even_odd).astype(BF16)
@@ -79,12 +85,16 @@
                 else:
                     piece = plane[row * 16 : row * 16 + 16]
                 send_ref[y, p * 3 + b] = piece
-    copies[1].wait()
+        outs[p].start()
+    copies[2].wait()
     error = mm(error_rows, err_ref[0].reshape(256, 128)).astype(BF16)
     for y in range(8):
         for u in range(2):
             start = y * 32 + u * 16
             send_ref[y, 6, :, u * 128 : u * 128 + 128] = error[start : start + 16]
+    outs[2].start()
+    for out in outs:
+        out.wait()
 
 
 def turn_body(w_ref, even_ref, odd_ref):
@@ -136,11 +146,20 @@
         part_ref[:, c * 1152 : c * 1152 + 1152] = parts[c].astype(BF16)
 
 
-def keep_body(core_ref, both_ref, ze, zo, other_ref, part_ref):
-    parts = taps_of(core_rows(core_ref[0]), both_ref[...], ze, zo)
-    for c in range(3):
-        cols = slice(c * 1152, c * 1152 + 1152)
-        part_ref[:, cols] = (parts[c] + other_ref[:, cols].astype(F32)).astype(BF16)
+def keep_body(core_ref, both_ref, ze, zo, other_ref, part_hbm, part_ref, sems):
+    order = core_rows(core_ref[0])
+    both = both_ref[...]
+    now = mm(order, both[:, :128]).astype(BF16)
+    after = mm(order, both[:, 128:]).astype(BF16)
+    copies = []
+    for c, (grad, stack) in enumerate(((after, zo), (now, ze), (now, zo))):
+        cols = pl.ds(c * 1152, 1152)
+        total = mm_nt(grad, stack[...]) + other_ref[:, cols].astype(F32)
+        part_ref[:, cols] = total.astype(BF16)
+        copies.append(pltpu.make_async_copy(part_ref.at[:, cols], part_hbm.at[:, cols], sems.at[c]))
+        copies[-1].start()
+    for copy in copies:
+        copy.wait()
 
 
 def sum_body(in_ref, out_ref):
@@ -214,9 +233,12 @@
         [
             pltpu.VMEM(volume.shape, BF16),
             pltpu.VMEM(out_error.shape, BF16),
-            pltpu.SemaphoreType.DMA((2,)),
+            pltpu.VMEM((8, 7, 16, 256), BF16),
+            pltpu.SemaphoreType.DMA((3,)),
+            pltpu.SemaphoreType.DMA((3,)),
         ],
         62500000,
+        ANY,
     )(volume, out_error)
     received = exchange(send, "filt")
     even, odd = call(
@@ -234,7 +256,13 @@
     other = lax.ppermute(part, "slab", CORE_PAIRS)
     right = shifted_2(grad, "filt", -1)
     part = call(
-        keep_body, shape((128, 3456), BF16), [SMEM, VMEM, VMEM, VMEM, VMEM], (113 * mb, 3 * mb)
+        keep_body,
+        shape((128, 3456), BF16),
+        [SMEM, VMEM, VMEM, VMEM, VMEM],
+        (113 * mb, 3 * mb),
+        [pltpu.VMEM((128, 3456), BF16), pltpu.SemaphoreType.DMA((3,))],
+        LIMIT,
+        ANY,
     )(core, both, ze, zo, other)
     own = jnp.stack([grad, right])
     upper = shifted_2(own, "slab", -1)

time: 104 us -> 104 us (level)
  no operation moved by 1% of the time
where the time goes in v8:
time: 104 us
  blocking collectives  43.5 us (42%)
  starting transfers between devices  31.4 us (30%)
  waiting for transfers between devices  17.7 us (17%)
  Pallas kernels  9.44 us (9%)
    all_to_all x3, blocking collectives, exchange(): lax.all_to_all(value, axis, split_axis=0, concat_axis=0, axis_index_group...  43.5 us
    all_to_all x2, starting transfers between devices, exchange(): lax.all_to_all(value, axis, split_axis=0, concat_axis=0, axis_index_group...  16.5 us
    ppermute x3, starting transfers between devices, shifted_2(): lax.ppermute(value, axis, [(source, source + steps) for source in range(f...  13 us
    ppermute x3, waiting for transfers between devices, shifted_2(): lax.ppermute(value, axis, [(source, source + steps) for source in range(f...  10.6 us
    all_to_all x2, waiting for transfers between devices, exchange(): lax.all_to_all(value, axis, split_axis=0, concat_axis=0, axis_index_group...  4.74 us
    pallas_call x1, Pallas kernels, on_device(): call(pack_body, shape((8, 7, 16, 256), BF16), [ANY] * 2, (2 * mb, mb), [p...  2.58 us
    ppermute x1, waiting for transfers between devices, on_device(): other = lax.ppermute(part, 'slab', CORE_PAIRS)  2.39 us
  transfers between devices with their start and end apart: 6, of which 5 were waited for; matrix products, arithmetic and copies ran while one was open for 1% of the time, Pallas kernels for 2%

profile of v8, /device:TPU:1, one launch (start us, length us, event | category | flops | bytes accessed | tf_op | source)
XLA Modules:
  0.0 103.7 jit_solution(13924220692879964990)
XLA Ops:
  0.6 2.6 %shard_map.50 = bf16[8,7,16,256]{3,2,1,0:T(8,128)(2,1)} custom-call(bf16[2,16,16,256]{3,2,1,0:T(8,128)(2,1)} %vol_hbm.1, bf16[1,32,8,128]{3,2,1,0:T(8,128)(2,1)} %err_hbm.1), custom_call_target="tpu_custom_call" | custom-call | flops 2097152 | bytes 1048576 | tf_op jit(solution)/shard_map/pallas_call | solution.py:228
  3.2 20.3 %all_to_all.25.rec_ref = bf16[8,7,16,256]{3,2,1,0:T(8,128)(2,1)S(1)} all-to-all(bf16[8,7,16,256]{3,2,1,0:T(8,128)(2,1)} %shard_map.50), channel_id=1, replica_groups=mesh['slab'=64,'filt'=8] {'filt'}, dimensions={0} | all-to-all | bytes 917504 | tf_op jit(solution)/shard_map/all_to_all | solution.py:211
  23.6 8.3 %collective-permute-start = (bf16[8,3,16,256]{3,2,1,0:T(8,128)(2,1)S(1)}, bf16[8,3,16,256]{3,2,1,0:T(8,128)(2,1)S(1)}, u32[]{:S(2)}, u32[]{:S(2)}) collective-permute-start(bf16[8,3,16,256]{3,2,1,0:T(8,128)(2,1)S(1)} %slice.4), channel_id=1, source_target_pairs={{0,8},{8,16},{16,24},{24,32},{32,40},{40,48},{48,56},{56,64},{64,7... | collective-permute-start | bytes 589832 | tf_op jit(solution)/shard_map/ppermute | solution.py:207
  31.9 1.1 %shard_map.51 = (bf16[256,1152]{1,0:T(8,128)(2,1)S(1)}, bf16[512,1152]{1,0:T(8,128)(2,1)S(1)}) custom-call(bf16[9,3,128,256]{3,2,1,0:T(8,128)(2,1)S(1)} %bitcast.9), custom_call_target="tpu_custom_call" | custom-call | flops 473956352 | bytes 4194304 | tf_op jit(solution)/shard_map/pallas_call | solution.py:244
  32.9 1.5 %collective-permute-done.rim_ref = bf16[8,3,16,256]{3,2,1,0:T(8,128)(2,1)S(1)} collective-permute-done((bf16[8,3,16,256]{3,2,1,0:T(8,128)(2,1)S(1)}, bf16[8,3,16,256]{3,2,1,0:T(8,128)(2,1)S(1)}, u32[]{:S(2)}, u32[]{:S(2)}) %collective-permute-start) | collective-permute-done | bytes 196640 | tf_op jit(solution)/shard_map/ppermute | solution.py:207
  34.4 1.4 %shard_map.52 = (bf16[256,128]{1,0:T(8,128)(2,1)S(1)}, bf16[256,256]{1,0:T(8,128)(2,1)S(1)}, bf16[1152,128]{1,0:T(8,128)(2,1)S(1)}, bf16[1152,128]{1,0:T(8,128)(2,1)S(1)}, bf16[128,3456]{1,0:T(8,128)(2,1)S(1)}) custom-call(s32[1]{0:T(128)} %bitcast.core_ref, bf16[8,7,16,256]{3,2,1,0:T(8,128)(2,1)S(1)} %all_to_all.25.rec_ref, ...), custom_call_target="tpu_custom_call" | custom-call | flops 475004928 | bytes 4194304 | tf_op jit(solution)/shard_map/pallas_call | solution.py:249
  35.9 1.9 %collective-permute-start.2 = (bf16[128,3456]{1,0:T(8,128)(2,1)S(1)}, bf16[128,3456]{1,0:T(8,128)(2,1)S(1)}, u32[]{:S(2)}, u32[]{:S(2)}) collective-permute-start(bf16[128,3456]{1,0:T(8,128)(2,1)S(1)} %get-tuple-element.17), channel_id=1, source_target_pairs={{0,8},{8,0},{16,24},{24,16},{32,40},{40,32},{48,56},{56,48},{64,72... | collective-permute-start | bytes 2654216 | tf_op jit(solution)/shard_map/ppermute | solution.py:256
  37.8 2.4 %collective-permute-done.2.other_ref = bf16[128,3456]{1,0:T(8,128)(2,1)S(1)} collective-permute-done((bf16[128,3456]{1,0:T(8,128)(2,1)S(1)}, bf16[128,3456]{1,0:T(8,128)(2,1)S(1)}, u32[]{:S(2)}, u32[]{:S(2)}) %collective-permute-start.2) | collective-permute-done | bytes 884768 | tf_op jit(solution)/shard_map/ppermute | solution.py:256
  40.2 1.3 %shard_map.53 = bf16[128,3456]{1,0:T(8,128)(2,1)} custom-call(s32[1]{0:T(128)} %bitcast.core_ref, bf16[256,256]{1,0:T(8,128)(2,1)S(1)} %get-tuple-element.14.both_ref, bf16[1152,128]{1,0:T(8,128)(2,1)S(1)} %get-tuple-element.15.ze, bf16[1152,128]{1,0:T(8,128)(2,1)S(1)} %get-tuple-element.16.zo, bf16[128,3456]{1,0:T(8,128)(2,1)S(1)} %collective-permute-done.2.other_ref), custom_call_target="tpu_custom_call" | custom-call | flops 118489088 | bytes 3145728 | tf_op jit(solution)/shard_map/pallas_call | solution.py:258
  41.5 9.0 %all-to-all-start.1 = ((bf16[8,16,3456]{2,1,0:T(8,128)(2,1)}), bf16[8,16,3456]{2,1,0:T(8,128)(2,1)S(1)}, u32[]{:S(2)}, u32[]{:S(2)}) async-start(bf16[8,16,3456]{2,1,0:T(8,128)(2,1)} %bitcast.4), calls=%async_computation.1 | async-start | bytes 1769472 | tf_op jit(solution)/shard_map/all_to_all | solution.py:211
  50.6 1.3 %collective-permute-start.1 = (bf16[256,128]{1,0:T(8,128)(2,1)S(1)}, bf16[256,128]{1,0:T(8,128)(2,1)S(1)}, u32[]{:S(2)}, u32[]{:S(2)}) collective-permute-start(bf16[256,128]{1,0:T(8,128)(2,1)S(1)} %get-tuple-element.13), channel_id=1, source_target_pairs={{1,0},{2,1},{3,2},{4,3},{5,4},{6,5},{7,6},{9,8},{10,9},{11,10},{12... | collective-permute-start | bytes 196616 | tf_op jit(solution)/shard_map/ppermute | solution.py:207
  51.9 4.0 %collective-permute-done.1 = bf16[256,128]{1,0:T(8,128)(2,1)S(1)} collective-permute-done((bf16[256,128]{1,0:T(8,128)(2,1)S(1)}, bf16[256,128]{1,0:T(8,128)(2,1)S(1)}, u32[]{:S(2)}, u32[]{:S(2)}) %collective-permute-start.1) | collective-permute-done | bytes 65568 | tf_op jit(solution)/shard_map/ppermute | solution.py:207
  55.9 3.4 %collective-permute-start.3 = (bf16[2,256,128]{2,1,0:T(8,128)(2,1)S(1)}, bf16[2,256,128]{2,1,0:T(8,128)(2,1)S(1)}, u32[]{:S(2)}, u32[]{:S(2)}) collective-permute-start(bf16[2,256,128]{2,1,0:T(8,128)(2,1)S(1)} %pad_maximum_fusion.own_ref), channel_id=1, source_target_pairs={{8,0},{16,8},{24,16},{32,24},{40,32},{48,40},{56,48},{64,56},{72,6... | collective-permute-start | bytes 393224 | tf_op jit(solution)/shard_map/ppermute | solution.py:207
  59.3 5.1 %collective-permute-done.3.up_ref = bf16[2,256,128]{2,1,0:T(8,128)(2,1)S(1)} collective-permute-done((bf16[2,256,128]{2,1,0:T(8,128)(2,1)S(1)}, bf16[2,256,128]{2,1,0:T(8,128)(2,1)S(1)}, u32[]{:S(2)}, u32[]{:S(2)}) %collective-permute-start.3) | collective-permute-done | bytes 131104 | tf_op jit(solution)/shard_map/ppermute | solution.py:207
  64.4 0.0 all-to-all-done.1.in_ref
  64.4 0.1 shard_map.55
  64.5 10.4 %all_to_all.26.in_ref = bf16[8,2,3456]{2,1,0:T(2,128)(2,1)S(1)} all-to-all(bf16[8,2,3456]{2,1,0:T(2,128)(2,1)S(1)} %shard_map.55), channel_id=1, replica_groups=mesh['slab'=64,'filt'=8] {'filt'}, dimensions={0} | all-to-all | bytes 221184 | tf_op jit(solution)/shard_map/all_to_all | solution.py:211
  75.0 12.7 %all_to_all.27.in_ref = bf16[4,2,3456]{2,1,0:T(2,128)(2,1)S(1)} all-to-all(bf16[4,2,3456]{2,1,0:T(2,128)(2,1)S(1)} %shard_map.56), channel_id=1, replica_groups={{0,32,64,96},{8,40,72,104},{16,48,80,112},{24,56,88,120},{128,160,192,2..., dimensions={0} | all-to-all | bytes 110592 | tf_op jit(solution)/shard_map/all_to_all | solution.py:211
  87.7 0.7 shard_map.57
  88.4 7.4 %all-to-all-start.4 = ((bf16[16,2,3456]{2,1,0:T(2,128)(2,1)}), bf16[16,2,3456]{2,1,0:T(2,128)(2,1)S(1)}, u32[]{:S(2)}, u32[]{:S(2)}) async-start(bf16[16,2,3456]{2,1,0:T(2,128)(2,1)} %shard_map.57), calls=%async_computation.4 | async-start | bytes 442368 | tf_op jit(solution)/shard_map/all_to_all | solution.py:211
  95.8 1.1 %shard_map.54 = bf16[2,2,128,256]{3,2,1,0:T(8,128)(2,1)S(1)} custom-call(bf16[2,256,128]{2,1,0:T(8,128)(2,1)S(1)} %pad_maximum_fusion.own_ref, bf16[2,256,128]{2,1,0:T(8,128)(2,1)S(1)} %collective-permute-done.3.up_ref, bf16[9,3,128,256]{3,2,1,0:T(8,128)(2,1)S(1)} %bitcast.10), custom_call_target="tpu_custom_call" | custom-call | flops 236978176 | bytes 3145728 | tf_op jit(solution)/shard_map/pallas_call | solution.py:274
  97.0 1.0 copy.5
  98.0 4.7 %all-to-all-done.4.in_ref = bf16[16,2,3456]{2,1,0:T(2,128)(2,1)S(1)} async-done(((bf16[16,2,3456]{2,1,0:T(2,128)(2,1)}), bf16[16,2,3456]{2,1,0:T(2,128)(2,1)S(1)}, u32[]{:S(2)}, u32[]{:S(2)}) %all-to-all-start.4) | async-done | bytes 221216 | tf_op jit(solution)/shard_map/all_to_all | solution.py:211
  102.7 1.0 shard_map.58
  (5 shorter events, 0.1 us)
Async XLA Ops:
  0.6 31.2 %copy-start = (bf16[3,3,3,128,256]{4,3,2,1,0:T(8,128)(2,1)S(1)}, bf16[3,3,3,128,256]{4,3,2,1,0:T(8,128)(2,1)}, u32[]{:S(2)}) copy-start(bf16[3,3,3,128,256]{4,3,2,1,0:T(8,128)(2,1)} %param.4) | copy-start | bytes 5308420
  23.6 10.9 %collective-permute-start = (bf16[8,3,16,256]{3,2,1,0:T(8,128)(2,1)S(1)}, bf16[8,3,16,256]{3,2,1,0:T(8,128)(2,1)S(1)}, u32[]{:S(2)}, u32[]{:S(2)}) collective-permute-start(bf16[8,3,16,256]{3,2,1,0:T(8,128)(2,1)S(1)} %slice.4), channel_id=1, source_target_pairs={{0,8},{8,16},{16,24},{24,32},{32,40},{40,48},{48,56},{56,64},{64,7... | collective-permute-start | bytes 589832 | tf_op jit(solution)/shard_map/ppermute | solution.py:207
  35.9 4.3 %collective-permute-start.2 = (bf16[128,3456]{1,0:T(8,128)(2,1)S(1)}, bf16[128,3456]{1,0:T(8,128)(2,1)S(1)}, u32[]{:S(2)}, u32[]{:S(2)}) collective-permute-start(bf16[128,3456]{1,0:T(8,128)(2,1)S(1)} %get-tuple-element.17), channel_id=1, source_target_pairs={{0,8},{8,0},{16,24},{24,16},{32,40},{40,32},{48,56},{56,48},{64,72... | collective-permute-start | bytes 2654216 | tf_op jit(solution)/shard_map/ppermute | solution.py:256
  41.5 22.8 %all-to-all-start.1 = ((bf16[8,16,3456]{2,1,0:T(8,128)(2,1)}), bf16[8,16,3456]{2,1,0:T(8,128)(2,1)S(1)}, u32[]{:S(2)}, u32[]{:S(2)}) async-start(bf16[8,16,3456]{2,1,0:T(8,128)(2,1)} %bitcast.4), calls=%async_computation.1 | async-start | bytes 1769472 | tf_op jit(solution)/shard_map/all_to_all | solution.py:211
  50.6 5.3 %collective-permute-start.1 = (bf16[256,128]{1,0:T(8,128)(2,1)S(1)}, bf16[256,128]{1,0:T(8,128)(2,1)S(1)}, u32[]{:S(2)}, u32[]{:S(2)}) collective-permute-start(bf16[256,128]{1,0:T(8,128)(2,1)S(1)} %get-tuple-element.13), channel_id=1, source_target_pairs={{1,0},{2,1},{3,2},{4,3},{5,4},{6,5},{7,6},{9,8},{10,9},{11,10},{12... | collective-permute-start | bytes 196616 | tf_op jit(solution)/shard_map/ppermute | solution.py:207
  55.9 8.5 %collective-permute-start.3 = (bf16[2,256,128]{2,1,0:T(8,128)(2,1)S(1)}, bf16[2,256,128]{2,1,0:T(8,128)(2,1)S(1)}, u32[]{:S(2)}, u32[]{:S(2)}) collective-permute-start(bf16[2,256,128]{2,1,0:T(8,128)(2,1)S(1)} %pad_maximum_fusion.own_ref), channel_id=1, source_target_pairs={{8,0},{16,8},{24,16},{32,24},{40,32},{48,40},{56,48},{64,56},{72,6... | collective-permute-start | bytes 393224 | tf_op jit(solution)/shard_map/ppermute | solution.py:207
  88.4 14.3 %all-to-all-start.4 = ((bf16[16,2,3456]{2,1,0:T(2,128)(2,1)}), bf16[16,2,3456]{2,1,0:T(2,128)(2,1)S(1)}, u32[]{:S(2)}, u32[]{:S(2)}) async-start(bf16[16,2,3456]{2,1,0:T(2,128)(2,1)} %shard_map.57), calls=%async_computation.4 | async-start | bytes 442368 | tf_op jit(solution)/shard_map/all_to_all | solution.py:211

commit v9 on v8

--- a/solution.py
+++ b/solution.py
@@ -17,7 +17,11 @@
 
 
 X4, Z4, B2 = range(4), range(4), range(2)
-WIDE = [[slab_of(x, 2 * zh + zl, c) for x in X4 for zl in B2] for zh in Z4 for c in B2]
+WIDE = [
+    [slab_of(x, 2 * zh + zl, c) * 8 + y for x in X4 for zl in B2 for y in range(8)]
+    for zh in Z4
+    for c in B2
+]
 FAR = [[slab_of(x, 2 * zh + zl, c) for zh in Z4] for x in X4 for zl in B2 for c in B2]
 NEAR = [[slab_of(x, 2 * zh + zl, c) for x in X4 for zl in B2 for c in B2] for zh in Z4]
 CORE_PAIRS = [(s, s ^ 1) for s in range(64)]
@@ -266,10 +270,9 @@
     )(core, both, ze, zo, other)
     own = jnp.stack([grad, right])
     upper = shifted_2(own, "slab", -1)
-    tiles = exchange(part.reshape(8, 16, 3456), "slab", WIDE)
+    tiles = exchange(part.reshape(64, 2, 3456), ("slab", "filt"), WIDE)
     tiles, upper = lax.optimization_barrier((tiles, upper))
-    tiles = add_up(tiles, 8)
-    tiles = add_up(exchange(tiles, "filt"), 4)
+    tiles = add_up(tiles, 4)
     tiles = add_up(exchange(tiles, "slab", FAR), 16)
     in_grad = call(
         input_body, shape((2, 2, 128, 256), BF16), [VMEM] * 3, (226 * mb, 3 * mb)

time: 104 us -> 111 us (1.067); the launches traced: 104 us -> 109 us
  waiting for transfers between devices: 17.7 us -> 31.7 us
  blocking collectives: 43.5 us -> 32.4 us
  local copies, waits for them, and re-layouts: 0.99 us -> 2.26 us
    ppermute x3, waiting for transfers between devices: 10.6 us -> 24.6 us  [shifted_2(): lax.ppermute(value, axis, [(source, source + steps) for source in range(f...]
    all_to_all x3 -> x2, blocking collectives: 43.5 us -> 32.4 us  [exchange(): lax.all_to_all(value, axis, split_axis=0, concat_axis=0, axis_index_group...]
    reshape x0 -> x1, local copies, waits for them, and re-layouts: none -> 1.26 us  [on_device(): tiles = exchange(part.reshape(64, 2, 3456), ('slab', 'filt'), WIDE)]
where the time goes in v9:
time: 111 us; the launch traced here: 109 us
  blocking collectives  32.4 us (29%)
  starting transfers between devices  32.4 us (29%)
  waiting for transfers between devices  31.7 us (29%)
  Pallas kernels  9.08 us (8%)
  local copies, waits for them, and re-layouts  2.26 us (2%)
    all_to_all x2, blocking collectives, exchange(): lax.all_to_all(value, axis, split_axis=0, concat_axis=0, axis_index_group...  32.4 us
    ppermute x3, waiting for transfers between devices, shifted_2(): lax.ppermute(value, axis, [(source, source + steps) for source in range(f...  24.6 us
    all_to_all x2, starting transfers between devices, exchange(): lax.all_to_all(value, axis, split_axis=0, concat_axis=0, axis_index_group...  17 us
    ppermute x3, starting transfers between devices, shifted_2(): lax.ppermute(value, axis, [(source, source + steps) for source in range(f...  13.5 us
    all_to_all x2, waiting for transfers between devices, exchange(): lax.all_to_all(value, axis, split_axis=0, concat_axis=0, axis_index_group...  4.74 us
    pallas_call x1, Pallas kernels, on_device(): call(pack_body, shape((8, 7, 16, 256), BF16), [ANY] * 2, (2 * mb, mb), [p...  2.58 us
    ppermute x1, waiting for transfers between devices, on_device(): other = lax.ppermute(part, 'slab', CORE_PAIRS)  2.39 us
  transfers between devices with their start and end apart: 6, of which 5 were waited for; matrix products, arithmetic and copies ran while one was open for 1% of the time, Pallas kernels for 2%

profile of v9, /device:TPU:1, one launch (start us, length us, event | category | flops | bytes accessed | tf_op | source)
XLA Modules:
  0.0 108.6 jit_solution(12645507440435068353)
XLA Ops:
  0.6 2.6 %shard_map.50 = bf16[8,7,16,256]{3,2,1,0:T(8,128)(2,1)} custom-call(bf16[2,16,16,256]{3,2,1,0:T(8,128)(2,1)} %vol_hbm.1, bf16[1,32,8,128]{3,2,1,0:T(8,128)(2,1)} %err_hbm.1), custom_call_target="tpu_custom_call" | custom-call | flops 2097152 | bytes 1048576 | tf_op jit(solution)/shard_map/pallas_call | solution.py:232
  3.2 20.3 %all_to_all.20.rec_ref = bf16[8,7,16,256]{3,2,1,0:T(8,128)(2,1)S(1)} all-to-all(bf16[8,7,16,256]{3,2,1,0:T(8,128)(2,1)} %shard_map.50), channel_id=1, replica_groups=mesh['slab'=64,'filt'=8] {'filt'}, dimensions={0} | all-to-all | bytes 917504 | tf_op jit(solution)/shard_map/all_to_all | solution.py:215
  23.6 8.3 %collective-permute-start = (bf16[8,3,16,256]{3,2,1,0:T(8,128)(2,1)S(1)}, bf16[8,3,16,256]{3,2,1,0:T(8,128)(2,1)S(1)}, u32[]{:S(2)}, u32[]{:S(2)}) collective-permute-start(bf16[8,3,16,256]{3,2,1,0:T(8,128)(2,1)S(1)} %slice.4), channel_id=1, source_target_pairs={{0,8},{8,16},{16,24},{24,32},{32,40},{40,48},{48,56},{56,64},{64,7... | collective-permute-start | bytes 589832 | tf_op jit(solution)/shard_map/ppermute | solution.py:211
  31.9 1.1 shard_map.51
  32.9 1.5 %collective-permute-done.rim_ref = bf16[8,3,16,256]{3,2,1,0:T(8,128)(2,1)S(1)} collective-permute-done((bf16[8,3,16,256]{3,2,1,0:T(8,128)(2,1)S(1)}, bf16[8,3,16,256]{3,2,1,0:T(8,128)(2,1)S(1)}, u32[]{:S(2)}, u32[]{:S(2)}) %collective-permute-start) | collective-permute-done | bytes 196640 | tf_op jit(solution)/shard_map/ppermute | solution.py:211
  34.4 1.4 %shard_map.52 = (bf16[256,128]{1,0:T(8,128)(2,1)S(1)}, bf16[256,256]{1,0:T(8,128)(2,1)S(1)}, bf16[1152,128]{1,0:T(8,128)(2,1)S(1)}, bf16[1152,128]{1,0:T(8,128)(2,1)S(1)}, bf16[128,3456]{1,0:T(8,128)(2,1)S(1)}) custom-call(s32[1]{0:T(128)} %bitcast.core_ref, bf16[8,7,16,256]{3,2,1,0:T(8,128)(2,1)S(1)} %all_to_all.20.rec_ref, ...), custom_call_target="tpu_custom_call" | custom-call | flops 475004928 | bytes 4194304 | tf_op jit(solution)/shard_map/pallas_call | solution.py:253
  35.9 1.9 %collective-permute-start.2 = (bf16[128,3456]{1,0:T(8,128)(2,1)S(1)}, bf16[128,3456]{1,0:T(8,128)(2,1)S(1)}, u32[]{:S(2)}, u32[]{:S(2)}) collective-permute-start(bf16[128,3456]{1,0:T(8,128)(2,1)S(1)} %get-tuple-element.17), channel_id=1, source_target_pairs={{0,8},{8,0},{16,24},{24,16},{32,40},{40,32},{48,56},{56,48},{64,72... | collective-permute-start | bytes 2654216 | tf_op jit(solution)/shard_map/ppermute | solution.py:260
  37.8 2.4 %collective-permute-done.2.other_ref = bf16[128,3456]{1,0:T(8,128)(2,1)S(1)} collective-permute-done((bf16[128,3456]{1,0:T(8,128)(2,1)S(1)}, bf16[128,3456]{1,0:T(8,128)(2,1)S(1)}, u32[]{:S(2)}, u32[]{:S(2)}) %collective-permute-start.2) | collective-permute-done | bytes 884768 | tf_op jit(solution)/shard_map/ppermute | solution.py:260
  40.2 0.9 shard_map.53
  41.2 1.3 %reshape.18 = bf16[64,2,3456]{2,1,0:T(2,128)(2,1)} reshape(bf16[128,3456]{1,0:T(8,128)(2,1)S(1)} %shard_map.53) | data formatting | bytes 1769472 | tf_op jit(solution)/shard_map/reshape | solution.py:273
  42.4 11.4 %all-to-all-start.1 = ((bf16[64,2,3456]{2,1,0:T(2,128)(2,1)}), bf16[64,2,3456]{2,1,0:T(2,128)(2,1)S(1)}, u32[]{:S(2)}, u32[]{:S(2)}) async-start(bf16[64,2,3456]{2,1,0:T(2,128)(2,1)} %reshape.18), calls=%async_computation.1 | async-start | bytes 1769472 | tf_op jit(solution)/shard_map/all_to_all | solution.py:215
  53.8 1.3 %collective-permute-start.1 = (bf16[256,128]{1,0:T(8,128)(2,1)S(1)}, bf16[256,128]{1,0:T(8,128)(2,1)S(1)}, u32[]{:S(2)}, u32[]{:S(2)}) collective-permute-start(bf16[256,128]{1,0:T(8,128)(2,1)S(1)} %get-tuple-element.13), channel_id=1, source_target_pairs={{1,0},{2,1},{3,2},{4,3},{5,4},{6,5},{7,6},{9,8},{10,9},{11,10},{12... | collective-permute-start | bytes 196616 | tf_op jit(solution)/shard_map/ppermute | solution.py:211
  55.1 19.4 %collective-permute-done.1 = bf16[256,128]{1,0:T(8,128)(2,1)S(1)} collective-permute-done((bf16[256,128]{1,0:T(8,128)(2,1)S(1)}, bf16[256,128]{1,0:T(8,128)(2,1)S(1)}, u32[]{:S(2)}, u32[]{:S(2)}) %collective-permute-start.1) | collective-permute-done | bytes 65568 | tf_op jit(solution)/shard_map/ppermute | solution.py:211
  74.6 4.0 %collective-permute-start.3 = (bf16[2,256,128]{2,1,0:T(8,128)(2,1)S(1)}, bf16[2,256,128]{2,1,0:T(8,128)(2,1)S(1)}, u32[]{:S(2)}, u32[]{:S(2)}) collective-permute-start(bf16[2,256,128]{2,1,0:T(8,128)(2,1)S(1)} %pad_maximum_fusion.own_ref), channel_id=1, source_target_pairs={{8,0},{16,8},{24,16},{32,24},{40,32},{48,40},{56,48},{64,56},{72,6... | collective-permute-start | bytes 393224 | tf_op jit(solution)/shard_map/ppermute | solution.py:211
  78.5 3.7 %collective-permute-done.3.up_ref = bf16[2,256,128]{2,1,0:T(8,128)(2,1)S(1)} collective-permute-done((bf16[2,256,128]{2,1,0:T(8,128)(2,1)S(1)}, bf16[2,256,128]{2,1,0:T(8,128)(2,1)S(1)}, u32[]{:S(2)}, u32[]{:S(2)}) %collective-permute-start.3) | collective-permute-done | bytes 131104 | tf_op jit(solution)/shard_map/ppermute | solution.py:211
  82.3 0.0 all-to-all-done.1.in_ref
  82.3 0.2 shard_map.55
  82.4 12.0 %all_to_all.21.in_ref = bf16[4,2,3456]{2,1,0:T(2,128)(2,1)S(1)} all-to-all(bf16[4,2,3456]{2,1,0:T(2,128)(2,1)S(1)} %shard_map.55), channel_id=1, replica_groups={{0,32,64,96},{8,40,72,104},{16,48,80,112},{24,56,88,120},{128,160,192,2..., dimensions={0} | all-to-all | bytes 110592 | tf_op jit(solution)/shard_map/all_to_all | solution.py:215
  94.5 0.7 shard_map.56
  95.2 5.6 %all-to-all-start.3 = ((bf16[16,2,3456]{2,1,0:T(2,128)(2,1)}), bf16[16,2,3456]{2,1,0:T(2,128)(2,1)S(1)}, u32[]{:S(2)}, u32[]{:S(2)}) async-start(bf16[16,2,3456]{2,1,0:T(2,128)(2,1)} %shard_map.56), calls=%async_computation.3 | async-start | bytes 442368 | tf_op jit(solution)/shard_map/all_to_all | solution.py:215
  100.8 1.2 %shard_map.54 = bf16[2,2,128,256]{3,2,1,0:T(8,128)(2,1)S(1)} custom-call(bf16[2,256,128]{2,1,0:T(8,128)(2,1)S(1)} %pad_maximum_fusion.own_ref, bf16[2,256,128]{2,1,0:T(8,128)(2,1)S(1)} %collective-permute-done.3.up_ref, bf16[9,3,128,256]{3,2,1,0:T(8,128)(2,1)S(1)} %bitcast.9), custom_call_target="tpu_custom_call" | custom-call | flops 236978176 | bytes 3145728 | tf_op jit(solution)/shard_map/pallas_call | solution.py:277
  101.9 1.0 copy.5
  102.9 4.7 %all-to-all-done.3.in_ref = bf16[16,2,3456]{2,1,0:T(2,128)(2,1)S(1)} async-done(((bf16[16,2,3456]{2,1,0:T(2,128)(2,1)}), bf16[16,2,3456]{2,1,0:T(2,128)(2,1)S(1)}, u32[]{:S(2)}, u32[]{:S(2)}) %all-to-all-start.3) | async-done | bytes 221216 | tf_op jit(solution)/shard_map/all_to_all | solution.py:215
  107.6 1.0 shard_map.57
  (4 shorter events, 0.0 us)
Async XLA Ops:
  0.6 31.2 %copy-start = (bf16[3,3,3,128,256]{4,3,2,1,0:T(8,128)(2,1)S(1)}, bf16[3,3,3,128,256]{4,3,2,1,0:T(8,128)(2,1)}, u32[]{:S(2)}) copy-start(bf16[3,3,3,128,256]{4,3,2,1,0:T(8,128)(2,1)} %param.4) | copy-start | bytes 5308420
  23.6 10.9 %collective-permute-start = (bf16[8,3,16,256]{3,2,1,0:T(8,128)(2,1)S(1)}, bf16[8,3,16,256]{3,2,1,0:T(8,128)(2,1)S(1)}, u32[]{:S(2)}, u32[]{:S(2)}) collective-permute-start(bf16[8,3,16,256]{3,2,1,0:T(8,128)(2,1)S(1)} %slice.4), channel_id=1, source_target_pairs={{0,8},{8,16},{16,24},{24,32},{32,40},{40,48},{48,56},{56,64},{64,7... | collective-permute-start | bytes 589832 | tf_op jit(solution)/shard_map/ppermute | solution.py:211
  35.9 4.3 %collective-permute-start.2 = (bf16[128,3456]{1,0:T(8,128)(2,1)S(1)}, bf16[128,3456]{1,0:T(8,128)(2,1)S(1)}, u32[]{:S(2)}, u32[]{:S(2)}) collective-permute-start(bf16[128,3456]{1,0:T(8,128)(2,1)S(1)} %get-tuple-element.17), channel_id=1, source_target_pairs={{0,8},{8,0},{16,24},{24,16},{32,40},{40,32},{48,56},{56,48},{64,72... | collective-permute-start | bytes 2654216 | tf_op jit(solution)/shard_map/ppermute | solution.py:260
  42.4 39.8 %all-to-all-start.1 = ((bf16[64,2,3456]{2,1,0:T(2,128)(2,1)}), bf16[64,2,3456]{2,1,0:T(2,128)(2,1)S(1)}, u32[]{:S(2)}, u32[]{:S(2)}) async-start(bf16[64,2,3456]{2,1,0:T(2,128)(2,1)} %reshape.18), calls=%async_computation.1 | async-start | bytes 1769472 | tf_op jit(solution)/shard_map/all_to_all | solution.py:215
  53.8 20.7 %collective-permute-start.1 = (bf16[256,128]{1,0:T(8,128)(2,1)S(1)}, bf16[256,128]{1,0:T(8,128)(2,1)S(1)}, u32[]{:S(2)}, u32[]{:S(2)}) collective-permute-start(bf16[256,128]{1,0:T(8,128)(2,1)S(1)} %get-tuple-element.13), channel_id=1, source_target_pairs={{1,0},{2,1},{3,2},{4,3},{5,4},{6,5},{7,6},{9,8},{10,9},{11,10},{12... | collective-permute-start | bytes 196616 | tf_op jit(solution)/shard_map/ppermute | solution.py:211
  74.6 7.7 %collective-permute-start.3 = (bf16[2,256,128]{2,1,0:T(8,128)(2,1)S(1)}, bf16[2,256,128]{2,1,0:T(8,128)(2,1)S(1)}, u32[]{:S(2)}, u32[]{:S(2)}) collective-permute-start(bf16[2,256,128]{2,1,0:T(8,128)(2,1)S(1)} %pad_maximum_fusion.own_ref), channel_id=1, source_target_pairs={{8,0},{16,8},{24,16},{32,24},{40,32},{48,40},{56,48},{64,56},{72,6... | collective-permute-start | bytes 393224 | tf_op jit(solution)/shard_map/ppermute | solution.py:211
  95.2 12.4 %all-to-all-start.3 = ((bf16[16,2,3456]{2,1,0:T(2,128)(2,1)}), bf16[16,2,3456]{2,1,0:T(2,128)(2,1)S(1)}, u32[]{:S(2)}, u32[]{:S(2)}) async-start(bf16[16,2,3456]{2,1,0:T(2,128)(2,1)} %shard_map.56), calls=%async_computation.3 | async-start | bytes 442368 | tf_op jit(solution)/shard_map/all_to_all | solution.py:215

commit v10 on v8

--- a/solution.py
+++ b/solution.py
@@ -55,25 +55,19 @@
     )
 
 
-def pack_body(vol_hbm, err_hbm, send_hbm, vol_ref, err_ref, send_ref, sems, out_sems):
+def pack_body(vol_hbm, err_hbm, send_ref, vol_ref, err_ref, sems):
     copies = [
-        pltpu.make_async_copy(vol_hbm.at[0], vol_ref.at[0], sems.at[0]),
-        pltpu.make_async_copy(vol_hbm.at[1], vol_ref.at[1], sems.at[1]),
-        pltpu.make_async_copy(err_hbm, err_ref, sems.at[2]),
+        pltpu.make_async_copy(vol_hbm, vol_ref, sems.at[0]),
+        pltpu.make_async_copy(err_hbm, err_ref, sems.at[1]),
     ]
     for copy in copies:
         copy.start()
-    outs = [
-        pltpu.make_async_copy(send_ref.at[:, 0:3], send_hbm.at[:, 0:3], out_sems.at[0]),
-        pltpu.make_async_copy(send_ref.at[:, 3:6], send_hbm.at[:, 3:6], out_sems.at[1]),
-        pltpu.make_async_copy(send_ref.at[:, 6:7], send_hbm.at[:, 6:7], out_sems.at[2]),
-    ]
     i, j = iotas(256, 256)
     row_first = ones_where(j == ((i & 15) << 4) + (i >> 4))
     even_odd = ones_where(i == ((j & 127) << 1) + (j >> 7))
     error_rows = ones_where(j == ((i & 31) << 3) + (i >> 5))
+    copies[0].wait()
     for p in range(2):
-        copies[p].wait()
         plane = vol_ref[p].reshape(256, 256)
         plane = mm(row_first, plane).astype(BF16)
         plane = mm(plane, even_odd).astype(BF16)
@@ -85,16 +79,12 @@
                 else:
                     piece = plane[row * 16 : row * 16 + 16]
                 send_ref[y, p * 3 + b] = piece
-        outs[p].start()
-    copies[2].wait()
+    copies[1].wait()
     error = mm(error_rows, err_ref[0].reshape(256, 128)).astype(BF16)
     for y in range(8):
         for u in range(2):
             start = y * 32 + u * 16
             send_ref[y, 6, :, u * 128 : u * 128 + 128] = error[start : start + 16]
-    outs[2].start()
-    for out in outs:
-        out.wait()
 
 
 def turn_body(w_ref, even_ref, odd_ref):
@@ -180,11 +170,12 @@
                 out_ref[ab * 3 + c, 2 * m : 2 * m + 2] = rows[:, start : start + 128]
 
 
-def input_body(own_ref, up_ref, w_ref, out_ref):
+def input_body(own_ref, right_ref, up_ref, diag_ref, w_ref, out_ref):
     lane = lax.broadcasted_iota(jnp.int32, (128, 128), 1)
     i, j = iotas(256, 256)
     weave = ones_where(j == ((i & 127) << 1) + (i >> 7))
-    taps = ((( 1, 0),), ((2, 0), (0, 1)))
+    taps = (((1, 0),), ((2, 0), (0, 1)))
+    grads = ((own_ref[...], right_ref[...]), (up_ref[...], diag_ref[...]))
     for ed in range(2):
         for er in range(2):
             sums = []
@@ -192,8 +183,7 @@
                 total = None
                 for a, od in taps[ed]:
                     for b, pd in taps[er]:
-                        grad = (up_ref if od else own_ref)[pd]
-                        term = mm(w_ref[a * 3 + b, c], grad)
+                        term = mm(w_ref[a * 3 + b, c], grads[od][pd])
                         total = term if total is None else total + term
                 sums.append(total)
             nxt = jnp.where(lane == 127, 0.0, pltpu.roll(sums[0], 127, 1))
@@ -233,12 +223,9 @@
         [
             pltpu.VMEM(volume.shape, BF16),
             pltpu.VMEM(out_error.shape, BF16),
-            pltpu.VMEM((8, 7, 16, 256), BF16),
-            pltpu.SemaphoreType.DMA((3,)),
-            pltpu.SemaphoreType.DMA((3,)),
+            pltpu.SemaphoreType.DMA((2,)),
         ],
         62500000,
-        ANY,
     )(volume, out_error)
     received = exchange(send, "filt")
     even, odd = call(
@@ -264,16 +251,20 @@
         LIMIT,
         ANY,
     )(core, both, ze, zo, other)
-    own = jnp.stack([grad, right])
-    upper = shifted_2(own, "slab", -1)
+    upper = shifted_2(grad, "slab", -1)
+    diagonal = lax.ppermute(
+        grad,
+        ("slab", "filt"),
+        [(8 * s + y, 8 * s + y - 9) for s in range(1, 64) for y in range(1, 8)],
+    )
     tiles = exchange(part.reshape(8, 16, 3456), "slab", WIDE)
-    tiles, upper = lax.optimization_barrier((tiles, upper))
+    tiles, right, upper, diagonal = lax.optimization_barrier((tiles, right, upper, diagonal))
     tiles = add_up(tiles, 8)
     tiles = add_up(exchange(tiles, "filt"), 4)
     tiles = add_up(exchange(tiles, "slab", FAR), 16)
     in_grad = call(
-        input_body, shape((2, 2, 128, 256), BF16), [VMEM] * 3, (226 * mb, 3 * mb)
-    )(own, upper, taps)
+        input_body, shape((2, 2, 128, 256), BF16), [VMEM] * 5, (226 * mb, 3 * mb)
+    )(grad, right, upper, diagonal, taps)
     in_grad = in_grad.transpose(0, 2, 1, 3)
 
     tiles = exchange(tiles, "slab", NEAR)

time: 104 us -> 105 us (level)
    ppermute x3, waiting for transfers between devices: 10.6 us -> 7.98 us  [shifted_2(): lax.ppermute(value, axis, [(source, source + steps) for source in range(f...]
    ppermute x0 -> x1, waiting for transfers between devices: none -> 1.85 us  [on_device(): lax.ppermute(grad, ('slab', 'filt'), [(8 * s + y, 8 * s + y - 9) for s in...]
    ppermute x0 -> x1, starting transfers between devices: none -> 1.28 us  [on_device(): lax.ppermute(grad, ('slab', 'filt'), [(8 * s + y, 8 * s + y - 9) for s in...]
  transfers between devices with their start and end apart: 6 -> 7, of which waited for: 5 -> 6; matrix products, arithmetic and copies ran while one was open for 1% -> 1% of each run, Pallas kernels for 2% -> 2%
where the time goes in v10:
time: 105 us; the launch traced here: 104 us
  blocking collectives  43.5 us (41%)
  starting transfers between devices  31.8 us (30%)
  waiting for transfers between devices  17.5 us (17%)
  Pallas kernels  9.34 us (9%)
    all_to_all x3, blocking collectives, exchange(): lax.all_to_all(value, axis, split_axis=0, concat_axis=0, axis_index_group...  43.5 us
    all_to_all x2, starting transfers between devices, exchange(): lax.all_to_all(value, axis, split_axis=0, concat_axis=0, axis_index_group...  16.5 us
    ppermute x3, starting transfers between devices, shifted_2(): lax.ppermute(value, axis, [(source, source + steps) for source in range(f...  12.1 us
    ppermute x3, waiting for transfers between devices, shifted_2(): lax.ppermute(value, axis, [(source, source + steps) for source in range(f...  7.98 us
    all_to_all x2, waiting for transfers between devices, exchange(): lax.all_to_all(value, axis, split_axis=0, concat_axis=0, axis_index_group...  5.3 us
    pallas_call x1, Pallas kernels, on_device(): call(pack_body, shape((8, 7, 16, 256), BF16), [ANY] * 2, (2 * mb, mb), [p...  2.48 us
    ppermute x1, waiting for transfers between devices, on_device(): other = lax.ppermute(part, 'slab', CORE_PAIRS)  2.39 us
  transfers between devices with their start and end apart: 7, of which 6 were waited for; matrix products, arithmetic and copies ran while one was open for 1% of the time, Pallas kernels for 2%

profile of v10, /device:TPU:1, one launch (start us, length us, event | category | flops | bytes accessed | tf_op | source)
XLA Modules:
  0.0 104.0 jit_solution(5260098913444154301)
XLA Ops:
  0.6 2.5 %shard_map.50 = bf16[8,7,16,256]{3,2,1,0:T(8,128)(2,1)} custom-call(bf16[2,16,16,256]{3,2,1,0:T(8,128)(2,1)} %vol_hbm.1, bf16[1,32,8,128]{3,2,1,0:T(8,128)(2,1)} %err_hbm.1), custom_call_target="tpu_custom_call" | custom-call | flops 2097152 | bytes 1048576 | tf_op jit(solution)/shard_map/pallas_call | solution.py:218
  3.1 20.3 %all_to_all.25.rec_ref = bf16[8,7,16,256]{3,2,1,0:T(8,128)(2,1)S(1)} all-to-all(bf16[8,7,16,256]{3,2,1,0:T(8,128)(2,1)} %shard_map.50), channel_id=1, replica_groups=mesh['slab'=64,'filt'=8] {'filt'}, dimensions={0} | all-to-all | bytes 917504 | tf_op jit(solution)/shard_map/all_to_all | solution.py:201
  23.5 8.3 %collective-permute-start = (bf16[8,3,16,256]{3,2,1,0:T(8,128)(2,1)S(1)}, bf16[8,3,16,256]{3,2,1,0:T(8,128)(2,1)S(1)}, u32[]{:S(2)}, u32[]{:S(2)}) collective-permute-start(bf16[8,3,16,256]{3,2,1,0:T(8,128)(2,1)S(1)} %slice.4), channel_id=1, source_target_pairs={{0,8},{8,16},{16,24},{24,32},{32,40},{40,48},{48,56},{56,64},{64,7... | collective-permute-start | bytes 589832 | tf_op jit(solution)/shard_map/ppermute | solution.py:197
  31.8 1.1 %shard_map.51 = (bf16[256,1152]{1,0:T(8,128)(2,1)S(1)}, bf16[512,1152]{1,0:T(8,128)(2,1)S(1)}) custom-call(bf16[9,3,128,256]{3,2,1,0:T(8,128)(2,1)S(1)} %bitcast.7), custom_call_target="tpu_custom_call" | custom-call | flops 473956352 | bytes 4194304 | tf_op jit(solution)/shard_map/pallas_call | solution.py:231
  32.8 1.5 %collective-permute-done.rim_ref = bf16[8,3,16,256]{3,2,1,0:T(8,128)(2,1)S(1)} collective-permute-done((bf16[8,3,16,256]{3,2,1,0:T(8,128)(2,1)S(1)}, bf16[8,3,16,256]{3,2,1,0:T(8,128)(2,1)S(1)}, u32[]{:S(2)}, u32[]{:S(2)}) %collective-permute-start) | collective-permute-done | bytes 196640 | tf_op jit(solution)/shard_map/ppermute | solution.py:197
  34.3 1.4 %shard_map.52 = (bf16[256,128]{1,0:T(8,128)(2,1)S(1)}, bf16[256,256]{1,0:T(8,128)(2,1)S(1)}, bf16[1152,128]{1,0:T(8,128)(2,1)S(1)}, bf16[1152,128]{1,0:T(8,128)(2,1)S(1)}, bf16[128,3456]{1,0:T(8,128)(2,1)S(1)}) custom-call(s32[1]{0:T(128)} %bitcast.core_ref, bf16[8,7,16,256]{3,2,1,0:T(8,128)(2,1)S(1)} %all_to_all.25.rec_ref, ...), custom_call_target="tpu_custom_call" | custom-call | flops 475004928 | bytes 4194304 | tf_op jit(solution)/shard_map/pallas_call | solution.py:236
  35.8 1.9 %collective-permute-start.1 = (bf16[128,3456]{1,0:T(8,128)(2,1)S(1)}, bf16[128,3456]{1,0:T(8,128)(2,1)S(1)}, u32[]{:S(2)}, u32[]{:S(2)}) collective-permute-start(bf16[128,3456]{1,0:T(8,128)(2,1)S(1)} %get-tuple-element.19), channel_id=1, source_target_pairs={{0,8},{8,0},{16,24},{24,16},{32,40},{40,32},{48,56},{56,48},{64,72... | collective-permute-start | bytes 2654216 | tf_op jit(solution)/shard_map/ppermute | solution.py:243
  37.7 2.4 %collective-permute-done.1.other_ref = bf16[128,3456]{1,0:T(8,128)(2,1)S(1)} collective-permute-done((bf16[128,3456]{1,0:T(8,128)(2,1)S(1)}, bf16[128,3456]{1,0:T(8,128)(2,1)S(1)}, u32[]{:S(2)}, u32[]{:S(2)}) %collective-permute-start.1) | collective-permute-done | bytes 884768 | tf_op jit(solution)/shard_map/ppermute | solution.py:243
  40.1 1.3 %shard_map.53 = bf16[128,3456]{1,0:T(8,128)(2,1)} custom-call(s32[1]{0:T(128)} %bitcast.core_ref, bf16[256,256]{1,0:T(8,128)(2,1)S(1)} %get-tuple-element.16.both_ref, bf16[1152,128]{1,0:T(8,128)(2,1)S(1)} %get-tuple-element.17.ze, bf16[1152,128]{1,0:T(8,128)(2,1)S(1)} %get-tuple-element.18.zo, bf16[128,3456]{1,0:T(8,128)(2,1)S(1)} %collective-permute-done.1.other_ref), custom_call_target="tpu_custom_call" | custom-call | flops 118489088 | bytes 3145728 | tf_op jit(solution)/shard_map/pallas_call | solution.py:245
  41.4 9.1 %all-to-all-start.1 = ((bf16[8,16,3456]{2,1,0:T(8,128)(2,1)}), bf16[8,16,3456]{2,1,0:T(8,128)(2,1)S(1)}, u32[]{:S(2)}, u32[]{:S(2)}) async-start(bf16[8,16,3456]{2,1,0:T(8,128)(2,1)} %bitcast.2), calls=%async_computation.1 | async-start | bytes 1769472 | tf_op jit(solution)/shard_map/all_to_all | solution.py:201
  50.5 1.3 %collective-permute-start.4 = (bf16[256,128]{1,0:T(8,128)(2,1)S(1)}, bf16[256,128]{1,0:T(8,128)(2,1)S(1)}, u32[]{:S(2)}, u32[]{:S(2)}) collective-permute-start(bf16[256,128]{1,0:T(8,128)(2,1)S(1)} %get-tuple-element.15.own_ref), channel_id=1, source_target_pairs={{9,0},{10,1},{11,2},{12,3},{13,4},{14,5},{15,6},{17,8},{18,9},{19,... | collective-permute-start | bytes 196616 | tf_op jit(solution)/shard_map/ppermute | solution.py:255
  51.8 2.6 %collective-permute-start.3 = (bf16[256,128]{1,0:T(8,128)(2,1)S(1)}, bf16[256,128]{1,0:T(8,128)(2,1)S(1)}, u32[]{:S(2)}, u32[]{:S(2)}) collective-permute-start(bf16[256,128]{1,0:T(8,128)(2,1)S(1)} %get-tuple-element.15.own_ref), channel_id=1, source_target_pairs={{8,0},{16,8},{24,16},{32,24},{40,32},{48,40},{56,48},{64,56},{72,6... | collective-permute-start | bytes 196616 | tf_op jit(solution)/shard_map/ppermute | solution.py:197
  54.4 1.3 %collective-permute-start.2 = (bf16[256,128]{1,0:T(8,128)(2,1)S(1)}, bf16[256,128]{1,0:T(8,128)(2,1)S(1)}, u32[]{:S(2)}, u32[]{:S(2)}) collective-permute-start(bf16[256,128]{1,0:T(8,128)(2,1)S(1)} %get-tuple-element.15.own_ref), channel_id=1, source_target_pairs={{1,0},{2,1},{3,2},{4,3},{5,4},{6,5},{7,6},{9,8},{10,9},{11,10},{12... | collective-permute-start | bytes 196616 | tf_op jit(solution)/shard_map/ppermute | solution.py:197
  55.7 1.9 %collective-permute-done.4.diag_ref = bf16[256,128]{1,0:T(8,128)(2,1)S(1)} collective-permute-done((bf16[256,128]{1,0:T(8,128)(2,1)S(1)}, bf16[256,128]{1,0:T(8,128)(2,1)S(1)}, u32[]{:S(2)}, u32[]{:S(2)}) %collective-permute-start.4) | collective-permute-done | bytes 65568 | tf_op jit(solution)/shard_map/ppermute | solution.py:255
  57.5 6.5 %collective-permute-done.3.up_ref = bf16[256,128]{1,0:T(8,128)(2,1)S(1)} collective-permute-done((bf16[256,128]{1,0:T(8,128)(2,1)S(1)}, bf16[256,128]{1,0:T(8,128)(2,1)S(1)}, u32[]{:S(2)}, u32[]{:S(2)}) %collective-permute-start.3) | collective-permute-done | bytes 65568 | tf_op jit(solution)/shard_map/ppermute | solution.py:197
  64.0 0.6 all-to-all-done.1.in_ref
  64.7 10.4 %all_to_all.26.in_ref = bf16[8,2,3456]{2,1,0:T(2,128)(2,1)S(1)} all-to-all(bf16[8,2,3456]{2,1,0:T(2,128)(2,1)S(1)} %shard_map.55), channel_id=1, replica_groups=mesh['slab'=64,'filt'=8] {'filt'}, dimensions={0} | all-to-all | bytes 221184 | tf_op jit(solution)/shard_map/all_to_all | solution.py:201
  75.2 12.8 %all_to_all.27.in_ref = bf16[4,2,3456]{2,1,0:T(2,128)(2,1)S(1)} all-to-all(bf16[4,2,3456]{2,1,0:T(2,128)(2,1)S(1)} %shard_map.56), channel_id=1, replica_groups={{0,32,64,96},{8,40,72,104},{16,48,80,112},{24,56,88,120},{128,160,192,2..., dimensions={0} | all-to-all | bytes 110592 | tf_op jit(solution)/shard_map/all_to_all | solution.py:201
  88.0 0.7 shard_map.57
  88.7 7.5 %all-to-all-start.4 = ((bf16[16,2,3456]{2,1,0:T(2,128)(2,1)}), bf16[16,2,3456]{2,1,0:T(2,128)(2,1)S(1)}, u32[]{:S(2)}, u32[]{:S(2)}) async-start(bf16[16,2,3456]{2,1,0:T(2,128)(2,1)} %shard_map.57), calls=%async_computation.4 | async-start | bytes 442368 | tf_op jit(solution)/shard_map/all_to_all | solution.py:201
  96.1 1.2 %shard_map.54 = bf16[2,2,128,256]{3,2,1,0:T(8,128)(2,1)S(1)} custom-call(bf16[256,128]{1,0:T(8,128)(2,1)S(1)} %get-tuple-element.15.own_ref, bf16[256,128]{1,0:T(8,128)(2,1)S(1)} %collective-permute-done.2.right_ref, bf16[256,128]{1,0:T(8,128)(2,1)S(1)} %collective-permute-done.3.up_ref, bf16[256,128]{1,0:T(8,128)(2,1)S(1)} %collective-permute-done.4.diag_ref, ...), custom_call_target="tpu_custom_call" | custom-call | flops 236978176 | bytes 3145728 | tf_op jit(solution)/shard_map/pallas_call | solution.py:265
  97.3 1.0 copy.5
  98.3 4.7 %all-to-all-done.4.in_ref = bf16[16,2,3456]{2,1,0:T(2,128)(2,1)S(1)} async-done(((bf16[16,2,3456]{2,1,0:T(2,128)(2,1)}), bf16[16,2,3456]{2,1,0:T(2,128)(2,1)S(1)}, u32[]{:S(2)}, u32[]{:S(2)}) %all-to-all-start.4) | async-done | bytes 221216 | tf_op jit(solution)/shard_map/all_to_all | solution.py:201
  103.0 1.0 shard_map.58
  (6 shorter events, 0.2 us)
Async XLA Ops:
  0.6 31.1 %copy-start = (bf16[3,3,3,128,256]{4,3,2,1,0:T(8,128)(2,1)S(1)}, bf16[3,3,3,128,256]{4,3,2,1,0:T(8,128)(2,1)}, u32[]{:S(2)}) copy-start(bf16[3,3,3,128,256]{4,3,2,1,0:T(8,128)(2,1)} %param.4) | copy-start | bytes 5308420
  23.5 10.9 %collective-permute-start = (bf16[8,3,16,256]{3,2,1,0:T(8,128)(2,1)S(1)}, bf16[8,3,16,256]{3,2,1,0:T(8,128)(2,1)S(1)}, u32[]{:S(2)}, u32[]{:S(2)}) collective-permute-start(bf16[8,3,16,256]{3,2,1,0:T(8,128)(2,1)S(1)} %slice.4), channel_id=1, source_target_pairs={{0,8},{8,16},{16,24},{24,32},{32,40},{40,48},{48,56},{56,64},{64,7... | collective-permute-start | bytes 589832 | tf_op jit(solution)/shard_map/ppermute | solution.py:197
  35.8 4.3 %collective-permute-start.1 = (bf16[128,3456]{1,0:T(8,128)(2,1)S(1)}, bf16[128,3456]{1,0:T(8,128)(2,1)S(1)}, u32[]{:S(2)}, u32[]{:S(2)}) collective-permute-start(bf16[128,3456]{1,0:T(8,128)(2,1)S(1)} %get-tuple-element.19), channel_id=1, source_target_pairs={{0,8},{8,0},{16,24},{24,16},{32,40},{40,32},{48,56},{56,48},{64,72... | collective-permute-start | bytes 2654216 | tf_op jit(solution)/shard_map/ppermute | solution.py:243
  41.4 23.1 %all-to-all-start.1 = ((bf16[8,16,3456]{2,1,0:T(8,128)(2,1)}), bf16[8,16,3456]{2,1,0:T(8,128)(2,1)S(1)}, u32[]{:S(2)}, u32[]{:S(2)}) async-start(bf16[8,16,3456]{2,1,0:T(8,128)(2,1)} %bitcast.2), calls=%async_computation.1 | async-start | bytes 1769472 | tf_op jit(solution)/shard_map/all_to_all | solution.py:201
  50.5 7.0 %collective-permute-start.4 = (bf16[256,128]{1,0:T(8,128)(2,1)S(1)}, bf16[256,128]{1,0:T(8,128)(2,1)S(1)}, u32[]{:S(2)}, u32[]{:S(2)}) collective-permute-start(bf16[256,128]{1,0:T(8,128)(2,1)S(1)} %get-tuple-element.15.own_ref), channel_id=1, source_target_pairs={{9,0},{10,1},{11,2},{12,3},{13,4},{14,5},{15,6},{17,8},{18,9},{19,... | collective-permute-start | bytes 196616 | tf_op jit(solution)/shard_map/ppermute | solution.py:255
  51.8 12.2 %collective-permute-start.3 = (bf16[256,128]{1,0:T(8,128)(2,1)S(1)}, bf16[256,128]{1,0:T(8,128)(2,1)S(1)}, u32[]{:S(2)}, u32[]{:S(2)}) collective-permute-start(bf16[256,128]{1,0:T(8,128)(2,1)S(1)} %get-tuple-element.15.own_ref), channel_id=1, source_target_pairs={{8,0},{16,8},{24,16},{32,24},{40,32},{48,40},{56,48},{64,56},{72,6... | collective-permute-start | bytes 196616 | tf_op jit(solution)/shard_map/ppermute | solution.py:197
  54.4 9.6 %collective-permute-start.2 = (bf16[256,128]{1,0:T(8,128)(2,1)S(1)}, bf16[256,128]{1,0:T(8,128)(2,1)S(1)}, u32[]{:S(2)}, u32[]{:S(2)}) collective-permute-start(bf16[256,128]{1,0:T(8,128)(2,1)S(1)} %get-tuple-element.15.own_ref), channel_id=1, source_target_pairs={{1,0},{2,1},{3,2},{4,3},{5,4},{6,5},{7,6},{9,8},{10,9},{11,10},{12... | collective-permute-start | bytes 196616 | tf_op jit(solution)/shard_map/ppermute | solution.py:197
  88.7 14.3 %all-to-all-start.4 = ((bf16[16,2,3456]{2,1,0:T(2,128)(2,1)}), bf16[16,2,3456]{2,1,0:T(2,128)(2,1)S(1)}, u32[]{:S(2)}, u32[]{:S(2)}) async-start(bf16[16,2,3456]{2,1,0:T(2,128)(2,1)} %shard_map.57), calls=%async_computation.4 | async-start | bytes 442368 | tf_op jit(solution)/shard_map/all_to_all | solution.py:201

commit v11 on v10

--- a/solution.py
+++ b/solution.py
@@ -18,7 +18,12 @@
 
 X4, Z4, B2 = range(4), range(4), range(2)
 WIDE = [[slab_of(x, 2 * zh + zl, c) for x in X4 for zl in B2] for zh in Z4 for c in B2]
-FAR = [[slab_of(x, 2 * zh + zl, c) for zh in Z4] for x in X4 for zl in B2 for c in B2]
+FAR = [
+    [slab_of(x, 2 * zh + zl, c) * 8 + y for zh in Z4 for y in range(8)]
+    for x in X4
+    for zl in B2
+    for c in B2
+]
 NEAR = [[slab_of(x, 2 * zh + zl, c) for x in X4 for zl in B2 for c in B2] for zh in Z4]
 CORE_PAIRS = [(s, s ^ 1) for s in range(64)]
 
@@ -157,8 +162,8 @@
     for n in range(1, in_ref.shape[0]):
         total = total + in_ref[n].astype(F32)
     for n in range(out_ref.shape[0]):
-        rows = total if total.shape[0] == 2 else total[2 * n : 2 * n + 2]
-        out_ref[n] = rows.astype(BF16)
+        start = 2 * n % total.shape[0]
+        out_ref[n] = total[start : start + 2].astype(BF16)
 
 
 def last_body(in_ref, out_ref):
@@ -259,9 +264,8 @@
     )
     tiles = exchange(part.reshape(8, 16, 3456), "slab", WIDE)
     tiles, right, upper, diagonal = lax.optimization_barrier((tiles, right, upper, diagonal))
-    tiles = add_up(tiles, 8)
-    tiles = add_up(exchange(tiles, "filt"), 4)
-    tiles = add_up(exchange(tiles, "slab", FAR), 16)
+    tiles = add_up(tiles, 32)
+    tiles = add_up(exchange(tiles, ("slab", "filt"), FAR), 16)
     in_grad = call(
         input_body, shape((2, 2, 128, 256), BF16), [VMEM] * 5, (226 * mb, 3 * mb)
     )(grad, right, upper, diagonal, taps)

time: 105 us -> 103 us (0.981)
  blocking collectives: 43.5 us -> 40.7 us
  starting transfers between devices: 31.8 us -> 33.2 us
    all_to_all x3 -> x2, blocking collectives: 43.5 us -> 40.7 us  [exchange(): lax.all_to_all(value, axis, split_axis=0, concat_axis=0, axis_index_group...]
    all_to_all x2, starting transfers between devices: 16.5 us -> 17.8 us  [exchange(): lax.all_to_all(value, axis, split_axis=0, concat_axis=0, axis_index_group...]
where the time goes in v11:
time: 103 us; the launch traced here: 102 us
  blocking collectives  40.7 us (40%)
  starting transfers between devices  33.2 us (32%)
  waiting for transfers between devices  17.5 us (17%)
  Pallas kernels  9.38 us (9%)
    all_to_all x2, blocking collectives, exchange(): lax.all_to_all(value, axis, split_axis=0, concat_axis=0, axis_index_group...  40.7 us
    all_to_all x2, starting transfers between devices, exchange(): lax.all_to_all(value, axis, split_axis=0, concat_axis=0, axis_index_group...  17.8 us
    ppermute x3, starting transfers between devices, shifted_2(): lax.ppermute(value, axis, [(source, source + steps) for source in range(f...  12.1 us
    ppermute x3, waiting for transfers between devices, shifted_2(): lax.ppermute(value, axis, [(source, source + steps) for source in range(f...  7.98 us
    all_to_all x2, waiting for transfers between devices, exchange(): lax.all_to_all(value, axis, split_axis=0, concat_axis=0, axis_index_group...  5.3 us
    pallas_call x1, Pallas kernels, on_device(): call(pack_body, shape((8, 7, 16, 256), BF16), [ANY] * 2, (2 * mb, mb), [p...  2.48 us
    ppermute x1, waiting for transfers between devices, on_device(): other = lax.ppermute(part, 'slab', CORE_PAIRS)  2.39 us
  transfers between devices with their start and end apart: 7, of which 6 were waited for; matrix products, arithmetic and copies ran while one was open for 1% of the time, Pallas kernels for 2%

profile of v11, /device:TPU:1, one launch (start us, length us, event | category | flops | bytes accessed | tf_op | source)
XLA Modules:
  0.0 102.5 jit_solution(15222878978219823368)
XLA Ops:
  0.6 2.5 %shard_map.50 = bf16[8,7,16,256]{3,2,1,0:T(8,128)(2,1)} custom-call(bf16[2,16,16,256]{3,2,1,0:T(8,128)(2,1)} %vol_hbm.1, bf16[1,32,8,128]{3,2,1,0:T(8,128)(2,1)} %err_hbm.1), custom_call_target="tpu_custom_call" | custom-call | flops 2097152 | bytes 1048576 | tf_op jit(solution)/shard_map/pallas_call | solution.py:223
  3.1 20.3 %all_to_all.20.rec_ref = bf16[8,7,16,256]{3,2,1,0:T(8,128)(2,1)S(1)} all-to-all(bf16[8,7,16,256]{3,2,1,0:T(8,128)(2,1)} %shard_map.50), channel_id=1, replica_groups=mesh['slab'=64,'filt'=8] {'filt'}, dimensions={0} | all-to-all | bytes 917504 | tf_op jit(solution)/shard_map/all_to_all | solution.py:206
  23.5 8.3 %collective-permute-start = (bf16[8,3,16,256]{3,2,1,0:T(8,128)(2,1)S(1)}, bf16[8,3,16,256]{3,2,1,0:T(8,128)(2,1)S(1)}, u32[]{:S(2)}, u32[]{:S(2)}) collective-permute-start(bf16[8,3,16,256]{3,2,1,0:T(8,128)(2,1)S(1)} %slice.4), channel_id=1, source_target_pairs={{0,8},{8,16},{16,24},{24,32},{32,40},{40,48},{48,56},{56,64},{64,7... | collective-permute-start | bytes 589832 | tf_op jit(solution)/shard_map/ppermute | solution.py:202
  31.8 1.1 %shard_map.51 = (bf16[256,1152]{1,0:T(8,128)(2,1)S(1)}, bf16[512,1152]{1,0:T(8,128)(2,1)S(1)}) custom-call(bf16[9,3,128,256]{3,2,1,0:T(8,128)(2,1)S(1)} %bitcast.7), custom_call_target="tpu_custom_call" | custom-call | flops 473956352 | bytes 4194304 | tf_op jit(solution)/shard_map/pallas_call | solution.py:236
  32.8 1.5 %collective-permute-done.rim_ref = bf16[8,3,16,256]{3,2,1,0:T(8,128)(2,1)S(1)} collective-permute-done((bf16[8,3,16,256]{3,2,1,0:T(8,128)(2,1)S(1)}, bf16[8,3,16,256]{3,2,1,0:T(8,128)(2,1)S(1)}, u32[]{:S(2)}, u32[]{:S(2)}) %collective-permute-start) | collective-permute-done | bytes 196640 | tf_op jit(solution)/shard_map/ppermute | solution.py:202
  34.3 1.4 %shard_map.52 = (bf16[256,128]{1,0:T(8,128)(2,1)S(1)}, bf16[256,256]{1,0:T(8,128)(2,1)S(1)}, bf16[1152,128]{1,0:T(8,128)(2,1)S(1)}, bf16[1152,128]{1,0:T(8,128)(2,1)S(1)}, bf16[128,3456]{1,0:T(8,128)(2,1)S(1)}) custom-call(s32[1]{0:T(128)} %bitcast.core_ref, bf16[8,7,16,256]{3,2,1,0:T(8,128)(2,1)S(1)} %all_to_all.20.rec_ref, ...), custom_call_target="tpu_custom_call" | custom-call | flops 475004928 | bytes 4194304 | tf_op jit(solution)/shard_map/pallas_call | solution.py:241
  35.8 1.9 %collective-permute-start.1 = (bf16[128,3456]{1,0:T(8,128)(2,1)S(1)}, bf16[128,3456]{1,0:T(8,128)(2,1)S(1)}, u32[]{:S(2)}, u32[]{:S(2)}) collective-permute-start(bf16[128,3456]{1,0:T(8,128)(2,1)S(1)} %get-tuple-element.19), channel_id=1, source_target_pairs={{0,8},{8,0},{16,24},{24,16},{32,40},{40,32},{48,56},{56,48},{64,72... | collective-permute-start | bytes 2654216 | tf_op jit(solution)/shard_map/ppermute | solution.py:248
  37.7 2.4 %collective-permute-done.1.other_ref = bf16[128,3456]{1,0:T(8,128)(2,1)S(1)} collective-permute-done((bf16[128,3456]{1,0:T(8,128)(2,1)S(1)}, bf16[128,3456]{1,0:T(8,128)(2,1)S(1)}, u32[]{:S(2)}, u32[]{:S(2)}) %collective-permute-start.1) | collective-permute-done | bytes 884768 | tf_op jit(solution)/shard_map/ppermute | solution.py:248
  40.1 1.3 %shard_map.53 = bf16[128,3456]{1,0:T(8,128)(2,1)} custom-call(s32[1]{0:T(128)} %bitcast.core_ref, bf16[256,256]{1,0:T(8,128)(2,1)S(1)} %get-tuple-element.16.both_ref, bf16[1152,128]{1,0:T(8,128)(2,1)S(1)} %get-tuple-element.17.ze, bf16[1152,128]{1,0:T(8,128)(2,1)S(1)} %get-tuple-element.18.zo, bf16[128,3456]{1,0:T(8,128)(2,1)S(1)} %collective-permute-done.1.other_ref), custom_call_target="tpu_custom_call" | custom-call | flops 118489088 | bytes 3145728 | tf_op jit(solution)/shard_map/pallas_call | solution.py:250
  41.4 9.1 %all-to-all-start.1 = ((bf16[8,16,3456]{2,1,0:T(8,128)(2,1)}), bf16[8,16,3456]{2,1,0:T(8,128)(2,1)S(1)}, u32[]{:S(2)}, u32[]{:S(2)}) async-start(bf16[8,16,3456]{2,1,0:T(8,128)(2,1)} %bitcast.2), calls=%async_computation.1 | async-start | bytes 1769472 | tf_op jit(solution)/shard_map/all_to_all | solution.py:206
  50.5 1.3 %collective-permute-start.4 = (bf16[256,128]{1,0:T(8,128)(2,1)S(1)}, bf16[256,128]{1,0:T(8,128)(2,1)S(1)}, u32[]{:S(2)}, u32[]{:S(2)}) collective-permute-start(bf16[256,128]{1,0:T(8,128)(2,1)S(1)} %get-tuple-element.15.own_ref), channel_id=1, source_target_pairs={{9,0},{10,1},{11,2},{12,3},{13,4},{14,5},{15,6},{17,8},{18,9},{19,... | collective-permute-start | bytes 196616 | tf_op jit(solution)/shard_map/ppermute | solution.py:260
  51.8 2.6 %collective-permute-start.3 = (bf16[256,128]{1,0:T(8,128)(2,1)S(1)}, bf16[256,128]{1,0:T(8,128)(2,1)S(1)}, u32[]{:S(2)}, u32[]{:S(2)}) collective-permute-start(bf16[256,128]{1,0:T(8,128)(2,1)S(1)} %get-tuple-element.15.own_ref), channel_id=1, source_target_pairs={{8,0},{16,8},{24,16},{32,24},{40,32},{48,40},{56,48},{64,56},{72,6... | collective-permute-start | bytes 196616 | tf_op jit(solution)/shard_map/ppermute | solution.py:202
  54.4 1.3 %collective-permute-start.2 = (bf16[256,128]{1,0:T(8,128)(2,1)S(1)}, bf16[256,128]{1,0:T(8,128)(2,1)S(1)}, u32[]{:S(2)}, u32[]{:S(2)}) collective-permute-start(bf16[256,128]{1,0:T(8,128)(2,1)S(1)} %get-tuple-element.15.own_ref), channel_id=1, source_target_pairs={{1,0},{2,1},{3,2},{4,3},{5,4},{6,5},{7,6},{9,8},{10,9},{11,10},{12... | collective-permute-start | bytes 196616 | tf_op jit(solution)/shard_map/ppermute | solution.py:202
  55.7 1.9 %collective-permute-done.4.diag_ref = bf16[256,128]{1,0:T(8,128)(2,1)S(1)} collective-permute-done((bf16[256,128]{1,0:T(8,128)(2,1)S(1)}, bf16[256,128]{1,0:T(8,128)(2,1)S(1)}, u32[]{:S(2)}, u32[]{:S(2)}) %collective-permute-start.4) | collective-permute-done | bytes 65568 | tf_op jit(solution)/shard_map/ppermute | solution.py:260
  57.5 6.5 %collective-permute-done.3.up_ref = bf16[256,128]{1,0:T(8,128)(2,1)S(1)} collective-permute-done((bf16[256,128]{1,0:T(8,128)(2,1)S(1)}, bf16[256,128]{1,0:T(8,128)(2,1)S(1)}, u32[]{:S(2)}, u32[]{:S(2)}) %collective-permute-start.3) | collective-permute-done | bytes 65568 | tf_op jit(solution)/shard_map/ppermute | solution.py:202
  64.0 0.6 all-to-all-done.1.in_ref
  64.6 0.1 shard_map.55
  64.7 20.4 %all_to_all.21.in_ref = bf16[32,2,3456]{2,1,0:T(2,128)(2,1)S(1)} all-to-all(bf16[32,2,3456]{2,1,0:T(2,128)(2,1)S(1)} %shard_map.55), channel_id=1, replica_groups={{0,1,2,3,4,5,6,7,32,33,34,35,36,37,38,39,64,65,66,67,68,69,70,71,96,97,..., dimensions={0} | all-to-all | bytes 884736 | tf_op jit(solution)/shard_map/all_to_all | solution.py:206
  85.1 0.8 shard_map.56
  85.9 8.8 %all-to-all-start.3 = ((bf16[16,2,3456]{2,1,0:T(2,128)(2,1)}), bf16[16,2,3456]{2,1,0:T(2,128)(2,1)S(1)}, u32[]{:S(2)}, u32[]{:S(2)}) async-start(bf16[16,2,3456]{2,1,0:T(2,128)(2,1)} %shard_map.56), calls=%async_computation.3 | async-start | bytes 442368 | tf_op jit(solution)/shard_map/all_to_all | solution.py:206
  94.6 1.2 %shard_map.54 = bf16[2,2,128,256]{3,2,1,0:T(8,128)(2,1)S(1)} custom-call(bf16[256,128]{1,0:T(8,128)(2,1)S(1)} %get-tuple-element.15.own_ref, bf16[256,128]{1,0:T(8,128)(2,1)S(1)} %collective-permute-done.2.right_ref, bf16[256,128]{1,0:T(8,128)(2,1)S(1)} %collective-permute-done.3.up_ref, bf16[256,128]{1,0:T(8,128)(2,1)S(1)} %collective-permute-done.4.diag_ref, ...), custom_call_target="tpu_custom_call" | custom-call | flops 236978176 | bytes 3145728 | tf_op jit(solution)/shard_map/pallas_call | solution.py:269
  95.8 1.0 copy.5
  96.8 4.7 %all-to-all-done.3.in_ref = bf16[16,2,3456]{2,1,0:T(2,128)(2,1)S(1)} async-done(((bf16[16,2,3456]{2,1,0:T(2,128)(2,1)}), bf16[16,2,3456]{2,1,0:T(2,128)(2,1)S(1)}, u32[]{:S(2)}, u32[]{:S(2)}) %all-to-all-start.3) | async-done | bytes 221216 | tf_op jit(solution)/shard_map/all_to_all | solution.py:206
  101.5 1.0 shard_map.57
  (4 shorter events, 0.0 us)
Async XLA Ops:
  0.6 31.1 %copy-start = (bf16[3,3,3,128,256]{4,3,2,1,0:T(8,128)(2,1)S(1)}, bf16[3,3,3,128,256]{4,3,2,1,0:T(8,128)(2,1)}, u32[]{:S(2)}) copy-start(bf16[3,3,3,128,256]{4,3,2,1,0:T(8,128)(2,1)} %param.4) | copy-start | bytes 5308420
  23.5 10.9 %collective-permute-start = (bf16[8,3,16,256]{3,2,1,0:T(8,128)(2,1)S(1)}, bf16[8,3,16,256]{3,2,1,0:T(8,128)(2,1)S(1)}, u32[]{:S(2)}, u32[]{:S(2)}) collective-permute-start(bf16[8,3,16,256]{3,2,1,0:T(8,128)(2,1)S(1)} %slice.4), channel_id=1, source_target_pairs={{0,8},{8,16},{16,24},{24,32},{32,40},{40,48},{48,56},{56,64},{64,7... | collective-permute-start | bytes 589832 | tf_op jit(solution)/shard_map/ppermute | solution.py:202
  35.8 4.3 %collective-permute-start.1 = (bf16[128,3456]{1,0:T(8,128)(2,1)S(1)}, bf16[128,3456]{1,0:T(8,128)(2,1)S(1)}, u32[]{:S(2)}, u32[]{:S(2)}) collective-permute-start(bf16[128,3456]{1,0:T(8,128)(2,1)S(1)} %get-tuple-element.19), channel_id=1, source_target_pairs={{0,8},{8,0},{16,24},{24,16},{32,40},{40,32},{48,56},{56,48},{64,72... | collective-permute-start | bytes 2654216 | tf_op jit(solution)/shard_map/ppermute | solution.py:248
  41.4 23.1 %all-to-all-start.1 = ((bf16[8,16,3456]{2,1,0:T(8,128)(2,1)}), bf16[8,16,3456]{2,1,0:T(8,128)(2,1)S(1)}, u32[]{:S(2)}, u32[]{:S(2)}) async-start(bf16[8,16,3456]{2,1,0:T(8,128)(2,1)} %bitcast.2), calls=%async_computation.1 | async-start | bytes 1769472 | tf_op jit(solution)/shard_map/all_to_all | solution.py:206
  50.5 7.0 %collective-permute-start.4 = (bf16[256,128]{1,0:T(8,128)(2,1)S(1)}, bf16[256,128]{1,0:T(8,128)(2,1)S(1)}, u32[]{:S(2)}, u32[]{:S(2)}) collective-permute-start(bf16[256,128]{1,0:T(8,128)(2,1)S(1)} %get-tuple-element.15.own_ref), channel_id=1, source_target_pairs={{9,0},{10,1},{11,2},{12,3},{13,4},{14,5},{15,6},{17,8},{18,9},{19,... | collective-permute-start | bytes 196616 | tf_op jit(solution)/shard_map/ppermute | solution.py:260
  51.8 12.2 %collective-permute-start.3 = (bf16[256,128]{1,0:T(8,128)(2,1)S(1)}, bf16[256,128]{1,0:T(8,128)(2,1)S(1)}, u32[]{:S(2)}, u32[]{:S(2)}) collective-permute-start(bf16[256,128]{1,0:T(8,128)(2,1)S(1)} %get-tuple-element.15.own_ref), channel_id=1, source_target_pairs={{8,0},{16,8},{24,16},{32,24},{40,32},{48,40},{56,48},{64,56},{72,6... | collective-permute-start | bytes 196616 | tf_op jit(solution)/shard_map/ppermute | solution.py:202
  54.4 9.6 %collective-permute-start.2 = (bf16[256,128]{1,0:T(8,128)(2,1)S(1)}, bf16[256,128]{1,0:T(8,128)(2,1)S(1)}, u32[]{:S(2)}, u32[]{:S(2)}) collective-permute-start(bf16[256,128]{1,0:T(8,128)(2,1)S(1)} %get-tuple-element.15.own_ref), channel_id=1, source_target_pairs={{1,0},{2,1},{3,2},{4,3},{5,4},{6,5},{7,6},{9,8},{10,9},{11,10},{12... | collective-permute-start | bytes 196616 | tf_op jit(solution)/shard_map/ppermute | solution.py:202
  85.9 15.6 %all-to-all-start.3 = ((bf16[16,2,3456]{2,1,0:T(2,128)(2,1)}), bf16[16,2,3456]{2,1,0:T(2,128)(2,1)S(1)}, u32[]{:S(2)}, u32[]{:S(2)}) async-start(bf16[16,2,3456]{2,1,0:T(2,128)(2,1)} %shard_map.56), calls=%async_computation.3 | async-start | bytes 442368 | tf_op jit(solution)/shard_map/all_to_all | solution.py:206

commit v12 on v11

--- a/solution.py
+++ b/solution.py
@@ -16,15 +16,27 @@
     return (x * 8 + z) * 2 + core
 
 
-X4, Z4, B2 = range(4), range(4), range(2)
-WIDE = [[slab_of(x, 2 * zh + zl, c) for x in X4 for zl in B2] for zh in Z4 for c in B2]
+X4, Q4, B2 = range(4), range(4), range(2)
+
+
+def member_of(x, zh, zl, c, yh, yl):
+    return slab_of(x, 2 * zh + zl, c) * 8 + 2 * yh + yl
+
+
+WIDE = [
+    [member_of(x, zh, zl, c, yh, yl) for x in X4 for zl in B2 for yl in B2]
+    for zh in Q4
+    for c in B2
+    for yh in Q4
+]
 FAR = [
-    [slab_of(x, 2 * zh + zl, c) * 8 + y for zh in Z4 for y in range(8)]
+    [member_of(x, zh, zl, c, yh, yl) for zh in Q4 for yh in Q4]
     for x in X4
     for zl in B2
     for c in B2
+    for yl in B2
 ]
-NEAR = [[slab_of(x, 2 * zh + zl, c) for x in X4 for zl in B2 for c in B2] for zh in Z4]
+NEAR = [[slab_of(x, 2 * zh + zl, c) for x in X4 for zl in B2 for c in B2] for zh in Q4]
 CORE_PAIRS = [(s, s ^ 1) for s in range(64)]
 
 
@@ -104,7 +116,8 @@
 
 def core_rows(core):
     i, j = iotas(128, 256)
-    return ones_where(j == (((i >> 1) & 7) << 5) + ((i >> 4) << 2) + (i & 1) + core * 2)
+    tile = (((i >> 1) & 3) << 6) + (((i >> 3) & 1) << 5)
+    return ones_where(j == tile + ((i >> 4) << 2) + (i & 1) + core * 2)
 
 
 def taps_of(order, both, ze, zo):
@@ -262,9 +275,9 @@
         ("slab", "filt"),
         [(8 * s + y, 8 * s + y - 9) for s in range(1, 64) for y in range(1, 8)],
     )
-    tiles = exchange(part.reshape(8, 16, 3456), "slab", WIDE)
+    tiles = exchange(part.reshape(16, 8, 3456), ("slab", "filt"), WIDE)
     tiles, right, upper, diagonal = lax.optimization_barrier((tiles, right, upper, diagonal))
-    tiles = add_up(tiles, 32)
+    tiles = add_up(tiles, 16)
     tiles = add_up(exchange(tiles, ("slab", "filt"), FAR), 16)
     in_grad = call(
         input_body, shape((2, 2, 128, 256), BF16), [VMEM] * 5, (226 * mb, 3 * mb)

time: 103 us -> 101 us (0.981)
  starting transfers between devices: 33.2 us -> 31.5 us
  blocking collectives: 40.7 us -> 39.6 us
  waiting for transfers between devices: 17.5 us -> 18.6 us
    ppermute x1, waiting for transfers between devices: 1.85 us -> 9.97 us  [on_device(): lax.ppermute(grad, ('slab', 'filt'), [(8 * s + y, 8 * s + y - 9) for s in...]
    ppermute x3, waiting for transfers between devices: 7.98 us -> 1.49 us  [shifted_2(): lax.ppermute(value, axis, [(source, source + steps) for source in range(f...]
    all_to_all x2, starting transfers between devices: 17.8 us -> 16.2 us  [exchange(): lax.all_to_all(value, axis, split_axis=0, concat_axis=0, axis_index_group...]
    all_to_all x2, blocking collectives: 40.7 us -> 39.6 us  [exchange(): lax.all_to_all(value, axis, split_axis=0, concat_axis=0, axis_index_group...]
  transfers between devices with their start and end apart: 7 -> 7, of which waited for: 6 -> 4; matrix products, arithmetic and copies ran while one was open for 1% -> 1% of each run, Pallas kernels for 2% -> 2%
where the time goes in v12:
time: 101 us
  blocking collectives  39.6 us (39%)
  starting transfers between devices  31.5 us (31%)
  waiting for transfers between devices  18.6 us (18%)
  Pallas kernels  9.34 us (9%)
    all_to_all x2, blocking collectives, exchange(): lax.all_to_all(value, axis, split_axis=0, concat_axis=0, axis_index_group...  39.6 us
    all_to_all x2, starting transfers between devices, exchange(): lax.all_to_all(value, axis, split_axis=0, concat_axis=0, axis_index_group...  16.2 us
    ppermute x3, starting transfers between devices, shifted_2(): lax.ppermute(value, axis, [(source, source + steps) for source in range(f...  12.1 us
    ppermute x1, waiting for transfers between devices, on_device(): lax.ppermute(grad, ('slab', 'filt'), [(8 * s + y, 8 * s + y - 9) for s in...  9.97 us
    all_to_all x2, waiting for transfers between devices, exchange(): lax.all_to_all(value, axis, split_axis=0, concat_axis=0, axis_index_group...  4.73 us
    pallas_call x1, Pallas kernels, on_device(): call(pack_body, shape((8, 7, 16, 256), BF16), [ANY] * 2, (2 * mb, mb), [p...  2.48 us
    ppermute x1, waiting for transfers between devices, on_device(): other = lax.ppermute(part, 'slab', CORE_PAIRS)  2.39 us
  transfers between devices with their start and end apart: 7, of which 4 were waited for; matrix products, arithmetic and copies ran while one was open for 1% of the time, Pallas kernels for 2%

profile of v12, /device:TPU:1, one launch (start us, length us, event | category | flops | bytes accessed | tf_op | source)
XLA Modules:
  0.0 100.8 jit_solution(2516037045770656409)
XLA Ops:
  0.6 2.5 %shard_map.50 = bf16[8,7,16,256]{3,2,1,0:T(8,128)(2,1)} custom-call(bf16[2,16,16,256]{3,2,1,0:T(8,128)(2,1)} %vol_hbm.1, bf16[1,32,8,128]{3,2,1,0:T(8,128)(2,1)} %err_hbm.1), custom_call_target="tpu_custom_call" | custom-call | flops 2097152 | bytes 1048576 | tf_op jit(solution)/shard_map/pallas_call | solution.py:236
  3.1 20.3 %all_to_all.20.rec_ref = bf16[8,7,16,256]{3,2,1,0:T(8,128)(2,1)S(1)} all-to-all(bf16[8,7,16,256]{3,2,1,0:T(8,128)(2,1)} %shard_map.50), channel_id=1, replica_groups=mesh['slab'=64,'filt'=8] {'filt'}, dimensions={0} | all-to-all | bytes 917504 | tf_op jit(solution)/shard_map/all_to_all | solution.py:219
  23.5 8.3 %collective-permute-start = (bf16[8,3,16,256]{3,2,1,0:T(8,128)(2,1)S(1)}, bf16[8,3,16,256]{3,2,1,0:T(8,128)(2,1)S(1)}, u32[]{:S(2)}, u32[]{:S(2)}) collective-permute-start(bf16[8,3,16,256]{3,2,1,0:T(8,128)(2,1)S(1)} %slice.4), channel_id=1, source_target_pairs={{0,8},{8,16},{16,24},{24,32},{32,40},{40,48},{48,56},{56,64},{64,7... | collective-permute-start | bytes 589832 | tf_op jit(solution)/shard_map/ppermute | solution.py:215
  31.8 1.1 %shard_map.51 = (bf16[256,1152]{1,0:T(8,128)(2,1)S(1)}, bf16[512,1152]{1,0:T(8,128)(2,1)S(1)}) custom-call(bf16[9,3,128,256]{3,2,1,0:T(8,128)(2,1)S(1)} %bitcast.7), custom_call_target="tpu_custom_call" | custom-call | flops 473956352 | bytes 4194304 | tf_op jit(solution)/shard_map/pallas_call | solution.py:249
  32.8 1.5 %collective-permute-done.rim_ref = bf16[8,3,16,256]{3,2,1,0:T(8,128)(2,1)S(1)} collective-permute-done((bf16[8,3,16,256]{3,2,1,0:T(8,128)(2,1)S(1)}, bf16[8,3,16,256]{3,2,1,0:T(8,128)(2,1)S(1)}, u32[]{:S(2)}, u32[]{:S(2)}) %collective-permute-start) | collective-permute-done | bytes 196640 | tf_op jit(solution)/shard_map/ppermute | solution.py:215
  34.3 1.5 %shard_map.52 = (bf16[256,128]{1,0:T(8,128)(2,1)S(1)}, bf16[256,256]{1,0:T(8,128)(2,1)S(1)}, bf16[1152,128]{1,0:T(8,128)(2,1)S(1)}, bf16[1152,128]{1,0:T(8,128)(2,1)S(1)}, bf16[128,3456]{1,0:T(8,128)(2,1)S(1)}) custom-call(s32[1]{0:T(128)} %bitcast.core_ref, bf16[8,7,16,256]{3,2,1,0:T(8,128)(2,1)S(1)} %all_to_all.20.rec_ref, ...), custom_call_target="tpu_custom_call" | custom-call | flops 475004928 | bytes 4194304 | tf_op jit(solution)/shard_map/pallas_call | solution.py:254
  35.8 1.9 %collective-permute-start.1 = (bf16[128,3456]{1,0:T(8,128)(2,1)S(1)}, bf16[128,3456]{1,0:T(8,128)(2,1)S(1)}, u32[]{:S(2)}, u32[]{:S(2)}) collective-permute-start(bf16[128,3456]{1,0:T(8,128)(2,1)S(1)} %get-tuple-element.19), channel_id=1, source_target_pairs={{0,8},{8,0},{16,24},{24,16},{32,40},{40,32},{48,56},{56,48},{64,72... | collective-permute-start | bytes 2654216 | tf_op jit(solution)/shard_map/ppermute | solution.py:261
  37.7 2.4 %collective-permute-done.1.other_ref = bf16[128,3456]{1,0:T(8,128)(2,1)S(1)} collective-permute-done((bf16[128,3456]{1,0:T(8,128)(2,1)S(1)}, bf16[128,3456]{1,0:T(8,128)(2,1)S(1)}, u32[]{:S(2)}, u32[]{:S(2)}) %collective-permute-start.1) | collective-permute-done | bytes 884768 | tf_op jit(solution)/shard_map/ppermute | solution.py:261
  40.1 1.3 %shard_map.53 = bf16[128,3456]{1,0:T(8,128)(2,1)} custom-call(s32[1]{0:T(128)} %bitcast.core_ref, bf16[256,256]{1,0:T(8,128)(2,1)S(1)} %get-tuple-element.16.both_ref, bf16[1152,128]{1,0:T(8,128)(2,1)S(1)} %get-tuple-element.17.ze, bf16[1152,128]{1,0:T(8,128)(2,1)S(1)} %get-tuple-element.18.zo, bf16[128,3456]{1,0:T(8,128)(2,1)S(1)} %collective-permute-done.1.other_ref), custom_call_target="tpu_custom_call" | custom-call | flops 118489088 | bytes 3145728 | tf_op jit(solution)/shard_map/pallas_call | solution.py:263
  41.4 9.2 %all-to-all-start.1 = ((bf16[16,8,3456]{2,1,0:T(8,128)(2,1)}), bf16[16,8,3456]{2,1,0:T(8,128)(2,1)S(1)}, u32[]{:S(2)}, u32[]{:S(2)}) async-start(bf16[16,8,3456]{2,1,0:T(8,128)(2,1)} %bitcast.2), calls=%async_computation.1 | async-start | bytes 1769472 | tf_op jit(solution)/shard_map/all_to_all | solution.py:219
  50.6 1.3 %collective-permute-start.4 = (bf16[256,128]{1,0:T(8,128)(2,1)S(1)}, bf16[256,128]{1,0:T(8,128)(2,1)S(1)}, u32[]{:S(2)}, u32[]{:S(2)}) collective-permute-start(bf16[256,128]{1,0:T(8,128)(2,1)S(1)} %get-tuple-element.15.own_ref), channel_id=1, source_target_pairs={{9,0},{10,1},{11,2},{12,3},{13,4},{14,5},{15,6},{17,8},{18,9},{19,... | collective-permute-start | bytes 196616 | tf_op jit(solution)/shard_map/ppermute | solution.py:273
  51.9 2.6 %collective-permute-start.3 = (bf16[256,128]{1,0:T(8,128)(2,1)S(1)}, bf16[256,128]{1,0:T(8,128)(2,1)S(1)}, u32[]{:S(2)}, u32[]{:S(2)}) collective-permute-start(bf16[256,128]{1,0:T(8,128)(2,1)S(1)} %get-tuple-element.15.own_ref), channel_id=1, source_target_pairs={{8,0},{16,8},{24,16},{32,24},{40,32},{48,40},{56,48},{64,56},{72,6... | collective-permute-start | bytes 196616 | tf_op jit(solution)/shard_map/ppermute | solution.py:215
  54.5 1.3 %collective-permute-start.2 = (bf16[256,128]{1,0:T(8,128)(2,1)S(1)}, bf16[256,128]{1,0:T(8,128)(2,1)S(1)}, u32[]{:S(2)}, u32[]{:S(2)}) collective-permute-start(bf16[256,128]{1,0:T(8,128)(2,1)S(1)} %get-tuple-element.15.own_ref), channel_id=1, source_target_pairs={{1,0},{2,1},{3,2},{4,3},{5,4},{6,5},{7,6},{9,8},{10,9},{11,10},{12... | collective-permute-start | bytes 196616 | tf_op jit(solution)/shard_map/ppermute | solution.py:215
  55.8 10.0 %collective-permute-done.4.diag_ref = bf16[256,128]{1,0:T(8,128)(2,1)S(1)} collective-permute-done((bf16[256,128]{1,0:T(8,128)(2,1)S(1)}, bf16[256,128]{1,0:T(8,128)(2,1)S(1)}, u32[]{:S(2)}, u32[]{:S(2)}) %collective-permute-start.4) | collective-permute-done | bytes 65568 | tf_op jit(solution)/shard_map/ppermute | solution.py:273
  65.8 0.0 collective-permute-done.3.up_ref
  65.8 0.0 collective-permute-done.2.right_ref
  65.8 0.1 shard_map.55
  65.9 19.2 %all_to_all.21.in_ref = bf16[16,2,3456]{2,1,0:T(2,128)(2,1)S(1)} all-to-all(bf16[16,2,3456]{2,1,0:T(2,128)(2,1)S(1)} %shard_map.55), channel_id=1, replica_groups={{0,2,4,6,32,34,36,38,64,66,68,70,96,98,100,102},{1,3,5,7,33,35,37,39,65..., dimensions={0} | all-to-all | bytes 442368 | tf_op jit(solution)/shard_map/all_to_all | solution.py:219
  85.2 0.7 shard_map.56
  85.9 7.0 %all-to-all-start.3 = ((bf16[16,2,3456]{2,1,0:T(2,128)(2,1)}), bf16[16,2,3456]{2,1,0:T(2,128)(2,1)S(1)}, u32[]{:S(2)}, u32[]{:S(2)}) async-start(bf16[16,2,3456]{2,1,0:T(2,128)(2,1)} %shard_map.56), calls=%async_computation.3 | async-start | bytes 442368 | tf_op jit(solution)/shard_map/all_to_all | solution.py:219
  92.9 1.2 %shard_map.54 = bf16[2,2,128,256]{3,2,1,0:T(8,128)(2,1)S(1)} custom-call(bf16[256,128]{1,0:T(8,128)(2,1)S(1)} %get-tuple-element.15.own_ref, bf16[256,128]{1,0:T(8,128)(2,1)S(1)} %collective-permute-done.2.right_ref, bf16[256,128]{1,0:T(8,128)(2,1)S(1)} %collective-permute-done.3.up_ref, bf16[256,128]{1,0:T(8,128)(2,1)S(1)} %collective-permute-done.4.diag_ref, ...), custom_call_target="tpu_custom_call" | custom-call | flops 236978176 | bytes 3145728 | tf_op jit(solution)/shard_map/pallas_call | solution.py:282
  94.1 1.0 copy.5
  95.1 4.7 %all-to-all-done.3.in_ref = bf16[16,2,3456]{2,1,0:T(2,128)(2,1)S(1)} async-done(((bf16[16,2,3456]{2,1,0:T(2,128)(2,1)}), bf16[16,2,3456]{2,1,0:T(2,128)(2,1)S(1)}, u32[]{:S(2)}, u32[]{:S(2)}) %all-to-all-start.3) | async-done | bytes 221216 | tf_op jit(solution)/shard_map/all_to_all | solution.py:219
  99.8 1.0 shard_map.57
  (4 shorter events, 0.0 us)
Async XLA Ops:
  0.6 31.1 %copy-start = (bf16[3,3,3,128,256]{4,3,2,1,0:T(8,128)(2,1)S(1)}, bf16[3,3,3,128,256]{4,3,2,1,0:T(8,128)(2,1)}, u32[]{:S(2)}) copy-start(bf16[3,3,3,128,256]{4,3,2,1,0:T(8,128)(2,1)} %param.4) | copy-start | bytes 5308420
  23.5 10.9 %collective-permute-start = (bf16[8,3,16,256]{3,2,1,0:T(8,128)(2,1)S(1)}, bf16[8,3,16,256]{3,2,1,0:T(8,128)(2,1)S(1)}, u32[]{:S(2)}, u32[]{:S(2)}) collective-permute-start(bf16[8,3,16,256]{3,2,1,0:T(8,128)(2,1)S(1)} %slice.4), channel_id=1, source_target_pairs={{0,8},{8,16},{16,24},{24,32},{32,40},{40,48},{48,56},{56,64},{64,7... | collective-permute-start | bytes 589832 | tf_op jit(solution)/shard_map/ppermute | solution.py:215
  35.8 4.3 %collective-permute-start.1 = (bf16[128,3456]{1,0:T(8,128)(2,1)S(1)}, bf16[128,3456]{1,0:T(8,128)(2,1)S(1)}, u32[]{:S(2)}, u32[]{:S(2)}) collective-permute-start(bf16[128,3456]{1,0:T(8,128)(2,1)S(1)} %get-tuple-element.19), channel_id=1, source_target_pairs={{0,8},{8,0},{16,24},{24,16},{32,40},{40,32},{48,56},{56,48},{64,72... | collective-permute-start | bytes 2654216 | tf_op jit(solution)/shard_map/ppermute | solution.py:261
  41.4 24.3 %all-to-all-start.1 = ((bf16[16,8,3456]{2,1,0:T(8,128)(2,1)}), bf16[16,8,3456]{2,1,0:T(8,128)(2,1)S(1)}, u32[]{:S(2)}, u32[]{:S(2)}) async-start(bf16[16,8,3456]{2,1,0:T(8,128)(2,1)} %bitcast.2), calls=%async_computation.1 | async-start | bytes 1769472 | tf_op jit(solution)/shard_map/all_to_all | solution.py:219
  50.6 15.1 %collective-permute-start.4 = (bf16[256,128]{1,0:T(8,128)(2,1)S(1)}, bf16[256,128]{1,0:T(8,128)(2,1)S(1)}, u32[]{:S(2)}, u32[]{:S(2)}) collective-permute-start(bf16[256,128]{1,0:T(8,128)(2,1)S(1)} %get-tuple-element.15.own_ref), channel_id=1, source_target_pairs={{9,0},{10,1},{11,2},{12,3},{13,4},{14,5},{15,6},{17,8},{18,9},{19,... | collective-permute-start | bytes 196616 | tf_op jit(solution)/shard_map/ppermute | solution.py:273
  51.9 13.8 %collective-permute-start.3 = (bf16[256,128]{1,0:T(8,128)(2,1)S(1)}, bf16[256,128]{1,0:T(8,128)(2,1)S(1)}, u32[]{:S(2)}, u32[]{:S(2)}) collective-permute-start(bf16[256,128]{1,0:T(8,128)(2,1)S(1)} %get-tuple-element.15.own_ref), channel_id=1, source_target_pairs={{8,0},{16,8},{24,16},{32,24},{40,32},{48,40},{56,48},{64,56},{72,6... | collective-permute-start | bytes 196616 | tf_op jit(solution)/shard_map/ppermute | solution.py:215
  54.5 11.3 %collective-permute-start.2 = (bf16[256,128]{1,0:T(8,128)(2,1)S(1)}, bf16[256,128]{1,0:T(8,128)(2,1)S(1)}, u32[]{:S(2)}, u32[]{:S(2)}) collective-permute-start(bf16[256,128]{1,0:T(8,128)(2,1)S(1)} %get-tuple-element.15.own_ref), channel_id=1, source_target_pairs={{1,0},{2,1},{3,2},{4,3},{5,4},{6,5},{7,6},{9,8},{10,9},{11,10},{12... | collective-permute-start | bytes 196616 | tf_op jit(solution)/shard_map/ppermute | solution.py:215
  85.9 13.9 %all-to-all-start.3 = ((bf16[16,2,3456]{2,1,0:T(2,128)(2,1)}), bf16[16,2,3456]{2,1,0:T(2,128)(2,1)S(1)}, u32[]{:S(2)}, u32[]{:S(2)}) async-start(bf16[16,2,3456]{2,1,0:T(2,128)(2,1)} %shard_map.56), calls=%async_computation.3 | async-start | bytes 442368 | tf_op jit(solution)/shard_map/all_to_all | solution.py:219

commit v13 on v12

--- a/solution.py
+++ b/solution.py
@@ -259,7 +259,6 @@
     )(core, received, rim, even, odd)
 
     other = lax.ppermute(part, "slab", CORE_PAIRS)
-    right = shifted_2(grad, "filt", -1)
     part = call(
         keep_body,
         shape((128, 3456), BF16),
@@ -269,16 +268,19 @@
         LIMIT,
         ANY,
     )(core, both, ze, zo, other)
-    upper = shifted_2(grad, "slab", -1)
+    tiles = exchange(part.reshape(16, 8, 3456), ("slab", "filt"), WIDE)
+    tiles, late = lax.optimization_barrier((tiles, grad))
+    right = shifted_2(late, "filt", -1)
+    upper = shifted_2(late, "slab", -1)
     diagonal = lax.ppermute(
-        grad,
+        late,
         ("slab", "filt"),
         [(8 * s + y, 8 * s + y - 9) for s in range(1, 64) for y in range(1, 8)],
     )
-    tiles = exchange(part.reshape(16, 8, 3456), ("slab", "filt"), WIDE)
+    tiles = exchange(add_up(tiles, 16), ("slab", "filt"), FAR)
     tiles, right, upper, diagonal = lax.optimization_barrier((tiles, right, upper, diagonal))
     tiles = add_up(tiles, 16)
-    tiles = add_up(exchange(tiles, ("slab", "filt"), FAR), 16)
+
     in_grad = call(
         input_body, shape((2, 2, 128, 256), BF16), [VMEM] * 5, (226 * mb, 3 * mb)
     )(grad, right, upper, diagonal, taps)

time: 101 us -> 100 us (0.990)
  waiting for transfers between devices: 18.6 us -> 13.2 us
  blocking collectives: 39.6 us -> 41.2 us
  starting transfers between devices: 31.5 us -> 33.1 us
    ppermute x1, waiting for transfers between devices: 9.97 us -> 3.45 us  [on_device(): lax.ppermute(late, ('slab', 'filt'), [(8 * s + y, 8 * s + y - 9) for s in...]
    ppermute x3, starting transfers between devices: 12.1 us -> 14.5 us  [shifted_2(): lax.ppermute(value, axis, [(source, source + steps) for source in range(f...]
    all_to_all x2, blocking collectives: 39.6 us -> 41.2 us  [exchange(): lax.all_to_all(value, axis, split_axis=0, concat_axis=0, axis_index_group...]
    ppermute x3, waiting for transfers between devices: 1.49 us -> 2.59 us  [shifted_2(): lax.ppermute(value, axis, [(source, source + steps) for source in range(f...]
  transfers between devices with their start and end apart: 7 -> 7, of which waited for: 4 -> 5; matrix products, arithmetic and copies ran while one was open for 1% -> 1% of each run, Pallas kernels for 2% -> 2%
where the time goes in v13:
time: 100 us; the launch traced here: 98.9 us
  blocking collectives  41.2 us (41%)
  starting transfers between devices  33.1 us (33%)
  waiting for transfers between devices  13.2 us (13%)
  Pallas kernels  9.65 us (10%)
    all_to_all x2, blocking collectives, exchange(): lax.all_to_all(value, axis, split_axis=0, concat_axis=0, axis_index_group...  41.2 us
    all_to_all x2, starting transfers between devices, exchange(): lax.all_to_all(value, axis, split_axis=0, concat_axis=0, axis_index_group...  15.4 us
    ppermute x3, starting transfers between devices, shifted_2(): lax.ppermute(value, axis, [(source, source + steps) for source in range(f...  14.5 us
    all_to_all x2, waiting for transfers between devices, exchange(): lax.all_to_all(value, axis, split_axis=0, concat_axis=0, axis_index_group...  4.73 us
    ppermute x1, waiting for transfers between devices, on_device(): lax.ppermute(late, ('slab', 'filt'), [(8 * s + y, 8 * s + y - 9) for s in...  3.45 us
    ppermute x3, waiting for transfers between devices, shifted_2(): lax.ppermute(value, axis, [(source, source + steps) for source in range(f...  2.59 us
    pallas_call x1, Pallas kernels, on_device(): call(pack_body, shape((8, 7, 16, 256), BF16), [ANY] * 2, (2 * mb, mb), [p...  2.48 us
    ppermute x1, waiting for transfers between devices, on_device(): other = lax.ppermute(part, 'slab', CORE_PAIRS)  2.39 us
  transfers between devices with their start and end apart: 7, of which 5 were waited for; matrix products, arithmetic and copies ran while one was open for 1% of the time, Pallas kernels for 2%

profile of v13, /device:TPU:1, one launch (start us, length us, event | category | flops | bytes accessed | tf_op | source)
XLA Modules:
  0.0 98.9 jit_solution(6918964980568513684)
XLA Ops:
  0.6 2.5 %shard_map.50 = bf16[8,7,16,256]{3,2,1,0:T(8,128)(2,1)} custom-call(bf16[2,16,16,256]{3,2,1,0:T(8,128)(2,1)} %vol_hbm.1, bf16[1,32,8,128]{3,2,1,0:T(8,128)(2,1)} %err_hbm.1), custom_call_target="tpu_custom_call" | custom-call | flops 2097152 | bytes 1048576 | tf_op jit(solution)/shard_map/pallas_call | solution.py:236
  3.1 20.3 %all_to_all.20.rec_ref = bf16[8,7,16,256]{3,2,1,0:T(8,128)(2,1)S(1)} all-to-all(bf16[8,7,16,256]{3,2,1,0:T(8,128)(2,1)} %shard_map.50), channel_id=1, replica_groups=mesh['slab'=64,'filt'=8] {'filt'}, dimensions={0} | all-to-all | bytes 917504 | tf_op jit(solution)/shard_map/all_to_all | solution.py:219
  23.5 8.3 %collective-permute-start = (bf16[8,3,16,256]{3,2,1,0:T(8,128)(2,1)S(1)}, bf16[8,3,16,256]{3,2,1,0:T(8,128)(2,1)S(1)}, u32[]{:S(2)}, u32[]{:S(2)}) collective-permute-start(bf16[8,3,16,256]{3,2,1,0:T(8,128)(2,1)S(1)} %slice.4), channel_id=1, source_target_pairs={{0,8},{8,16},{16,24},{24,32},{32,40},{40,48},{48,56},{56,64},{64,7... | collective-permute-start | bytes 589832 | tf_op jit(solution)/shard_map/ppermute | solution.py:215
  31.8 1.1 %shard_map.51 = (bf16[256,1152]{1,0:T(8,128)(2,1)S(1)}, bf16[512,1152]{1,0:T(8,128)(2,1)S(1)}) custom-call(bf16[9,3,128,256]{3,2,1,0:T(8,128)(2,1)S(1)} %bitcast.7), custom_call_target="tpu_custom_call" | custom-call | flops 473956352 | bytes 4194304 | tf_op jit(solution)/shard_map/pallas_call | solution.py:249
  32.8 1.5 %collective-permute-done.rim_ref = bf16[8,3,16,256]{3,2,1,0:T(8,128)(2,1)S(1)} collective-permute-done((bf16[8,3,16,256]{3,2,1,0:T(8,128)(2,1)S(1)}, bf16[8,3,16,256]{3,2,1,0:T(8,128)(2,1)S(1)}, u32[]{:S(2)}, u32[]{:S(2)}) %collective-permute-start) | collective-permute-done | bytes 196640 | tf_op jit(solution)/shard_map/ppermute | solution.py:215
  34.3 1.5 %shard_map.52 = (bf16[256,128]{1,0:T(8,128)(2,1)S(1)}, bf16[256,256]{1,0:T(8,128)(2,1)S(1)}, bf16[1152,128]{1,0:T(8,128)(2,1)S(1)}, bf16[1152,128]{1,0:T(8,128)(2,1)S(1)}, bf16[128,3456]{1,0:T(8,128)(2,1)S(1)}) custom-call(s32[1]{0:T(128)} %bitcast.core_ref, bf16[8,7,16,256]{3,2,1,0:T(8,128)(2,1)S(1)} %all_to_all.20.rec_ref, ...), custom_call_target="tpu_custom_call" | custom-call | flops 475004928 | bytes 4194304 | tf_op jit(solution)/shard_map/pallas_call | solution.py:254
  35.8 1.9 %collective-permute-start.1 = (bf16[128,3456]{1,0:T(8,128)(2,1)S(1)}, bf16[128,3456]{1,0:T(8,128)(2,1)S(1)}, u32[]{:S(2)}, u32[]{:S(2)}) collective-permute-start(bf16[128,3456]{1,0:T(8,128)(2,1)S(1)} %get-tuple-element.21), channel_id=1, source_target_pairs={{0,8},{8,0},{16,24},{24,16},{32,40},{40,32},{48,56},{56,48},{64,72... | collective-permute-start | bytes 2654216 | tf_op jit(solution)/shard_map/ppermute | solution.py:261
  37.7 2.4 %collective-permute-done.1.other_ref = bf16[128,3456]{1,0:T(8,128)(2,1)S(1)} collective-permute-done((bf16[128,3456]{1,0:T(8,128)(2,1)S(1)}, bf16[128,3456]{1,0:T(8,128)(2,1)S(1)}, u32[]{:S(2)}, u32[]{:S(2)}) %collective-permute-start.1) | collective-permute-done | bytes 884768 | tf_op jit(solution)/shard_map/ppermute | solution.py:261
  40.1 0.9 shard_map.53
  41.1 20.9 %all_to_all.21.in_ref = bf16[16,8,3456]{2,1,0:T(8,128)(2,1)S(1)} all-to-all(bf16[16,8,3456]{2,1,0:T(8,128)(2,1)S(1)} %bitcast.9), channel_id=1, replica_groups={{0,1,16,17,128,129,144,145,256,257,272,273,384,385,400,401},{2,3,18,19,..., dimensions={0} | all-to-all | bytes 1769472 | tf_op jit(solution)/shard_map/all_to_all | solution.py:219
  62.0 0.8 shard_map.54
  62.8 7.3 %all-to-all-start.2 = ((bf16[16,2,3456]{2,1,0:T(2,128)(2,1)}), bf16[16,2,3456]{2,1,0:T(2,128)(2,1)S(1)}, u32[]{:S(2)}, u32[]{:S(2)}) async-start(bf16[16,2,3456]{2,1,0:T(2,128)(2,1)} %shard_map.54), calls=%async_computation.2 | async-start | bytes 442368 | tf_op jit(solution)/shard_map/all_to_all | solution.py:219
  70.1 1.3 %collective-permute-start.4 = (bf16[256,128]{1,0:T(8,128)(2,1)S(1)}, bf16[256,128]{1,0:T(8,128)(2,1)S(1)}, u32[]{:S(2)}, u32[]{:S(2)}) collective-permute-start(bf16[256,128]{1,0:T(8,128)(2,1)S(1)} %get-tuple-element.23.own_ref), channel_id=1, source_target_pairs={{9,0},{10,1},{11,2},{12,3},{13,4},{14,5},{15,6},{17,8},{18,9},{19,... | collective-permute-start | bytes 196616 | tf_op jit(solution)/shard_map/ppermute | solution.py:275
  71.4 4.9 %collective-permute-start.3 = (bf16[256,128]{1,0:T(8,128)(2,1)S(1)}, bf16[256,128]{1,0:T(8,128)(2,1)S(1)}, u32[]{:S(2)}, u32[]{:S(2)}) collective-permute-start(bf16[256,128]{1,0:T(8,128)(2,1)S(1)} %get-tuple-element.23.own_ref), channel_id=1, source_target_pairs={{8,0},{16,8},{24,16},{32,24},{40,32},{48,40},{56,48},{64,56},{72,6... | collective-permute-start | bytes 196616 | tf_op jit(solution)/shard_map/ppermute | solution.py:215
  76.4 1.3 %collective-permute-start.2 = (bf16[256,128]{1,0:T(8,128)(2,1)S(1)}, bf16[256,128]{1,0:T(8,128)(2,1)S(1)}, u32[]{:S(2)}, u32[]{:S(2)}) collective-permute-start(bf16[256,128]{1,0:T(8,128)(2,1)S(1)} %get-tuple-element.23.own_ref), channel_id=1, source_target_pairs={{1,0},{2,1},{3,2},{4,3},{5,4},{6,5},{7,6},{9,8},{10,9},{11,10},{12... | collective-permute-start | bytes 196616 | tf_op jit(solution)/shard_map/ppermute | solution.py:215
  77.7 3.4 %collective-permute-done.4.diag_ref = bf16[256,128]{1,0:T(8,128)(2,1)S(1)} collective-permute-done((bf16[256,128]{1,0:T(8,128)(2,1)S(1)}, bf16[256,128]{1,0:T(8,128)(2,1)S(1)}, u32[]{:S(2)}, u32[]{:S(2)}) %collective-permute-start.4) | collective-permute-done | bytes 65568 | tf_op jit(solution)/shard_map/ppermute | solution.py:275
  81.1 0.0 collective-permute-done.3.up_ref
  81.1 1.1 %collective-permute-done.2.right_ref = bf16[256,128]{1,0:T(8,128)(2,1)S(1)} collective-permute-done((bf16[256,128]{1,0:T(8,128)(2,1)S(1)}, bf16[256,128]{1,0:T(8,128)(2,1)S(1)}, u32[]{:S(2)}, u32[]{:S(2)}) %collective-permute-start.2) | collective-permute-done | bytes 65568 | tf_op jit(solution)/shard_map/ppermute | solution.py:215
  82.2 0.7 shard_map.56
  83.0 8.1 %all-to-all-start.3 = ((bf16[16,2,3456]{2,1,0:T(2,128)(2,1)}), bf16[16,2,3456]{2,1,0:T(2,128)(2,1)S(1)}, u32[]{:S(2)}, u32[]{:S(2)}) async-start(bf16[16,2,3456]{2,1,0:T(2,128)(2,1)} %shard_map.56), calls=%async_computation.3 | async-start | bytes 442368 | tf_op jit(solution)/shard_map/all_to_all | solution.py:219
  91.0 1.2 %shard_map.55 = bf16[2,2,128,256]{3,2,1,0:T(8,128)(2,1)S(1)} custom-call(bf16[256,128]{1,0:T(8,128)(2,1)S(1)} %get-tuple-element.23.own_ref, bf16[256,128]{1,0:T(8,128)(2,1)S(1)} %collective-permute-done.2.right_ref, bf16[256,128]{1,0:T(8,128)(2,1)S(1)} %collective-permute-done.3.up_ref, bf16[256,128]{1,0:T(8,128)(2,1)S(1)} %collective-permute-done.4.diag_ref, ...), custom_call_target="tpu_custom_call" | custom-call | flops 236978176 | bytes 3145728 | tf_op jit(solution)/shard_map/pallas_call | solution.py:284
  92.2 1.0 copy.5
  93.2 4.7 %all-to-all-done.3.in_ref = bf16[16,2,3456]{2,1,0:T(2,128)(2,1)S(1)} async-done(((bf16[16,2,3456]{2,1,0:T(2,128)(2,1)}), bf16[16,2,3456]{2,1,0:T(2,128)(2,1)S(1)}, u32[]{:S(2)}, u32[]{:S(2)}) %all-to-all-start.3) | async-done | bytes 221216 | tf_op jit(solution)/shard_map/all_to_all | solution.py:219
  97.9 1.0 shard_map.57
  (4 shorter events, 0.0 us)
Async XLA Ops:
  0.6 31.1 %copy-start = (bf16[3,3,3,128,256]{4,3,2,1,0:T(8,128)(2,1)S(1)}, bf16[3,3,3,128,256]{4,3,2,1,0:T(8,128)(2,1)}, u32[]{:S(2)}) copy-start(bf16[3,3,3,128,256]{4,3,2,1,0:T(8,128)(2,1)} %param.4) | copy-start | bytes 5308420
  23.5 10.9 %collective-permute-start = (bf16[8,3,16,256]{3,2,1,0:T(8,128)(2,1)S(1)}, bf16[8,3,16,256]{3,2,1,0:T(8,128)(2,1)S(1)}, u32[]{:S(2)}, u32[]{:S(2)}) collective-permute-start(bf16[8,3,16,256]{3,2,1,0:T(8,128)(2,1)S(1)} %slice.4), channel_id=1, source_target_pairs={{0,8},{8,16},{16,24},{24,32},{32,40},{40,48},{48,56},{56,64},{64,7... | collective-permute-start | bytes 589832 | tf_op jit(solution)/shard_map/ppermute | solution.py:215
  35.8 4.3 %collective-permute-start.1 = (bf16[128,3456]{1,0:T(8,128)(2,1)S(1)}, bf16[128,3456]{1,0:T(8,128)(2,1)S(1)}, u32[]{:S(2)}, u32[]{:S(2)}) collective-permute-start(bf16[128,3456]{1,0:T(8,128)(2,1)S(1)} %get-tuple-element.21), channel_id=1, source_target_pairs={{0,8},{8,0},{16,24},{24,16},{32,40},{40,32},{48,56},{56,48},{64,72... | collective-permute-start | bytes 2654216 | tf_op jit(solution)/shard_map/ppermute | solution.py:261
  62.8 19.4 %all-to-all-start.2 = ((bf16[16,2,3456]{2,1,0:T(2,128)(2,1)}), bf16[16,2,3456]{2,1,0:T(2,128)(2,1)S(1)}, u32[]{:S(2)}, u32[]{:S(2)}) async-start(bf16[16,2,3456]{2,1,0:T(2,128)(2,1)} %shard_map.54), calls=%async_computation.2 | async-start | bytes 442368 | tf_op jit(solution)/shard_map/all_to_all | solution.py:219
  70.1 11.0 %collective-permute-start.4 = (bf16[256,128]{1,0:T(8,128)(2,1)S(1)}, bf16[256,128]{1,0:T(8,128)(2,1)S(1)}, u32[]{:S(2)}, u32[]{:S(2)}) collective-permute-start(bf16[256,128]{1,0:T(8,128)(2,1)S(1)} %get-tuple-element.23.own_ref), channel_id=1, source_target_pairs={{9,0},{10,1},{11,2},{12,3},{13,4},{14,5},{15,6},{17,8},{18,9},{19,... | collective-permute-start | bytes 196616 | tf_op jit(solution)/shard_map/ppermute | solution.py:275
  71.4 9.7 %collective-permute-start.3 = (bf16[256,128]{1,0:T(8,128)(2,1)S(1)}, bf16[256,128]{1,0:T(8,128)(2,1)S(1)}, u32[]{:S(2)}, u32[]{:S(2)}) collective-permute-start(bf16[256,128]{1,0:T(8,128)(2,1)S(1)} %get-tuple-element.23.own_ref), channel_id=1, source_target_pairs={{8,0},{16,8},{24,16},{32,24},{40,32},{48,40},{56,48},{64,56},{72,6... | collective-permute-start | bytes 196616 | tf_op jit(solution)/shard_map/ppermute | solution.py:215
  76.4 5.9 %collective-permute-start.2 = (bf16[256,128]{1,0:T(8,128)(2,1)S(1)}, bf16[256,128]{1,0:T(8,128)(2,1)S(1)}, u32[]{:S(2)}, u32[]{:S(2)}) collective-permute-start(bf16[256,128]{1,0:T(8,128)(2,1)S(1)} %get-tuple-element.23.own_ref), channel_id=1, source_target_pairs={{1,0},{2,1},{3,2},{4,3},{5,4},{6,5},{7,6},{9,8},{10,9},{11,10},{12... | collective-permute-start | bytes 196616 | tf_op jit(solution)/shard_map/ppermute | solution.py:215
  83.0 14.9 %all-to-all-start.3 = ((bf16[16,2,3456]{2,1,0:T(2,128)(2,1)}), bf16[16,2,3456]{2,1,0:T(2,128)(2,1)S(1)}, u32[]{:S(2)}, u32[]{:S(2)}) async-start(bf16[16,2,3456]{2,1,0:T(2,128)(2,1)} %shard_map.56), calls=%async_computation.3 | async-start | bytes 442368 | tf_op jit(solution)/shard_map/all_to_all | solution.py:219

commit v14 on v12

--- a/solution.py
+++ b/solution.py
@@ -188,12 +188,12 @@
                 out_ref[ab * 3 + c, 2 * m : 2 * m + 2] = rows[:, start : start + 128]
 
 
-def input_body(own_ref, right_ref, up_ref, diag_ref, w_ref, out_ref):
+def input_body(own_ref, up_ref, w_ref, out_ref):
     lane = lax.broadcasted_iota(jnp.int32, (128, 128), 1)
     i, j = iotas(256, 256)
     weave = ones_where(j == ((i & 127) << 1) + (i >> 7))
     taps = (((1, 0),), ((2, 0), (0, 1)))
-    grads = ((own_ref[...], right_ref[...]), (up_ref[...], diag_ref[...]))
+    grads = ((own_ref[0], own_ref[1]), (up_ref[0], up_ref[1]))
     for ed in range(2):
         for er in range(2):
             sums = []
@@ -269,19 +269,17 @@
         LIMIT,
         ANY,
     )(core, both, ze, zo, other)
-    upper = shifted_2(grad, "slab", -1)
-    diagonal = lax.ppermute(
-        grad,
-        ("slab", "filt"),
-        [(8 * s + y, 8 * s + y - 9) for s in range(1, 64) for y in range(1, 8)],
-    )
     tiles = exchange(part.reshape(16, 8, 3456), ("slab", "filt"), WIDE)
-    tiles, right, upper, diagonal = lax.optimization_barrier((tiles, right, upper, diagonal))
+    tiles, right = lax.optimization_barrier((tiles, right))
+    own = jnp.stack([grad, right])
+    upper = shifted_2(own, "slab", -1)
+    tiles = exchange(add_up(tiles, 16), ("slab", "filt"), FAR)
+    tiles, upper = lax.optimization_barrier((tiles, upper))
     tiles = add_up(tiles, 16)
-    tiles = add_up(exchange(tiles, ("slab", "filt"), FAR), 16)
+
     in_grad = call(
-        input_body, shape((2, 2, 128, 256), BF16), [VMEM] * 5, (226 * mb, 3 * mb)
-    )(grad, right, upper, diagonal, taps)
+        input_body, shape((2, 2, 128, 256), BF16), [VMEM] * 3, (226 * mb, 3 * mb)
+    )(own, upper, taps)
     in_grad = in_grad.transpose(0, 2, 1, 3)
 
     tiles = exchange(tiles, "slab", NEAR)

time: 101 us -> 101 us (level)
  blocking collectives: 39.6 us -> 20.3 us
  waiting for transfers between devices: 18.6 us -> 27.9 us
  starting transfers between devices: 31.5 us -> 39.9 us
    all_to_all x2 -> x1, blocking collectives: 39.6 us -> 20.3 us  [exchange(): lax.all_to_all(value, axis, split_axis=0, concat_axis=0, axis_index_group...]
    ppermute x3, waiting for transfers between devices: 1.49 us -> 19.5 us  [shifted_2(): lax.ppermute(value, axis, [(source, source + steps) for source in range(f...]
    ppermute x1 -> x0, waiting for transfers between devices: 9.97 us -> none  [on_device(): lax.ppermute(grad, ('slab', 'filt'), [(8 * s + y, 8 * s + y - 9) for s in...]
    all_to_all x2 -> x3, starting transfers between devices: 16.2 us -> 24.7 us  [exchange(): lax.all_to_all(value, axis, split_axis=0, concat_axis=0, axis_index_group...]
    ppermute x1 -> x0, starting transfers between devices: 1.29 us -> none  [on_device(): lax.ppermute(grad, ('slab', 'filt'), [(8 * s + y, 8 * s + y - 9) for s in...]
    all_to_all x2 -> x3, waiting for transfers between devices: 4.73 us -> 6 us  [exchange(): lax.all_to_all(value, axis, split_axis=0, concat_axis=0, axis_index_group...]
    ppermute x3, starting transfers between devices: 12.1 us -> 13.3 us  [shifted_2(): lax.ppermute(value, axis, [(source, source + steps) for source in range(f...]
  transfers between devices with their start and end apart: 7 -> 7, of which waited for: 4 -> 6; matrix products, arithmetic and copies ran while one was open for 1% -> 1% of each run, Pallas kernels for 2% -> 2%
where the time goes in v14:
time: 101 us; the launch traced here: 100 us
  starting transfers between devices  39.9 us (40%)
  waiting for transfers between devices  27.9 us (28%)
  blocking collectives  20.3 us (20%)
  Pallas kernels  10.1 us (10%)
    all_to_all x3, starting transfers between devices, exchange(): lax.all_to_all(value, axis, split_axis=0, concat_axis=0, axis_index_group...  24.7 us
    all_to_all x1, blocking collectives, exchange(): lax.all_to_all(value, axis, split_axis=0, concat_axis=0, axis_index_group...  20.3 us
    ppermute x3, waiting for transfers between devices, shifted_2(): lax.ppermute(value, axis, [(source, source + steps) for source in range(f...  19.5 us
    ppermute x3, starting transfers between devices, shifted_2(): lax.ppermute(value, axis, [(source, source + steps) for source in range(f...  13.3 us
    all_to_all x3, waiting for transfers between devices, exchange(): lax.all_to_all(value, axis, split_axis=0, concat_axis=0, axis_index_group...  6 us
    pallas_call x1, Pallas kernels, on_device(): call(pack_body, shape((8, 7, 16, 256), BF16), [ANY] * 2, (2 * mb, mb), [p...  2.5 us
    ppermute x1, waiting for transfers between devices, on_device(): other = lax.ppermute(part, 'slab', CORE_PAIRS)  2.39 us
  transfers between devices with their start and end apart: 7, of which 6 were waited for; matrix products, arithmetic and copies ran while one was open for 1% of the time, Pallas kernels for 2%

profile of v14, /device:TPU:1, one launch (start us, length us, event | category | flops | bytes accessed | tf_op | source)
XLA Modules:
  0.0 100.0 jit_solution(3330904543758498509)
XLA Ops:
  0.6 2.5 %shard_map.50 = bf16[8,7,16,256]{3,2,1,0:T(8,128)(2,1)} custom-call(bf16[2,16,16,256]{3,2,1,0:T(8,128)(2,1)} %vol_hbm.1, bf16[1,32,8,128]{3,2,1,0:T(8,128)(2,1)} %err_hbm.1), custom_call_target="tpu_custom_call" | custom-call | flops 2097152 | bytes 1048576 | tf_op jit(solution)/shard_map/pallas_call | solution.py:236
  3.1 20.3 %all_to_all.20.rec_ref = bf16[8,7,16,256]{3,2,1,0:T(8,128)(2,1)S(1)} all-to-all(bf16[8,7,16,256]{3,2,1,0:T(8,128)(2,1)} %shard_map.50), channel_id=1, replica_groups=mesh['slab'=64,'filt'=8] {'filt'}, dimensions={0} | all-to-all | bytes 917504 | tf_op jit(solution)/shard_map/all_to_all | solution.py:219
  23.5 8.3 %collective-permute-start = (bf16[8,3,16,256]{3,2,1,0:T(8,128)(2,1)S(1)}, bf16[8,3,16,256]{3,2,1,0:T(8,128)(2,1)S(1)}, u32[]{:S(2)}, u32[]{:S(2)}) collective-permute-start(bf16[8,3,16,256]{3,2,1,0:T(8,128)(2,1)S(1)} %slice.4), channel_id=1, source_target_pairs={{0,8},{8,16},{16,24},{24,32},{32,40},{40,48},{48,56},{56,64},{64,7... | collective-permute-start | bytes 589832 | tf_op jit(solution)/shard_map/ppermute | solution.py:215
  31.8 1.1 %shard_map.51 = (bf16[256,1152]{1,0:T(8,128)(2,1)S(1)}, bf16[512,1152]{1,0:T(8,128)(2,1)S(1)}) custom-call(bf16[9,3,128,256]{3,2,1,0:T(8,128)(2,1)S(1)} %bitcast.9), custom_call_target="tpu_custom_call" | custom-call | flops 473956352 | bytes 4194304 | tf_op jit(solution)/shard_map/pallas_call | solution.py:249
  32.9 1.5 %collective-permute-done.rim_ref = bf16[8,3,16,256]{3,2,1,0:T(8,128)(2,1)S(1)} collective-permute-done((bf16[8,3,16,256]{3,2,1,0:T(8,128)(2,1)S(1)}, bf16[8,3,16,256]{3,2,1,0:T(8,128)(2,1)S(1)}, u32[]{:S(2)}, u32[]{:S(2)}) %collective-permute-start) | collective-permute-done | bytes 196640 | tf_op jit(solution)/shard_map/ppermute | solution.py:215
  34.4 1.5 %shard_map.52 = (bf16[256,128]{1,0:T(8,128)(2,1)S(1)}, bf16[256,256]{1,0:T(8,128)(2,1)S(1)}, bf16[1152,128]{1,0:T(8,128)(2,1)S(1)}, bf16[1152,128]{1,0:T(8,128)(2,1)S(1)}, bf16[128,3456]{1,0:T(8,128)(2,1)S(1)}) custom-call(s32[1]{0:T(128)} %bitcast.core_ref, bf16[8,7,16,256]{3,2,1,0:T(8,128)(2,1)S(1)} %all_to_all.20.rec_ref, ...), custom_call_target="tpu_custom_call" | custom-call | flops 475004928 | bytes 4194304 | tf_op jit(solution)/shard_map/pallas_call | solution.py:254
  35.8 1.9 %collective-permute-start.1 = (bf16[128,3456]{1,0:T(8,128)(2,1)S(1)}, bf16[128,3456]{1,0:T(8,128)(2,1)S(1)}, u32[]{:S(2)}, u32[]{:S(2)}) collective-permute-start(bf16[128,3456]{1,0:T(8,128)(2,1)S(1)} %get-tuple-element.19), channel_id=1, source_target_pairs={{0,8},{8,0},{16,24},{24,16},{32,40},{40,32},{48,56},{56,48},{64,72... | collective-permute-start | bytes 2654216 | tf_op jit(solution)/shard_map/ppermute | solution.py:261
  37.7 2.4 %collective-permute-done.1.other_ref = bf16[128,3456]{1,0:T(8,128)(2,1)S(1)} collective-permute-done((bf16[128,3456]{1,0:T(8,128)(2,1)S(1)}, bf16[128,3456]{1,0:T(8,128)(2,1)S(1)}, u32[]{:S(2)}, u32[]{:S(2)}) %collective-permute-start.1) | collective-permute-done | bytes 884768 | tf_op jit(solution)/shard_map/ppermute | solution.py:261
  40.1 1.3 %shard_map.53 = bf16[128,3456]{1,0:T(8,128)(2,1)} custom-call(s32[1]{0:T(128)} %bitcast.core_ref, bf16[256,256]{1,0:T(8,128)(2,1)S(1)} %get-tuple-element.16.both_ref, bf16[1152,128]{1,0:T(8,128)(2,1)S(1)} %get-tuple-element.17.ze, bf16[1152,128]{1,0:T(8,128)(2,1)S(1)} %get-tuple-element.18.zo, bf16[128,3456]{1,0:T(8,128)(2,1)S(1)} %collective-permute-done.1.other_ref), custom_call_target="tpu_custom_call" | custom-call | flops 118489088 | bytes 3145728 | tf_op jit(solution)/shard_map/pallas_call | solution.py:263
  41.5 9.2 %all-to-all-start.1 = ((bf16[16,8,3456]{2,1,0:T(8,128)(2,1)}), bf16[16,8,3456]{2,1,0:T(8,128)(2,1)S(1)}, u32[]{:S(2)}, u32[]{:S(2)}) async-start(bf16[16,8,3456]{2,1,0:T(8,128)(2,1)} %bitcast.3), calls=%async_computation.1 | async-start | bytes 1769472 | tf_op jit(solution)/shard_map/all_to_all | solution.py:219
  50.6 1.3 %collective-permute-start.2 = (bf16[256,128]{1,0:T(8,128)(2,1)S(1)}, bf16[256,128]{1,0:T(8,128)(2,1)S(1)}, u32[]{:S(2)}, u32[]{:S(2)}) collective-permute-start(bf16[256,128]{1,0:T(8,128)(2,1)S(1)} %get-tuple-element.15), channel_id=1, source_target_pairs={{1,0},{2,1},{3,2},{4,3},{5,4},{6,5},{7,6},{9,8},{10,9},{11,10},{12... | collective-permute-start | bytes 196616 | tf_op jit(solution)/shard_map/ppermute | solution.py:215
  51.9 11.5 %collective-permute-done.2 = bf16[256,128]{1,0:T(8,128)(2,1)S(1)} collective-permute-done((bf16[256,128]{1,0:T(8,128)(2,1)S(1)}, bf16[256,128]{1,0:T(8,128)(2,1)S(1)}, u32[]{:S(2)}, u32[]{:S(2)}) %collective-permute-start.2) | collective-permute-done | bytes 65568 | tf_op jit(solution)/shard_map/ppermute | solution.py:215
  63.4 0.0 all-to-all-done.1.in_ref
  63.5 0.8 shard_map.54
  64.3 7.3 %all-to-all-start.2 = ((bf16[16,2,3456]{2,1,0:T(2,128)(2,1)}), bf16[16,2,3456]{2,1,0:T(2,128)(2,1)S(1)}, u32[]{:S(2)}, u32[]{:S(2)}) async-start(bf16[16,2,3456]{2,1,0:T(2,128)(2,1)} %shard_map.54), calls=%async_computation.2 | async-start | bytes 442368 | tf_op jit(solution)/shard_map/all_to_all | solution.py:219
  71.6 3.7 %collective-permute-start.3 = (bf16[2,256,128]{2,1,0:T(8,128)(2,1)S(1)}, bf16[2,256,128]{2,1,0:T(8,128)(2,1)S(1)}, u32[]{:S(2)}, u32[]{:S(2)}) collective-permute-start(bf16[2,256,128]{2,1,0:T(8,128)(2,1)S(1)} %pad_maximum_fusion.own_ref), channel_id=1, source_target_pairs={{8,0},{16,8},{24,16},{32,24},{40,32},{48,40},{56,48},{64,56},{72,6... | collective-permute-start | bytes 393224 | tf_op jit(solution)/shard_map/ppermute | solution.py:215
  75.3 6.5 %collective-permute-done.3.up_ref = bf16[2,256,128]{2,1,0:T(8,128)(2,1)S(1)} collective-permute-done((bf16[2,256,128]{2,1,0:T(8,128)(2,1)S(1)}, bf16[2,256,128]{2,1,0:T(8,128)(2,1)S(1)}, u32[]{:S(2)}, u32[]{:S(2)}) %collective-permute-start.3) | collective-permute-done | bytes 131104 | tf_op jit(solution)/shard_map/ppermute | solution.py:215
  81.8 1.3 %all-to-all-done.2.in_ref = bf16[16,2,3456]{2,1,0:T(2,128)(2,1)S(1)} async-done(((bf16[16,2,3456]{2,1,0:T(2,128)(2,1)}), bf16[16,2,3456]{2,1,0:T(2,128)(2,1)S(1)}, u32[]{:S(2)}, u32[]{:S(2)}) %all-to-all-start.2) | async-done | bytes 221216 | tf_op jit(solution)/shard_map/all_to_all | solution.py:219
  83.1 0.7 shard_map.56
  83.9 8.3 %all-to-all-start.3 = ((bf16[16,2,3456]{2,1,0:T(2,128)(2,1)}), bf16[16,2,3456]{2,1,0:T(2,128)(2,1)S(1)}, u32[]{:S(2)}, u32[]{:S(2)}) async-start(bf16[16,2,3456]{2,1,0:T(2,128)(2,1)} %shard_map.56), calls=%async_computation.3 | async-start | bytes 442368 | tf_op jit(solution)/shard_map/all_to_all | solution.py:219
  92.1 1.2 %shard_map.55 = bf16[2,2,128,256]{3,2,1,0:T(8,128)(2,1)S(1)} custom-call(bf16[2,256,128]{2,1,0:T(8,128)(2,1)S(1)} %pad_maximum_fusion.own_ref, bf16[2,256,128]{2,1,0:T(8,128)(2,1)S(1)} %collective-permute-done.3.up_ref, bf16[9,3,128,256]{3,2,1,0:T(8,128)(2,1)S(1)} %bitcast.10), custom_call_target="tpu_custom_call" | custom-call | flops 236978176 | bytes 3145728 | tf_op jit(solution)/shard_map/pallas_call | solution.py:280
  93.3 1.0 copy.5
  94.3 4.7 %all-to-all-done.3.in_ref = bf16[16,2,3456]{2,1,0:T(2,128)(2,1)S(1)} async-done(((bf16[16,2,3456]{2,1,0:T(2,128)(2,1)}), bf16[16,2,3456]{2,1,0:T(2,128)(2,1)S(1)}, u32[]{:S(2)}, u32[]{:S(2)}) %all-to-all-start.3) | async-done | bytes 221216 | tf_op jit(solution)/shard_map/all_to_all | solution.py:219
  99.0 1.0 shard_map.57
  (4 shorter events, 0.0 us)
Async XLA Ops:
  0.6 31.1 %copy-start = (bf16[3,3,3,128,256]{4,3,2,1,0:T(8,128)(2,1)S(1)}, bf16[3,3,3,128,256]{4,3,2,1,0:T(8,128)(2,1)}, u32[]{:S(2)}) copy-start(bf16[3,3,3,128,256]{4,3,2,1,0:T(8,128)(2,1)} %param.4) | copy-start | bytes 5308420
  23.5 10.9 %collective-permute-start = (bf16[8,3,16,256]{3,2,1,0:T(8,128)(2,1)S(1)}, bf16[8,3,16,256]{3,2,1,0:T(8,128)(2,1)S(1)}, u32[]{:S(2)}, u32[]{:S(2)}) collective-permute-start(bf16[8,3,16,256]{3,2,1,0:T(8,128)(2,1)S(1)} %slice.4), channel_id=1, source_target_pairs={{0,8},{8,16},{16,24},{24,32},{32,40},{40,48},{48,56},{56,64},{64,7... | collective-permute-start | bytes 589832 | tf_op jit(solution)/shard_map/ppermute | solution.py:215
  35.8 4.3 %collective-permute-start.1 = (bf16[128,3456]{1,0:T(8,128)(2,1)S(1)}, bf16[128,3456]{1,0:T(8,128)(2,1)S(1)}, u32[]{:S(2)}, u32[]{:S(2)}) collective-permute-start(bf16[128,3456]{1,0:T(8,128)(2,1)S(1)} %get-tuple-element.19), channel_id=1, source_target_pairs={{0,8},{8,0},{16,24},{24,16},{32,40},{40,32},{48,56},{56,48},{64,72... | collective-permute-start | bytes 2654216 | tf_op jit(solution)/shard_map/ppermute | solution.py:261
  41.5 22.0 %all-to-all-start.1 = ((bf16[16,8,3456]{2,1,0:T(8,128)(2,1)}), bf16[16,8,3456]{2,1,0:T(8,128)(2,1)S(1)}, u32[]{:S(2)}, u32[]{:S(2)}) async-start(bf16[16,8,3456]{2,1,0:T(8,128)(2,1)} %bitcast.3), calls=%async_computation.1 | async-start | bytes 1769472 | tf_op jit(solution)/shard_map/all_to_all | solution.py:219
  50.6 12.8 %collective-permute-start.2 = (bf16[256,128]{1,0:T(8,128)(2,1)S(1)}, bf16[256,128]{1,0:T(8,128)(2,1)S(1)}, u32[]{:S(2)}, u32[]{:S(2)}) collective-permute-start(bf16[256,128]{1,0:T(8,128)(2,1)S(1)} %get-tuple-element.15), channel_id=1, source_target_pairs={{1,0},{2,1},{3,2},{4,3},{5,4},{6,5},{7,6},{9,8},{10,9},{11,10},{12... | collective-permute-start | bytes 196616 | tf_op jit(solution)/shard_map/ppermute | solution.py:215
  64.3 18.9 %all-to-all-start.2 = ((bf16[16,2,3456]{2,1,0:T(2,128)(2,1)}), bf16[16,2,3456]{2,1,0:T(2,128)(2,1)S(1)}, u32[]{:S(2)}, u32[]{:S(2)}) async-start(bf16[16,2,3456]{2,1,0:T(2,128)(2,1)} %shard_map.54), calls=%async_computation.2 | async-start | bytes 442368 | tf_op jit(solution)/shard_map/all_to_all | solution.py:219
  71.6 10.2 %collective-permute-start.3 = (bf16[2,256,128]{2,1,0:T(8,128)(2,1)S(1)}, bf16[2,256,128]{2,1,0:T(8,128)(2,1)S(1)}, u32[]{:S(2)}, u32[]{:S(2)}) collective-permute-start(bf16[2,256,128]{2,1,0:T(8,128)(2,1)S(1)} %pad_maximum_fusion.own_ref), channel_id=1, source_target_pairs={{8,0},{16,8},{24,16},{32,24},{40,32},{48,40},{56,48},{64,56},{72,6... | collective-permute-start | bytes 393224 | tf_op jit(solution)/shard_map/ppermute | solution.py:215
  83.9 15.1 %all-to-all-start.3 = ((bf16[16,2,3456]{2,1,0:T(2,128)(2,1)}), bf16[16,2,3456]{2,1,0:T(2,128)(2,1)S(1)}, u32[]{:S(2)}, u32[]{:S(2)}) async-start(bf16[16,2,3456]{2,1,0:T(2,128)(2,1)} %shard_map.56), calls=%async_computation.3 | async-start | bytes 442368 | tf_op jit(solution)/shard_map/all_to_all | solution.py:219

commit v15 on v13

--- a/solution.py
+++ b/solution.py
@@ -40,13 +40,13 @@
 CORE_PAIRS = [(s, s ^ 1) for s in range(64)]
 
 
-def call(body, out_shape, in_specs, cost, scratch=(), limit=LIMIT, out_spec=VMEM):
+def call(body, out_shape, in_specs, cost, scratch=(), limit=LIMIT):
     many = isinstance(out_shape, (tuple, list))
     return pl.pallas_call(
         body,
         out_shape=out_shape,
         in_specs=in_specs,
-        out_specs=[out_spec] * len(out_shape) if many else out_spec,
+        out_specs=[VMEM] * len(out_shape) if many else VMEM,
         scratch_shapes=list(scratch),
         compiler_params=pltpu.CompilerParams(vmem_limit_bytes=limit),
         cost_estimate=pl.CostEstimate(flops=cost[0], bytes_accessed=cost[1], transcendentals=0),
@@ -154,20 +154,11 @@
         part_ref[:, c * 1152 : c * 1152 + 1152] = parts[c].astype(BF16)
 
 
-def keep_body(core_ref, both_ref, ze, zo, other_ref, part_hbm, part_ref, sems):
-    order = core_rows(core_ref[0])
-    both = both_ref[...]
-    now = mm(order, both[:, :128]).astype(BF16)
-    after = mm(order, both[:, 128:]).astype(BF16)
-    copies = []
-    for c, (grad, stack) in enumerate(((after, zo), (now, ze), (now, zo))):
-        cols = pl.ds(c * 1152, 1152)
-        total = mm_nt(grad, stack[...]) + other_ref[:, cols].astype(F32)
-        part_ref[:, cols] = total.astype(BF16)
-        copies.append(pltpu.make_async_copy(part_ref.at[:, cols], part_hbm.at[:, cols], sems.at[c]))
-        copies[-1].start()
-    for copy in copies:
-        copy.wait()
+def keep_body(core_ref, both_ref, ze, zo, other_ref, part_ref):
+    parts = taps_of(core_rows(core_ref[0]), both_ref[...], ze, zo)
+    for c in range(3):
+        cols = slice(c * 1152, c * 1152 + 1152)
+        part_ref[:, cols] = (parts[c] + other_ref[:, cols].astype(F32)).astype(BF16)
 
 
 def sum_body(in_ref, out_ref):
@@ -260,13 +251,7 @@
 
     other = lax.ppermute(part, "slab", CORE_PAIRS)
     part = call(
-        keep_body,
-        shape((128, 3456), BF16),
-        [SMEM, VMEM, VMEM, VMEM, VMEM],
-        (113 * mb, 3 * mb),
-        [pltpu.VMEM((128, 3456), BF16), pltpu.SemaphoreType.DMA((3,))],
-        LIMIT,
-        ANY,
+        keep_body, shape((128, 3456), BF16), [SMEM, VMEM, VMEM, VMEM, VMEM], (113 * mb, 3 * mb)
     )(core, both, ze, zo, other)
     tiles = exchange(part.reshape(16, 8, 3456), ("slab", "filt"), WIDE)
     tiles, late = lax.optimization_barrier((tiles, grad))

time: 100 us -> 99.8 us (level)
  no operation moved by 1% of the time
where the time goes in v15:
time: 99.8 us; the launch traced here: 98.5 us
  blocking collectives  41.2 us (41%)
  starting transfers between devices  33.1 us (33%)
  waiting for transfers between devices  13.2 us (13%)
  Pallas kernels  9.23 us (9%)
    all_to_all x2, blocking collectives, exchange(): lax.all_to_all(value, axis, split_axis=0, concat_axis=0, axis_index_group...  41.2 us
    all_to_all x2, starting transfers between devices, exchange(): lax.all_to_all(value, axis, split_axis=0, concat_axis=0, axis_index_group...  15.4 us
    ppermute x3, starting transfers between devices, shifted_2(): lax.ppermute(value, axis, [(source, source + steps) for source in range(f...  14.5 us
    all_to_all x2, waiting for transfers between devices, exchange(): lax.all_to_all(value, axis, split_axis=0, concat_axis=0, axis_index_group...  4.73 us
    ppermute x1, waiting for transfers between devices, on_device(): lax.ppermute(late, ('slab', 'filt'), [(8 * s + y, 8 * s + y - 9) for s in...  3.45 us
    ppermute x3, waiting for transfers between devices, shifted_2(): lax.ppermute(value, axis, [(source, source + steps) for source in range(f...  2.59 us
    pallas_call x1, Pallas kernels, on_device(): call(pack_body, shape((8, 7, 16, 256), BF16), [ANY] * 2, (2 * mb, mb), [p...  2.48 us
    ppermute x1, waiting for transfers between devices, on_device(): other = lax.ppermute(part, 'slab', CORE_PAIRS)  2.39 us
  transfers between devices with their start and end apart: 7, of which 5 were waited for; matrix products, arithmetic and copies ran while one was open for 1% of the time, Pallas kernels for 2%

profile of v15, /device:TPU:1, one launch (start us, length us, event | category | flops | bytes accessed | tf_op | source)
XLA Modules:
  0.0 98.5 jit_solution(13645322433446015131)
XLA Ops:
  0.6 2.5 %shard_map.50 = bf16[8,7,16,256]{3,2,1,0:T(8,128)(2,1)} custom-call(bf16[2,16,16,256]{3,2,1,0:T(8,128)(2,1)} %vol_hbm.1, bf16[1,32,8,128]{3,2,1,0:T(8,128)(2,1)} %err_hbm.1), custom_call_target="tpu_custom_call" | custom-call | flops 2097152 | bytes 1048576 | tf_op jit(solution)/shard_map/pallas_call | solution.py:227
  3.1 20.3 %all_to_all.20.rec_ref = bf16[8,7,16,256]{3,2,1,0:T(8,128)(2,1)S(1)} all-to-all(bf16[8,7,16,256]{3,2,1,0:T(8,128)(2,1)} %shard_map.50), channel_id=1, replica_groups=mesh['slab'=64,'filt'=8] {'filt'}, dimensions={0} | all-to-all | bytes 917504 | tf_op jit(solution)/shard_map/all_to_all | solution.py:210
  23.5 8.3 %collective-permute-start = (bf16[8,3,16,256]{3,2,1,0:T(8,128)(2,1)S(1)}, bf16[8,3,16,256]{3,2,1,0:T(8,128)(2,1)S(1)}, u32[]{:S(2)}, u32[]{:S(2)}) collective-permute-start(bf16[8,3,16,256]{3,2,1,0:T(8,128)(2,1)S(1)} %slice.4), channel_id=1, source_target_pairs={{0,8},{8,16},{16,24},{24,32},{32,40},{40,48},{48,56},{56,64},{64,7... | collective-permute-start | bytes 589832 | tf_op jit(solution)/shard_map/ppermute | solution.py:206
  31.8 1.1 %shard_map.51 = (bf16[256,1152]{1,0:T(8,128)(2,1)S(1)}, bf16[512,1152]{1,0:T(8,128)(2,1)S(1)}) custom-call(bf16[9,3,128,256]{3,2,1,0:T(8,128)(2,1)S(1)} %bitcast.7), custom_call_target="tpu_custom_call" | custom-call | flops 473956352 | bytes 4194304 | tf_op jit(solution)/shard_map/pallas_call | solution.py:240
  32.8 1.5 %collective-permute-done.rim_ref = bf16[8,3,16,256]{3,2,1,0:T(8,128)(2,1)S(1)} collective-permute-done((bf16[8,3,16,256]{3,2,1,0:T(8,128)(2,1)S(1)}, bf16[8,3,16,256]{3,2,1,0:T(8,128)(2,1)S(1)}, u32[]{:S(2)}, u32[]{:S(2)}) %collective-permute-start) | collective-permute-done | bytes 196640 | tf_op jit(solution)/shard_map/ppermute | solution.py:206
  34.3 1.5 %shard_map.52 = (bf16[256,128]{1,0:T(8,128)(2,1)S(1)}, bf16[256,256]{1,0:T(8,128)(2,1)S(1)}, bf16[1152,128]{1,0:T(8,128)(2,1)S(1)}, bf16[1152,128]{1,0:T(8,128)(2,1)S(1)}, bf16[128,3456]{1,0:T(8,128)(2,1)S(1)}) custom-call(s32[1]{0:T(128)} %bitcast.core_ref, bf16[8,7,16,256]{3,2,1,0:T(8,128)(2,1)S(1)} %all_to_all.20.rec_ref, ...), custom_call_target="tpu_custom_call" | custom-call | flops 475004928 | bytes 4194304 | tf_op jit(solution)/shard_map/pallas_call | solution.py:245
  35.8 1.9 %collective-permute-start.1 = (bf16[128,3456]{1,0:T(8,128)(2,1)S(1)}, bf16[128,3456]{1,0:T(8,128)(2,1)S(1)}, u32[]{:S(2)}, u32[]{:S(2)}) collective-permute-start(bf16[128,3456]{1,0:T(8,128)(2,1)S(1)} %get-tuple-element.21), channel_id=1, source_target_pairs={{0,8},{8,0},{16,24},{24,16},{32,40},{40,32},{48,56},{56,48},{64,72... | collective-permute-start | bytes 2654216 | tf_op jit(solution)/shard_map/ppermute | solution.py:252
  37.7 2.4 %collective-permute-done.1.other_ref = bf16[128,3456]{1,0:T(8,128)(2,1)S(1)} collective-permute-done((bf16[128,3456]{1,0:T(8,128)(2,1)S(1)}, bf16[128,3456]{1,0:T(8,128)(2,1)S(1)}, u32[]{:S(2)}, u32[]{:S(2)}) %collective-permute-start.1) | collective-permute-done | bytes 884768 | tf_op jit(solution)/shard_map/ppermute | solution.py:252
  40.1 0.5 shard_map.53
  40.6 20.9 %all_to_all.21.in_ref = bf16[16,8,3456]{2,1,0:T(8,128)(2,1)S(1)} all-to-all(bf16[16,8,3456]{2,1,0:T(8,128)(2,1)S(1)} %bitcast.9), channel_id=1, replica_groups={{0,1,16,17,128,129,144,145,256,257,272,273,384,385,400,401},{2,3,18,19,..., dimensions={0} | all-to-all | bytes 1769472 | tf_op jit(solution)/shard_map/all_to_all | solution.py:210
  61.5 0.8 shard_map.54
  62.4 7.3 %all-to-all-start.2 = ((bf16[16,2,3456]{2,1,0:T(2,128)(2,1)}), bf16[16,2,3456]{2,1,0:T(2,128)(2,1)S(1)}, u32[]{:S(2)}, u32[]{:S(2)}) async-start(bf16[16,2,3456]{2,1,0:T(2,128)(2,1)} %shard_map.54), calls=%async_computation.2 | async-start | bytes 442368 | tf_op jit(solution)/shard_map/all_to_all | solution.py:210
  69.7 1.3 %collective-permute-start.4 = (bf16[256,128]{1,0:T(8,128)(2,1)S(1)}, bf16[256,128]{1,0:T(8,128)(2,1)S(1)}, u32[]{:S(2)}, u32[]{:S(2)}) collective-permute-start(bf16[256,128]{1,0:T(8,128)(2,1)S(1)} %get-tuple-element.23.own_ref), channel_id=1, source_target_pairs={{9,0},{10,1},{11,2},{12,3},{13,4},{14,5},{15,6},{17,8},{18,9},{19,... | collective-permute-start | bytes 196616 | tf_op jit(solution)/shard_map/ppermute | solution.py:260
  71.0 4.9 %collective-permute-start.3 = (bf16[256,128]{1,0:T(8,128)(2,1)S(1)}, bf16[256,128]{1,0:T(8,128)(2,1)S(1)}, u32[]{:S(2)}, u32[]{:S(2)}) collective-permute-start(bf16[256,128]{1,0:T(8,128)(2,1)S(1)} %get-tuple-element.23.own_ref), channel_id=1, source_target_pairs={{8,0},{16,8},{24,16},{32,24},{40,32},{48,40},{56,48},{64,56},{72,6... | collective-permute-start | bytes 196616 | tf_op jit(solution)/shard_map/ppermute | solution.py:206
  75.9 1.3 %collective-permute-start.2 = (bf16[256,128]{1,0:T(8,128)(2,1)S(1)}, bf16[256,128]{1,0:T(8,128)(2,1)S(1)}, u32[]{:S(2)}, u32[]{:S(2)}) collective-permute-start(bf16[256,128]{1,0:T(8,128)(2,1)S(1)} %get-tuple-element.23.own_ref), channel_id=1, source_target_pairs={{1,0},{2,1},{3,2},{4,3},{5,4},{6,5},{7,6},{9,8},{10,9},{11,10},{12... | collective-permute-start | bytes 196616 | tf_op jit(solution)/shard_map/ppermute | solution.py:206
  77.2 3.4 %collective-permute-done.4.diag_ref = bf16[256,128]{1,0:T(8,128)(2,1)S(1)} collective-permute-done((bf16[256,128]{1,0:T(8,128)(2,1)S(1)}, bf16[256,128]{1,0:T(8,128)(2,1)S(1)}, u32[]{:S(2)}, u32[]{:S(2)}) %collective-permute-start.4) | collective-permute-done | bytes 65568 | tf_op jit(solution)/shard_map/ppermute | solution.py:260
  80.7 0.0 collective-permute-done.3.up_ref
  80.7 1.1 %collective-permute-done.2.right_ref = bf16[256,128]{1,0:T(8,128)(2,1)S(1)} collective-permute-done((bf16[256,128]{1,0:T(8,128)(2,1)S(1)}, bf16[256,128]{1,0:T(8,128)(2,1)S(1)}, u32[]{:S(2)}, u32[]{:S(2)}) %collective-permute-start.2) | collective-permute-done | bytes 65568 | tf_op jit(solution)/shard_map/ppermute | solution.py:206
  81.8 0.7 shard_map.56
  82.5 8.1 %all-to-all-start.3 = ((bf16[16,2,3456]{2,1,0:T(2,128)(2,1)}), bf16[16,2,3456]{2,1,0:T(2,128)(2,1)S(1)}, u32[]{:S(2)}, u32[]{:S(2)}) async-start(bf16[16,2,3456]{2,1,0:T(2,128)(2,1)} %shard_map.56), calls=%async_computation.3 | async-start | bytes 442368 | tf_op jit(solution)/shard_map/all_to_all | solution.py:210
  90.6 1.2 %shard_map.55 = bf16[2,2,128,256]{3,2,1,0:T(8,128)(2,1)S(1)} custom-call(bf16[256,128]{1,0:T(8,128)(2,1)S(1)} %get-tuple-element.23.own_ref, bf16[256,128]{1,0:T(8,128)(2,1)S(1)} %collective-permute-done.2.right_ref, bf16[256,128]{1,0:T(8,128)(2,1)S(1)} %collective-permute-done.3.up_ref, bf16[256,128]{1,0:T(8,128)(2,1)S(1)} %collective-permute-done.4.diag_ref, ...), custom_call_target="tpu_custom_call" | custom-call | flops 236978176 | bytes 3145728 | tf_op jit(solution)/shard_map/pallas_call | solution.py:269
  91.8 1.0 copy.5
  92.8 4.7 %all-to-all-done.3.in_ref = bf16[16,2,3456]{2,1,0:T(2,128)(2,1)S(1)} async-done(((bf16[16,2,3456]{2,1,0:T(2,128)(2,1)}), bf16[16,2,3456]{2,1,0:T(2,128)(2,1)S(1)}, u32[]{:S(2)}, u32[]{:S(2)}) %all-to-all-start.3) | async-done | bytes 221216 | tf_op jit(solution)/shard_map/all_to_all | solution.py:210
  97.5 1.0 shard_map.57
  (4 shorter events, 0.0 us)
Async XLA Ops:
  0.6 31.1 %copy-start = (bf16[3,3,3,128,256]{4,3,2,1,0:T(8,128)(2,1)S(1)}, bf16[3,3,3,128,256]{4,3,2,1,0:T(8,128)(2,1)}, u32[]{:S(2)}) copy-start(bf16[3,3,3,128,256]{4,3,2,1,0:T(8,128)(2,1)} %param.4) | copy-start | bytes 5308420
  23.5 10.9 %collective-permute-start = (bf16[8,3,16,256]{3,2,1,0:T(8,128)(2,1)S(1)}, bf16[8,3,16,256]{3,2,1,0:T(8,128)(2,1)S(1)}, u32[]{:S(2)}, u32[]{:S(2)}) collective-permute-start(bf16[8,3,16,256]{3,2,1,0:T(8,128)(2,1)S(1)} %slice.4), channel_id=1, source_target_pairs={{0,8},{8,16},{16,24},{24,32},{32,40},{40,48},{48,56},{56,64},{64,7... | collective-permute-start | bytes 589832 | tf_op jit(solution)/shard_map/ppermute | solution.py:206
  35.8 4.3 %collective-permute-start.1 = (bf16[128,3456]{1,0:T(8,128)(2,1)S(1)}, bf16[128,3456]{1,0:T(8,128)(2,1)S(1)}, u32[]{:S(2)}, u32[]{:S(2)}) collective-permute-start(bf16[128,3456]{1,0:T(8,128)(2,1)S(1)} %get-tuple-element.21), channel_id=1, source_target_pairs={{0,8},{8,0},{16,24},{24,16},{32,40},{40,32},{48,56},{56,48},{64,72... | collective-permute-start | bytes 2654216 | tf_op jit(solution)/shard_map/ppermute | solution.py:252
  62.4 19.4 %all-to-all-start.2 = ((bf16[16,2,3456]{2,1,0:T(2,128)(2,1)}), bf16[16,2,3456]{2,1,0:T(2,128)(2,1)S(1)}, u32[]{:S(2)}, u32[]{:S(2)}) async-start(bf16[16,2,3456]{2,1,0:T(2,128)(2,1)} %shard_map.54), calls=%async_computation.2 | async-start | bytes 442368 | tf_op jit(solution)/shard_map/all_to_all | solution.py:210
  69.7 11.0 %collective-permute-start.4 = (bf16[256,128]{1,0:T(8,128)(2,1)S(1)}, bf16[256,128]{1,0:T(8,128)(2,1)S(1)}, u32[]{:S(2)}, u32[]{:S(2)}) collective-permute-start(bf16[256,128]{1,0:T(8,128)(2,1)S(1)} %get-tuple-element.23.own_ref), channel_id=1, source_target_pairs={{9,0},{10,1},{11,2},{12,3},{13,4},{14,5},{15,6},{17,8},{18,9},{19,... | collective-permute-start | bytes 196616 | tf_op jit(solution)/shard_map/ppermute | solution.py:260
  71.0 9.7 %collective-permute-start.3 = (bf16[256,128]{1,0:T(8,128)(2,1)S(1)}, bf16[256,128]{1,0:T(8,128)(2,1)S(1)}, u32[]{:S(2)}, u32[]{:S(2)}) collective-permute-start(bf16[256,128]{1,0:T(8,128)(2,1)S(1)} %get-tuple-element.23.own_ref), channel_id=1, source_target_pairs={{8,0},{16,8},{24,16},{32,24},{40,32},{48,40},{56,48},{64,56},{72,6... | collective-permute-start | bytes 196616 | tf_op jit(solution)/shard_map/ppermute | solution.py:206
  75.9 5.9 %collective-permute-start.2 = (bf16[256,128]{1,0:T(8,128)(2,1)S(1)}, bf16[256,128]{1,0:T(8,128)(2,1)S(1)}, u32[]{:S(2)}, u32[]{:S(2)}) collective-permute-start(bf16[256,128]{1,0:T(8,128)(2,1)S(1)} %get-tuple-element.23.own_ref), channel_id=1, source_target_pairs={{1,0},{2,1},{3,2},{4,3},{5,4},{6,5},{7,6},{9,8},{10,9},{11,10},{12... | collective-permute-start | bytes 196616 | tf_op jit(solution)/shard_map/ppermute | solution.py:206
  82.5 14.9 %all-to-all-start.3 = ((bf16[16,2,3456]{2,1,0:T(2,128)(2,1)}), bf16[16,2,3456]{2,1,0:T(2,128)(2,1)S(1)}, u32[]{:S(2)}, u32[]{:S(2)}) async-start(bf16[16,2,3456]{2,1,0:T(2,128)(2,1)} %shard_map.56), calls=%async_computation.3 | async-start | bytes 442368 | tf_op jit(solution)/shard_map/all_to_all | solution.py:210

commit v16 on v15

--- a/solution.py
+++ b/solution.py
@@ -263,7 +263,7 @@
         [(8 * s + y, 8 * s + y - 9) for s in range(1, 64) for y in range(1, 8)],
     )
     tiles = exchange(add_up(tiles, 16), ("slab", "filt"), FAR)
-    tiles, right, upper, diagonal = lax.optimization_barrier((tiles, right, upper, diagonal))
+    tiles, upper, diagonal = lax.optimization_barrier((tiles, upper, diagonal))
     tiles = add_up(tiles, 16)
 
     in_grad = call(

time: 99.8 us -> 99 us (level)
    all_to_all x2, waiting for transfers between devices: 4.73 us -> 0.8 us  [exchange(): lax.all_to_all(value, axis, split_axis=0, concat_axis=0, axis_index_group...]
    ppermute x3, waiting for transfers between devices: 2.59 us -> 5.75 us  [shifted_2(): lax.ppermute(value, axis, [(source, source + steps) for source in range(f...]
    ppermute x1, waiting for transfers between devices: 3.45 us -> 4.75 us  [on_device(): lax.ppermute(late, ('slab', 'filt'), [(8 * s + y, 8 * s + y - 9) for s in...]
where the time goes in v16:
time: 99 us; the launch traced here: 98.5 us
  blocking collectives  41.2 us (42%)
  starting transfers between devices  32.6 us (33%)
  waiting for transfers between devices  13.7 us (14%)
  Pallas kernels  9.23 us (9%)
  local copies, waits for them, and re-layouts  0.99 us (1%)
    all_to_all x2, blocking collectives, exchange(): lax.all_to_all(value, axis, split_axis=0, concat_axis=0, axis_index_group...  41.2 us
    all_to_all x2, starting transfers between devices, exchange(): lax.all_to_all(value, axis, split_axis=0, concat_axis=0, axis_index_group...  15 us
    ppermute x3, starting transfers between devices, shifted_2(): lax.ppermute(value, axis, [(source, source + steps) for source in range(f...  14.5 us
    ppermute x3, waiting for transfers between devices, shifted_2(): lax.ppermute(value, axis, [(source, source + steps) for source in range(f...  5.75 us
    ppermute x1, waiting for transfers between devices, on_device(): lax.ppermute(late, ('slab', 'filt'), [(8 * s + y, 8 * s + y - 9) for s in...  4.75 us
    pallas_call x1, Pallas kernels, on_device(): call(pack_body, shape((8, 7, 16, 256), BF16), [ANY] * 2, (2 * mb, mb), [p...  2.48 us
    ppermute x1, waiting for transfers between devices, on_device(): other = lax.ppermute(part, 'slab', CORE_PAIRS)  2.39 us
  transfers between devices with their start and end apart: 7, of which 5 were waited for; matrix products, arithmetic and copies ran while one was open for 1% of the time, Pallas kernels for 2%

profile of v16, /device:TPU:1, one launch (start us, length us, event | category | flops | bytes accessed | tf_op | source)
XLA Modules:
  0.0 98.5 jit_solution(12846678411501937924)
XLA Ops:
  0.6 2.5 %shard_map.50 = bf16[8,7,16,256]{3,2,1,0:T(8,128)(2,1)} custom-call(bf16[2,16,16,256]{3,2,1,0:T(8,128)(2,1)} %vol_hbm.1, bf16[1,32,8,128]{3,2,1,0:T(8,128)(2,1)} %err_hbm.1), custom_call_target="tpu_custom_call" | custom-call | flops 2097152 | bytes 1048576 | tf_op jit(solution)/shard_map/pallas_call | solution.py:227
  3.1 20.3 %all_to_all.20.rec_ref = bf16[8,7,16,256]{3,2,1,0:T(8,128)(2,1)S(1)} all-to-all(bf16[8,7,16,256]{3,2,1,0:T(8,128)(2,1)} %shard_map.50), channel_id=1, replica_groups=mesh['slab'=64,'filt'=8] {'filt'}, dimensions={0} | all-to-all | bytes 917504 | tf_op jit(solution)/shard_map/all_to_all | solution.py:210
  23.5 8.3 %collective-permute-start = (bf16[8,3,16,256]{3,2,1,0:T(8,128)(2,1)S(1)}, bf16[8,3,16,256]{3,2,1,0:T(8,128)(2,1)S(1)}, u32[]{:S(2)}, u32[]{:S(2)}) collective-permute-start(bf16[8,3,16,256]{3,2,1,0:T(8,128)(2,1)S(1)} %slice.4), channel_id=1, source_target_pairs={{0,8},{8,16},{16,24},{24,32},{32,40},{40,48},{48,56},{56,64},{64,7... | collective-permute-start | bytes 589832 | tf_op jit(solution)/shard_map/ppermute | solution.py:206
  31.8 1.1 %shard_map.51 = (bf16[256,1152]{1,0:T(8,128)(2,1)S(1)}, bf16[512,1152]{1,0:T(8,128)(2,1)S(1)}) custom-call(bf16[9,3,128,256]{3,2,1,0:T(8,128)(2,1)S(1)} %bitcast.7), custom_call_target="tpu_custom_call" | custom-call | flops 473956352 | bytes 4194304 | tf_op jit(solution)/shard_map/pallas_call | solution.py:240
  32.8 1.5 %collective-permute-done.rim_ref = bf16[8,3,16,256]{3,2,1,0:T(8,128)(2,1)S(1)} collective-permute-done((bf16[8,3,16,256]{3,2,1,0:T(8,128)(2,1)S(1)}, bf16[8,3,16,256]{3,2,1,0:T(8,128)(2,1)S(1)}, u32[]{:S(2)}, u32[]{:S(2)}) %collective-permute-start) | collective-permute-done | bytes 196640 | tf_op jit(solution)/shard_map/ppermute | solution.py:206
  34.3 1.5 %shard_map.52 = (bf16[256,128]{1,0:T(8,128)(2,1)S(1)}, bf16[256,256]{1,0:T(8,128)(2,1)S(1)}, bf16[1152,128]{1,0:T(8,128)(2,1)S(1)}, bf16[1152,128]{1,0:T(8,128)(2,1)S(1)}, bf16[128,3456]{1,0:T(8,128)(2,1)S(1)}) custom-call(s32[1]{0:T(128)} %bitcast.core_ref, bf16[8,7,16,256]{3,2,1,0:T(8,128)(2,1)S(1)} %all_to_all.20.rec_ref, ...), custom_call_target="tpu_custom_call" | custom-call | flops 475004928 | bytes 4194304 | tf_op jit(solution)/shard_map/pallas_call | solution.py:245
  35.8 1.9 %collective-permute-start.1 = (bf16[128,3456]{1,0:T(8,128)(2,1)S(1)}, bf16[128,3456]{1,0:T(8,128)(2,1)S(1)}, u32[]{:S(2)}, u32[]{:S(2)}) collective-permute-start(bf16[128,3456]{1,0:T(8,128)(2,1)S(1)} %get-tuple-element.20), channel_id=1, source_target_pairs={{0,8},{8,0},{16,24},{24,16},{32,40},{40,32},{48,56},{56,48},{64,72... | collective-permute-start | bytes 2654216 | tf_op jit(solution)/shard_map/ppermute | solution.py:252
  37.7 2.4 %collective-permute-done.1.other_ref = bf16[128,3456]{1,0:T(8,128)(2,1)S(1)} collective-permute-done((bf16[128,3456]{1,0:T(8,128)(2,1)S(1)}, bf16[128,3456]{1,0:T(8,128)(2,1)S(1)}, u32[]{:S(2)}, u32[]{:S(2)}) %collective-permute-start.1) | collective-permute-done | bytes 884768 | tf_op jit(solution)/shard_map/ppermute | solution.py:252
  40.1 0.5 shard_map.53
  40.6 20.9 %all_to_all.21.in_ref = bf16[16,8,3456]{2,1,0:T(8,128)(2,1)S(1)} all-to-all(bf16[16,8,3456]{2,1,0:T(8,128)(2,1)S(1)} %bitcast.9), channel_id=1, replica_groups={{0,1,16,17,128,129,144,145,256,257,272,273,384,385,400,401},{2,3,18,19,..., dimensions={0} | all-to-all | bytes 1769472 | tf_op jit(solution)/shard_map/all_to_all | solution.py:210
  61.5 0.8 shard_map.54
  62.4 7.3 %all-to-all-start.2 = ((bf16[16,2,3456]{2,1,0:T(2,128)(2,1)}), bf16[16,2,3456]{2,1,0:T(2,128)(2,1)S(1)}, u32[]{:S(2)}, u32[]{:S(2)}) async-start(bf16[16,2,3456]{2,1,0:T(2,128)(2,1)} %shard_map.54), calls=%async_computation.2 | async-start | bytes 442368 | tf_op jit(solution)/shard_map/all_to_all | solution.py:210
  69.7 1.3 %collective-permute-start.4 = (bf16[256,128]{1,0:T(8,128)(2,1)S(1)}, bf16[256,128]{1,0:T(8,128)(2,1)S(1)}, u32[]{:S(2)}, u32[]{:S(2)}) collective-permute-start(bf16[256,128]{1,0:T(8,128)(2,1)S(1)} %get-tuple-element.21.own_ref), channel_id=1, source_target_pairs={{9,0},{10,1},{11,2},{12,3},{13,4},{14,5},{15,6},{17,8},{18,9},{19,... | collective-permute-start | bytes 196616 | tf_op jit(solution)/shard_map/ppermute | solution.py:260
  71.0 4.9 %collective-permute-start.3 = (bf16[256,128]{1,0:T(8,128)(2,1)S(1)}, bf16[256,128]{1,0:T(8,128)(2,1)S(1)}, u32[]{:S(2)}, u32[]{:S(2)}) collective-permute-start(bf16[256,128]{1,0:T(8,128)(2,1)S(1)} %get-tuple-element.21.own_ref), channel_id=1, source_target_pairs={{8,0},{16,8},{24,16},{32,24},{40,32},{48,40},{56,48},{64,56},{72,6... | collective-permute-start | bytes 196616 | tf_op jit(solution)/shard_map/ppermute | solution.py:206
  75.9 4.7 %collective-permute-done.4.diag_ref = bf16[256,128]{1,0:T(8,128)(2,1)S(1)} collective-permute-done((bf16[256,128]{1,0:T(8,128)(2,1)S(1)}, bf16[256,128]{1,0:T(8,128)(2,1)S(1)}, u32[]{:S(2)}, u32[]{:S(2)}) %collective-permute-start.4) | collective-permute-done | bytes 65568 | tf_op jit(solution)/shard_map/ppermute | solution.py:260
  80.7 0.0 collective-permute-done.3.up_ref
  80.7 0.8 all-to-all-done.2.in_ref
  81.5 0.7 shard_map.56
  82.2 7.6 %all-to-all-start.3 = ((bf16[16,2,3456]{2,1,0:T(2,128)(2,1)}), bf16[16,2,3456]{2,1,0:T(2,128)(2,1)S(1)}, u32[]{:S(2)}, u32[]{:S(2)}) async-start(bf16[16,2,3456]{2,1,0:T(2,128)(2,1)} %shard_map.56), calls=%async_computation.3 | async-start | bytes 442368 | tf_op jit(solution)/shard_map/all_to_all | solution.py:210
  89.9 1.3 %collective-permute-start.2 = (bf16[256,128]{1,0:T(8,128)(2,1)S(1)}, bf16[256,128]{1,0:T(8,128)(2,1)S(1)}, u32[]{:S(2)}, u32[]{:S(2)}) collective-permute-start(bf16[256,128]{1,0:T(8,128)(2,1)S(1)} %get-tuple-element.21.own_ref), channel_id=1, source_target_pairs={{1,0},{2,1},{3,2},{4,3},{5,4},{6,5},{7,6},{9,8},{10,9},{11,10},{12... | collective-permute-start | bytes 196616 | tf_op jit(solution)/shard_map/ppermute | solution.py:206
  91.1 4.3 %collective-permute-done.2.right_ref = bf16[256,128]{1,0:T(8,128)(2,1)S(1)} collective-permute-done((bf16[256,128]{1,0:T(8,128)(2,1)S(1)}, bf16[256,128]{1,0:T(8,128)(2,1)S(1)}, u32[]{:S(2)}, u32[]{:S(2)}) %collective-permute-start.2) | collective-permute-done | bytes 65568 | tf_op jit(solution)/shard_map/ppermute | solution.py:206
  95.4 1.2 %shard_map.55 = bf16[2,2,128,256]{3,2,1,0:T(8,128)(2,1)S(1)} custom-call(bf16[256,128]{1,0:T(8,128)(2,1)S(1)} %get-tuple-element.21.own_ref, bf16[256,128]{1,0:T(8,128)(2,1)S(1)} %collective-permute-done.2.right_ref, bf16[256,128]{1,0:T(8,128)(2,1)S(1)} %collective-permute-done.3.up_ref, bf16[256,128]{1,0:T(8,128)(2,1)S(1)} %collective-permute-done.4.diag_ref, ...), custom_call_target="tpu_custom_call" | custom-call | flops 236978176 | bytes 3145728 | tf_op jit(solution)/shard_map/pallas_call | solution.py:269
  96.6 1.0 copy.5
  97.5 1.0 shard_map.57
  (4 shorter events, 0.0 us)
Async XLA Ops:
  0.6 31.1 %copy-start = (bf16[3,3,3,128,256]{4,3,2,1,0:T(8,128)(2,1)S(1)}, bf16[3,3,3,128,256]{4,3,2,1,0:T(8,128)(2,1)}, u32[]{:S(2)}) copy-start(bf16[3,3,3,128,256]{4,3,2,1,0:T(8,128)(2,1)} %param.4) | copy-start | bytes 5308420
  23.5 10.9 %collective-permute-start = (bf16[8,3,16,256]{3,2,1,0:T(8,128)(2,1)S(1)}, bf16[8,3,16,256]{3,2,1,0:T(8,128)(2,1)S(1)}, u32[]{:S(2)}, u32[]{:S(2)}) collective-permute-start(bf16[8,3,16,256]{3,2,1,0:T(8,128)(2,1)S(1)} %slice.4), channel_id=1, source_target_pairs={{0,8},{8,16},{16,24},{24,32},{32,40},{40,48},{48,56},{56,64},{64,7... | collective-permute-start | bytes 589832 | tf_op jit(solution)/shard_map/ppermute | solution.py:206
  35.8 4.3 %collective-permute-start.1 = (bf16[128,3456]{1,0:T(8,128)(2,1)S(1)}, bf16[128,3456]{1,0:T(8,128)(2,1)S(1)}, u32[]{:S(2)}, u32[]{:S(2)}) collective-permute-start(bf16[128,3456]{1,0:T(8,128)(2,1)S(1)} %get-tuple-element.20), channel_id=1, source_target_pairs={{0,8},{8,0},{16,24},{24,16},{32,40},{40,32},{48,56},{56,48},{64,72... | collective-permute-start | bytes 2654216 | tf_op jit(solution)/shard_map/ppermute | solution.py:252
  62.4 19.1 %all-to-all-start.2 = ((bf16[16,2,3456]{2,1,0:T(2,128)(2,1)}), bf16[16,2,3456]{2,1,0:T(2,128)(2,1)S(1)}, u32[]{:S(2)}, u32[]{:S(2)}) async-start(bf16[16,2,3456]{2,1,0:T(2,128)(2,1)} %shard_map.54), calls=%async_computation.2 | async-start | bytes 442368 | tf_op jit(solution)/shard_map/all_to_all | solution.py:210
  69.7 11.0 %collective-permute-start.4 = (bf16[256,128]{1,0:T(8,128)(2,1)S(1)}, bf16[256,128]{1,0:T(8,128)(2,1)S(1)}, u32[]{:S(2)}, u32[]{:S(2)}) collective-permute-start(bf16[256,128]{1,0:T(8,128)(2,1)S(1)} %get-tuple-element.21.own_ref), channel_id=1, source_target_pairs={{9,0},{10,1},{11,2},{12,3},{13,4},{14,5},{15,6},{17,8},{18,9},{19,... | collective-permute-start | bytes 196616 | tf_op jit(solution)/shard_map/ppermute | solution.py:260
  71.0 9.7 %collective-permute-start.3 = (bf16[256,128]{1,0:T(8,128)(2,1)S(1)}, bf16[256,128]{1,0:T(8,128)(2,1)S(1)}, u32[]{:S(2)}, u32[]{:S(2)}) collective-permute-start(bf16[256,128]{1,0:T(8,128)(2,1)S(1)} %get-tuple-element.21.own_ref), channel_id=1, source_target_pairs={{8,0},{16,8},{24,16},{32,24},{40,32},{48,40},{56,48},{64,56},{72,6... | collective-permute-start | bytes 196616 | tf_op jit(solution)/shard_map/ppermute | solution.py:206
  82.2 15.3 %all-to-all-start.3 = ((bf16[16,2,3456]{2,1,0:T(2,128)(2,1)}), bf16[16,2,3456]{2,1,0:T(2,128)(2,1)S(1)}, u32[]{:S(2)}, u32[]{:S(2)}) async-start(bf16[16,2,3456]{2,1,0:T(2,128)(2,1)} %shard_map.56), calls=%async_computation.3 | async-start | bytes 442368 | tf_op jit(solution)/shard_map/all_to_all | solution.py:210
  89.9 5.5 %collective-permute-start.2 = (bf16[256,128]{1,0:T(8,128)(2,1)S(1)}, bf16[256,128]{1,0:T(8,128)(2,1)S(1)}, u32[]{:S(2)}, u32[]{:S(2)}) collective-permute-start(bf16[256,128]{1,0:T(8,128)(2,1)S(1)} %get-tuple-element.21.own_ref), channel_id=1, source_target_pairs={{1,0},{2,1},{3,2},{4,3},{5,4},{6,5},{7,6},{9,8},{10,9},{11,10},{12... | collective-permute-start | bytes 196616 | tf_op jit(solution)/shard_map/ppermute | solution.py:206

commit v17 on v16

--- a/solution.py
+++ b/solution.py
@@ -186,6 +186,7 @@
     taps = (((1, 0),), ((2, 0), (0, 1)))
     grads = ((own_ref[...], right_ref[...]), (up_ref[...], diag_ref[...]))
     for ed in range(2):
+        rows = []
         for er in range(2):
             sums = []
             for c in range(3):
@@ -197,7 +198,8 @@
                 sums.append(total)
             nxt = jnp.where(lane == 127, 0.0, pltpu.roll(sums[0], 127, 1))
             both = jnp.concatenate([sums[1].astype(BF16), (sums[2] + nxt).astype(BF16)], 1)
-            out_ref[ed, er] = mm(both, weave).astype(BF16)
+            rows.append(mm(both, weave))
+        out_ref[ed] = jnp.stack(rows, 1).astype(BF16)
 
 
 def shifted_2(value, axis, steps):
@@ -267,9 +269,8 @@
     tiles = add_up(tiles, 16)
 
     in_grad = call(
-        input_body, shape((2, 2, 128, 256), BF16), [VMEM] * 5, (226 * mb, 3 * mb)
+        input_body, shape((2, 128, 2, 256), BF16), [VMEM] * 5, (226 * mb, 3 * mb)
     )(grad, right, upper, diagonal, taps)
-    in_grad = in_grad.transpose(0, 2, 1, 3)
 
     tiles = exchange(tiles, "slab", NEAR)
     out = call(last_body, shape((27, 32, 128), F32), [VMEM], (mb, mb))(tiles)

time: 99 us -> 99.1 us (level)
  Pallas kernels: 9.23 us -> 10.3 us
    pallas_call x1, Pallas kernels: 1.16 us -> 2.22 us  [on_device(): call(input_body, shape((2, 128, 2, 256), BF16), [VMEM] * 5, (226 * mb, 3...]
  transfers between devices with their start and end apart: 7 -> 7, of which waited for: 5 -> 5; matrix products, arithmetic and copies ran while one was open for 1% -> 0% of each run, Pallas kernels for 2% -> 3%
where the time goes in v17:
time: 99.1 us; the launch traced here: 98.6 us
  blocking collectives  41.2 us (42%)
  starting transfers between devices  32.6 us (33%)
  waiting for transfers between devices  13.7 us (14%)
  Pallas kernels  10.3 us (10%)
    all_to_all x2, blocking collectives, exchange(): lax.all_to_all(value, axis, split_axis=0, concat_axis=0, axis_index_group...  41.2 us
    all_to_all x2, starting transfers between devices, exchange(): lax.all_to_all(value, axis, split_axis=0, concat_axis=0, axis_index_group...  15 us
    ppermute x3, starting transfers between devices, shifted_2(): lax.ppermute(value, axis, [(source, source + steps) for source in range(f...  14.5 us
    ppermute x3, waiting for transfers between devices, shifted_2(): lax.ppermute(value, axis, [(source, source + steps) for source in range(f...  5.75 us
    ppermute x1, waiting for transfers between devices, on_device(): lax.ppermute(late, ('slab', 'filt'), [(8 * s + y, 8 * s + y - 9) for s in...  4.75 us
    pallas_call x1, Pallas kernels, on_device(): call(pack_body, shape((8, 7, 16, 256), BF16), [ANY] * 2, (2 * mb, mb), [p...  2.48 us
    ppermute x1, waiting for transfers between devices, on_device(): other = lax.ppermute(part, 'slab', CORE_PAIRS)  2.39 us
    pallas_call x1, Pallas kernels, on_device(): call(input_body, shape((2, 128, 2, 256), BF16), [VMEM] * 5, (226 * mb, 3...  2.22 us
  transfers between devices with their start and end apart: 7, of which 5 were waited for; matrix products, arithmetic and copies ran while one was open for 0% of the time, Pallas kernels for 3%

profile of v17, /device:TPU:1, one launch (start us, length us, event | category | flops | bytes accessed | tf_op | source)
XLA Modules:
  0.0 98.6 jit_solution(14814157432906665097)
XLA Ops:
  0.6 2.5 %shard_map.50 = bf16[8,7,16,256]{3,2,1,0:T(8,128)(2,1)} custom-call(bf16[2,16,16,256]{3,2,1,0:T(8,128)(2,1)} %vol_hbm.1, bf16[1,32,8,128]{3,2,1,0:T(8,128)(2,1)} %err_hbm.1), custom_call_target="tpu_custom_call" | custom-call | flops 2097152 | bytes 1048576 | tf_op jit(solution)/shard_map/pallas_call | solution.py:229
  3.1 20.3 %all_to_all.20.rec_ref = bf16[8,7,16,256]{3,2,1,0:T(8,128)(2,1)S(1)} all-to-all(bf16[8,7,16,256]{3,2,1,0:T(8,128)(2,1)} %shard_map.50), channel_id=1, replica_groups=mesh['slab'=64,'filt'=8] {'filt'}, dimensions={0} | all-to-all | bytes 917504 | tf_op jit(solution)/shard_map/all_to_all | solution.py:212
  23.5 8.3 %collective-permute-start = (bf16[8,3,16,256]{3,2,1,0:T(8,128)(2,1)S(1)}, bf16[8,3,16,256]{3,2,1,0:T(8,128)(2,1)S(1)}, u32[]{:S(2)}, u32[]{:S(2)}) collective-permute-start(bf16[8,3,16,256]{3,2,1,0:T(8,128)(2,1)S(1)} %slice.4), channel_id=1, source_target_pairs={{0,8},{8,16},{16,24},{24,32},{32,40},{40,48},{48,56},{56,64},{64,7... | collective-permute-start | bytes 589832 | tf_op jit(solution)/shard_map/ppermute | solution.py:208
  31.8 1.1 %shard_map.51 = (bf16[256,1152]{1,0:T(8,128)(2,1)S(1)}, bf16[512,1152]{1,0:T(8,128)(2,1)S(1)}) custom-call(bf16[9,3,128,256]{3,2,1,0:T(8,128)(2,1)S(1)} %bitcast.6), custom_call_target="tpu_custom_call" | custom-call | flops 473956352 | bytes 4194304 | tf_op jit(solution)/shard_map/pallas_call | solution.py:242
  32.8 1.5 %collective-permute-done.rim_ref = bf16[8,3,16,256]{3,2,1,0:T(8,128)(2,1)S(1)} collective-permute-done((bf16[8,3,16,256]{3,2,1,0:T(8,128)(2,1)S(1)}, bf16[8,3,16,256]{3,2,1,0:T(8,128)(2,1)S(1)}, u32[]{:S(2)}, u32[]{:S(2)}) %collective-permute-start) | collective-permute-done | bytes 196640 | tf_op jit(solution)/shard_map/ppermute | solution.py:208
  34.3 1.5 %shard_map.52 = (bf16[256,128]{1,0:T(8,128)(2,1)S(1)}, bf16[256,256]{1,0:T(8,128)(2,1)S(1)}, bf16[1152,128]{1,0:T(8,128)(2,1)S(1)}, bf16[1152,128]{1,0:T(8,128)(2,1)S(1)}, bf16[128,3456]{1,0:T(8,128)(2,1)S(1)}) custom-call(s32[1]{0:T(128)} %bitcast.core_ref, bf16[8,7,16,256]{3,2,1,0:T(8,128)(2,1)S(1)} %all_to_all.20.rec_ref, ...), custom_call_target="tpu_custom_call" | custom-call | flops 475004928 | bytes 4194304 | tf_op jit(solution)/shard_map/pallas_call | solution.py:247
  35.8 1.9 %collective-permute-start.1 = (bf16[128,3456]{1,0:T(8,128)(2,1)S(1)}, bf16[128,3456]{1,0:T(8,128)(2,1)S(1)}, u32[]{:S(2)}, u32[]{:S(2)}) collective-permute-start(bf16[128,3456]{1,0:T(8,128)(2,1)S(1)} %get-tuple-element.20), channel_id=1, source_target_pairs={{0,8},{8,0},{16,24},{24,16},{32,40},{40,32},{48,56},{56,48},{64,72... | collective-permute-start | bytes 2654216 | tf_op jit(solution)/shard_map/ppermute | solution.py:254
  37.7 2.4 %collective-permute-done.1.other_ref = bf16[128,3456]{1,0:T(8,128)(2,1)S(1)} collective-permute-done((bf16[128,3456]{1,0:T(8,128)(2,1)S(1)}, bf16[128,3456]{1,0:T(8,128)(2,1)S(1)}, u32[]{:S(2)}, u32[]{:S(2)}) %collective-permute-start.1) | collective-permute-done | bytes 884768 | tf_op jit(solution)/shard_map/ppermute | solution.py:254
  40.1 0.5 shard_map.53
  40.6 20.9 %all_to_all.21.in_ref = bf16[16,8,3456]{2,1,0:T(8,128)(2,1)S(1)} all-to-all(bf16[16,8,3456]{2,1,0:T(8,128)(2,1)S(1)} %bitcast.8), channel_id=1, replica_groups={{0,1,16,17,128,129,144,145,256,257,272,273,384,385,400,401},{2,3,18,19,..., dimensions={0} | all-to-all | bytes 1769472 | tf_op jit(solution)/shard_map/all_to_all | solution.py:212
  61.5 0.8 shard_map.54
  62.4 7.3 %all-to-all-start.2 = ((bf16[16,2,3456]{2,1,0:T(2,128)(2,1)}), bf16[16,2,3456]{2,1,0:T(2,128)(2,1)S(1)}, u32[]{:S(2)}, u32[]{:S(2)}) async-start(bf16[16,2,3456]{2,1,0:T(2,128)(2,1)} %shard_map.54), calls=%async_computation.2 | async-start | bytes 442368 | tf_op jit(solution)/shard_map/all_to_all | solution.py:212
  69.7 1.3 %collective-permute-start.4 = (bf16[256,128]{1,0:T(8,128)(2,1)S(1)}, bf16[256,128]{1,0:T(8,128)(2,1)S(1)}, u32[]{:S(2)}, u32[]{:S(2)}) collective-permute-start(bf16[256,128]{1,0:T(8,128)(2,1)S(1)} %get-tuple-element.21.own_ref), channel_id=1, source_target_pairs={{9,0},{10,1},{11,2},{12,3},{13,4},{14,5},{15,6},{17,8},{18,9},{19,... | collective-permute-start | bytes 196616 | tf_op jit(solution)/shard_map/ppermute | solution.py:262
  71.0 4.9 %collective-permute-start.3 = (bf16[256,128]{1,0:T(8,128)(2,1)S(1)}, bf16[256,128]{1,0:T(8,128)(2,1)S(1)}, u32[]{:S(2)}, u32[]{:S(2)}) collective-permute-start(bf16[256,128]{1,0:T(8,128)(2,1)S(1)} %get-tuple-element.21.own_ref), channel_id=1, source_target_pairs={{8,0},{16,8},{24,16},{32,24},{40,32},{48,40},{56,48},{64,56},{72,6... | collective-permute-start | bytes 196616 | tf_op jit(solution)/shard_map/ppermute | solution.py:208
  75.9 4.7 %collective-permute-done.4.diag_ref = bf16[256,128]{1,0:T(8,128)(2,1)S(1)} collective-permute-done((bf16[256,128]{1,0:T(8,128)(2,1)S(1)}, bf16[256,128]{1,0:T(8,128)(2,1)S(1)}, u32[]{:S(2)}, u32[]{:S(2)}) %collective-permute-start.4) | collective-permute-done | bytes 65568 | tf_op jit(solution)/shard_map/ppermute | solution.py:262
  80.7 0.0 collective-permute-done.3.up_ref
  80.7 0.8 all-to-all-done.2.in_ref
  81.5 0.7 shard_map.56
  82.2 7.6 %all-to-all-start.3 = ((bf16[16,2,3456]{2,1,0:T(2,128)(2,1)}), bf16[16,2,3456]{2,1,0:T(2,128)(2,1)S(1)}, u32[]{:S(2)}, u32[]{:S(2)}) async-start(bf16[16,2,3456]{2,1,0:T(2,128)(2,1)} %shard_map.56), calls=%async_computation.3 | async-start | bytes 442368 | tf_op jit(solution)/shard_map/all_to_all | solution.py:212
  89.9 1.3 %collective-permute-start.2 = (bf16[256,128]{1,0:T(8,128)(2,1)S(1)}, bf16[256,128]{1,0:T(8,128)(2,1)S(1)}, u32[]{:S(2)}, u32[]{:S(2)}) collective-permute-start(bf16[256,128]{1,0:T(8,128)(2,1)S(1)} %get-tuple-element.21.own_ref), channel_id=1, source_target_pairs={{1,0},{2,1},{3,2},{4,3},{5,4},{6,5},{7,6},{9,8},{10,9},{11,10},{12... | collective-permute-start | bytes 196616 | tf_op jit(solution)/shard_map/ppermute | solution.py:208
  91.1 4.3 %collective-permute-done.2.right_ref = bf16[256,128]{1,0:T(8,128)(2,1)S(1)} collective-permute-done((bf16[256,128]{1,0:T(8,128)(2,1)S(1)}, bf16[256,128]{1,0:T(8,128)(2,1)S(1)}, u32[]{:S(2)}, u32[]{:S(2)}) %collective-permute-start.2) | collective-permute-done | bytes 65568 | tf_op jit(solution)/shard_map/ppermute | solution.py:208
  95.4 2.2 %shard_map.55 = bf16[2,128,2,256]{3,2,1,0:T(2,128)(2,1)} custom-call(bf16[256,128]{1,0:T(8,128)(2,1)S(1)} %get-tuple-element.21.own_ref, bf16[256,128]{1,0:T(8,128)(2,1)S(1)} %collective-permute-done.2.right_ref, bf16[256,128]{1,0:T(8,128)(2,1)S(1)} %collective-permute-done.3.up_ref, bf16[256,128]{1,0:T(8,128)(2,1)S(1)} %collective-permute-done.4.diag_ref, ...), custom_call_target="tpu_custom_call" | custom-call | flops 236978176 | bytes 3145728 | tf_op jit(solution)/shard_map/pallas_call | solution.py:271
  97.6 0.0 all-to-all-done.3.in_ref
  97.6 1.0 shard_map.57
  (3 shorter events, 0.0 us)
Async XLA Ops:
  0.6 31.1 %copy-start = (bf16[3,3,3,128,256]{4,3,2,1,0:T(8,128)(2,1)S(1)}, bf16[3,3,3,128,256]{4,3,2,1,0:T(8,128)(2,1)}, u32[]{:S(2)}) copy-start(bf16[3,3,3,128,256]{4,3,2,1,0:T(8,128)(2,1)} %param.4) | copy-start | bytes 5308420
  23.5 10.9 %collective-permute-start = (bf16[8,3,16,256]{3,2,1,0:T(8,128)(2,1)S(1)}, bf16[8,3,16,256]{3,2,1,0:T(8,128)(2,1)S(1)}, u32[]{:S(2)}, u32[]{:S(2)}) collective-permute-start(bf16[8,3,16,256]{3,2,1,0:T(8,128)(2,1)S(1)} %slice.4), channel_id=1, source_target_pairs={{0,8},{8,16},{16,24},{24,32},{32,40},{40,48},{48,56},{56,64},{64,7... | collective-permute-start | bytes 589832 | tf_op jit(solution)/shard_map/ppermute | solution.py:208
  35.8 4.3 %collective-permute-start.1 = (bf16[128,3456]{1,0:T(8,128)(2,1)S(1)}, bf16[128,3456]{1,0:T(8,128)(2,1)S(1)}, u32[]{:S(2)}, u32[]{:S(2)}) collective-permute-start(bf16[128,3456]{1,0:T(8,128)(2,1)S(1)} %get-tuple-element.20), channel_id=1, source_target_pairs={{0,8},{8,0},{16,24},{24,16},{32,40},{40,32},{48,56},{56,48},{64,72... | collective-permute-start | bytes 2654216 | tf_op jit(solution)/shard_map/ppermute | solution.py:254
  62.4 19.1 %all-to-all-start.2 = ((bf16[16,2,3456]{2,1,0:T(2,128)(2,1)}), bf16[16,2,3456]{2,1,0:T(2,128)(2,1)S(1)}, u32[]{:S(2)}, u32[]{:S(2)}) async-start(bf16[16,2,3456]{2,1,0:T(2,128)(2,1)} %shard_map.54), calls=%async_computation.2 | async-start | bytes 442368 | tf_op jit(solution)/shard_map/all_to_all | solution.py:212
  69.7 11.0 %collective-permute-start.4 = (bf16[256,128]{1,0:T(8,128)(2,1)S(1)}, bf16[256,128]{1,0:T(8,128)(2,1)S(1)}, u32[]{:S(2)}, u32[]{:S(2)}) collective-permute-start(bf16[256,128]{1,0:T(8,128)(2,1)S(1)} %get-tuple-element.21.own_ref), channel_id=1, source_target_pairs={{9,0},{10,1},{11,2},{12,3},{13,4},{14,5},{15,6},{17,8},{18,9},{19,... | collective-permute-start | bytes 196616 | tf_op jit(solution)/shard_map/ppermute | solution.py:262
  71.0 9.7 %collective-permute-start.3 = (bf16[256,128]{1,0:T(8,128)(2,1)S(1)}, bf16[256,128]{1,0:T(8,128)(2,1)S(1)}, u32[]{:S(2)}, u32[]{:S(2)}) collective-permute-start(bf16[256,128]{1,0:T(8,128)(2,1)S(1)} %get-tuple-element.21.own_ref), channel_id=1, source_target_pairs={{8,0},{16,8},{24,16},{32,24},{40,32},{48,40},{56,48},{64,56},{72,6... | collective-permute-start | bytes 196616 | tf_op jit(solution)/shard_map/ppermute | solution.py:208
  82.2 15.4 %all-to-all-start.3 = ((bf16[16,2,3456]{2,1,0:T(2,128)(2,1)}), bf16[16,2,3456]{2,1,0:T(2,128)(2,1)S(1)}, u32[]{:S(2)}, u32[]{:S(2)}) async-start(bf16[16,2,3456]{2,1,0:T(2,128)(2,1)} %shard_map.56), calls=%async_computation.3 | async-start | bytes 442368 | tf_op jit(solution)/shard_map/all_to_all | solution.py:212
  89.9 5.5 %collective-permute-start.2 = (bf16[256,128]{1,0:T(8,128)(2,1)S(1)}, bf16[256,128]{1,0:T(8,128)(2,1)S(1)}, u32[]{:S(2)}, u32[]{:S(2)}) collective-permute-start(bf16[256,128]{1,0:T(8,128)(2,1)S(1)} %get-tuple-element.21.own_ref), channel_id=1, source_target_pairs={{1,0},{2,1},{3,2},{4,3},{5,4},{6,5},{7,6},{9,8},{10,9},{11,10},{12... | collective-permute-start | bytes 196616 | tf_op jit(solution)/shard_map/ppermute | solution.py:208
